TPU v7x, 128 devices: a whole 4x4x4 slice. The times are simulated.
128 devices in a mesh: op: 32 (over z_lo, y, x), blk: 4 (over z_hi, core).
Axes of the slice: x: 4, y: 4, z: 4 (z_hi: 2, z_lo: 2; z = z_hi * 2 + z_lo), core: 2. Of those that a mesh axis runs over, the one named last changes fastest.
Arguments:
- wave_blocks: bfloat16 [16, 256, 256], P('blk'), may hold values from -6 to 6
- left_env: bfloat16 [512, 16, 256, 256], P('op', 'blk'), may hold values from -0.375 to 0.375
- right_env: bfloat16 [512, 16, 256, 256], P('op', 'blk'), may hold values from -0.015625 to 0.015625
- source: int32 [512, 16], P('op', 'blk'), may hold values from 0 to 15
- block_dims: int32 [2, 16], P(None, 'blk'), may hold values from 64 to 256, as said below
- energy: float32 [16], P('blk'), may hold values from 0.5 to 3
Outputs:
- applied_wave: float32 [16, 256, 256], P('blk')
- applied_corr: float32 [16, 256, 256], P('blk')
Inputs may be any that keep to these rules, and one draw needn't show every extreme that they name: `source`: each entry names a block. `block_dims`: 256 is reached in every draw.
All inputs are finite; a program needn't handle non-finite values.
Results may differ from a plain program's by a relative error of at most 0.0037.
Values may be sent and summed in bfloat16 or wider, within the bound.
No kernel may reach another device: no remote copies, remote signals or barrier semaphores. Data moves between devices by JAX's collectives and lax.ppermute only.
A program may use at most 64 MiB of HBM per device.

v0:
```python
import jax
import jax.numpy as jnp
from jax import lax
from jax.sharding import PartitionSpec as P


def live_mask(block_dims, row_count, block_size):
    row_ids = jnp.arange(row_count, dtype=jnp.int32)
    col_ids = jnp.arange(block_size, dtype=jnp.int32)
    rows_ok = row_ids[None, :, None] < block_dims[0][:, None, None]
    cols_ok = col_ids[None, None, :] < block_dims[1][:, None, None]
    return rows_ok & cols_ok


def gather_blocks(vector):
    return lax.all_gather(vector, "blk", axis=0, tiled=True)


def apply_terms(vector, left_env, right_env, source):
    whole = gather_blocks(vector)
    block_count = left_env.shape[1]
    block_size = left_env.shape[2]

    def add_term(total, pieces):
        left_term, right_term, source_term = pieces
        chosen = jnp.take(whole, source_term, axis=0)
        inner = jnp.einsum(
            "eij,ejk->eik", left_term, chosen, preferred_element_type=jnp.float32
        ).astype(jnp.bfloat16)
        return (
            total
            + jnp.einsum("eik,elk->eil", inner, right_term, preferred_element_type=jnp.float32),
            None,
        )

    zeros = jnp.zeros((block_count, block_size, block_size), jnp.float32)
    total, unused = lax.scan(add_term, zeros, (left_env, right_env, source))
    return total


def shards(wave_blocks, left_env, right_env, source, block_dims, energy):
    block_count = wave_blocks.shape[0]
    block_size = wave_blocks.shape[1]
    blk_count = lax.axis_size("blk")
    per_group = block_count // blk_count
    entries = block_count * blk_count * block_size * block_size
    live = live_mask(block_dims, block_size, block_size)
    wave_live = jnp.where(live, wave_blocks, jnp.zeros_like(wave_blocks))

    def apply_hamiltonian(vector):
        partial_value = apply_terms(vector, left_env, right_env, source)
        summed = lax.psum(partial_value, "op")
        grouped = summed.reshape(per_group, blk_count, block_size, block_size)
        moved = lax.all_to_all(grouped, "blk", split_axis=1, concat_axis=1, tiled=True).reshape(
            block_count, block_size, block_size
        )
        result = moved + energy[:, None, None] * vector.astype(jnp.float32)
        return jnp.where(live, result, jnp.zeros_like(result))

    applied_wave = apply_hamiltonian(wave_live)
    wave_float = wave_live.astype(jnp.float32)
    cross_sum, square_sum = lax.psum(
        (jnp.sum(wave_float * applied_wave), jnp.sum(wave_float * wave_float)), "blk"
    )
    rayleigh = cross_sum / entries / (square_sum / entries + 1e-06)
    residual = applied_wave - rayleigh * wave_float
    resid_sum = lax.psum(jnp.sum(residual * residual), "blk")
    correction = (residual * lax.rsqrt(resid_sum / entries + 1e-06)).astype(jnp.bfloat16)
    applied_corr = apply_hamiltonian(correction)
    return (applied_wave, applied_corr)


def solution(mesh):
    placed = (
        P("blk", None, None),
        P("op", "blk", None, None),
        P("op", "blk", None, None),
        P("op", "blk"),
        P(None, "blk"),
        P("blk"),
    )
    return jax.shard_map(
        shards,
        mesh=mesh,
        in_specs=placed,
        out_specs=(P("blk", None, None), P("blk", None, None)),
        check_vma=False,
    )
```

profile of v0, /device:TPU:0, one launch (start us, length us, event | category | flops | bytes accessed | tf_op | source)
XLA Modules:
  0.0 890.9 jit_solution(7192697461116417623)
XLA Ops:
  8.0 2.1 and_select_fusion.2
  11.0 28.6 %all-gather.3.cloned.1.call-done = bf16[16,256,256]{2,1,0:T(8,128)(2,1)} async-done(((bf16[4,256,256]{2,1,0:T(8,128)(2,1)}), bf16[16,256,256]{2,1,0:T(8,128)(2,1)}) %all-gather.3.cloned.1.call-update) | async-done | bytes 2097168 | tf_op jit(solution)/shard_map/all_gather | solution.py:16
  39.6 67.8 %while.22 = (s32[]{:T(128)}, f32[4,256,256]{2,1,0:T(8,128)S(1)}, bf16[16,4,256,256]{3,2,1,0:T(8,128)(2,1)}, s32[16,4]{1,0:T(8,128)S(1)}, bf16[16,256,256]{2,1,0:...) while((s32[]{:T(128)}, f32[4,256,256]{2,1,0:T(8,128)S(1)}, ...), condition=%wide.region_1.3_spmd.clone, body=%wide.region_0.2_spmd.clone.sunk | while | flops 269485088 | bytes 4723883 | solution.py:37
  39.6 2.2 gather_fusion
  43.9 2.2 gather_fusion
  46.0 2.0 convolution_add_fusion.4
  48.1 2.2 gather_fusion
  52.3 2.2 gather_fusion
  56.6 2.2 gather_fusion
  58.7 2.0 convolution_add_fusion.4
  60.8 2.2 gather_fusion
  63.0 2.0 convolution_add_fusion.4
  65.0 2.2 gather_fusion
  67.2 2.0 convolution_add_fusion.4
  69.3 2.2 gather_fusion
  71.4 2.0 convolution_add_fusion.4
  73.5 2.2 gather_fusion
  75.7 2.0 convolution_add_fusion.4
  77.7 2.2 gather_fusion
  82.0 2.2 gather_fusion
  86.2 2.2 gather_fusion
  88.4 2.0 convolution_add_fusion.4
  90.4 2.2 gather_fusion
  92.6 2.0 convolution_add_fusion.4
  94.7 2.2 gather_fusion
  96.9 2.0 convolution_add_fusion.4
  98.9 2.2 gather_fusion
  101.1 2.0 convolution_add_fusion.4
  103.1 2.2 gather_fusion
  105.3 2.0 convolution_add_fusion.4
  108.4 308.6 %all-reduce.4.cloned.1.call-done = f32[1,4,256,256]{3,2,0,1:T(8,128)} async-done(((f32[1,4,256,256]{3,2,0,1:T(8,128)}), f32[1,4,256,256]{3,2,0,1:T(8,128)}) %all-reduce.4.cloned.1.call-update) | async-done | bytes 1048592 | tf_op jit(solution)/shard_map/psum | solution.py:52
  417.0 20.1 %all_to_all.10 = f32[1,4,256,256]{3,2,0,1:T(8,128)S(1)} all-to-all(f32[1,4,256,256]{3,2,0,1:T(8,128)} %all-reduce.4.cloned.1.call-done), channel_id=1, replica_groups=mesh['op'=32,'blk'=4] {'blk'}, dimensions={1} | all-to-all | bytes 2097152 | tf_op jit(solution)/shard_map/all_to_all | solution.py:54
  438.3 7.9 all-reduce
  448.6 7.8 psum.38
  458.3 27.2 %all-gather.5.cloned.1.call-done = bf16[16,256,256]{2,1,0:T(8,128)(2,1)} async-done(((bf16[4,256,256]{2,1,0:T(8,128)(2,1)}), bf16[16,256,256]{2,1,0:T(8,128)(2,1)}) %all-gather.5.cloned.1.call-update) | async-done | bytes 2097168 | tf_op jit(solution)/shard_map/all_gather | solution.py:16
  485.5 67.8 %while.23 = (s32[]{:T(128)}, f32[4,256,256]{2,1,0:T(8,128)S(1)}, bf16[16,4,256,256]{3,2,1,0:T(8,128)(2,1)}, s32[16,4]{1,0:T(8,128)S(1)}, bf16[16,256,256]{2,1,0:...) while((s32[]{:T(128)}, f32[4,256,256]{2,1,0:T(8,128)S(1)}, ...), condition=%wide.region_10.12_spmd.clone, body=%wide.region_9.11_spmd.clone.sunk | while | flops 269485088 | bytes 4723883 | solution.py:37
  485.5 2.2 gather_fusion.1
  489.8 2.2 gather_fusion.1
  494.1 2.2 gather_fusion.1
  496.2 2.0 convolution_add_fusion.5
  498.3 2.2 gather_fusion.1
  500.5 2.0 convolution_add_fusion.5
  502.5 2.2 gather_fusion.1
  504.7 2.0 convolution_add_fusion.5
  506.8 2.2 gather_fusion.1
  508.9 2.0 convolution_add_fusion.5
  511.0 2.2 gather_fusion.1
  513.2 2.0 convolution_add_fusion.5
  515.2 2.2 gather_fusion.1
  519.5 2.2 gather_fusion.1
  523.7 2.2 gather_fusion.1
  525.9 2.0 convolution_add_fusion.5
  527.9 2.2 gather_fusion.1
  530.1 2.0 convolution_add_fusion.5
  532.2 2.2 gather_fusion.1
  534.4 2.0 convolution_add_fusion.5
  536.4 2.2 gather_fusion.1
  538.6 2.0 convolution_add_fusion.5
  540.6 2.2 gather_fusion.1
  542.8 2.0 convolution_add_fusion.5
  544.9 2.2 gather_fusion.1
  549.1 2.2 gather_fusion.1
  554.3 308.7 %all-reduce.6.cloned.1.call-done = f32[1,4,256,256]{3,2,0,1:T(8,128)} async-done(((f32[1,4,256,256]{3,2,0,1:T(8,128)}), f32[1,4,256,256]{3,2,0,1:T(8,128)}) %all-reduce.6.cloned.1.call-update) | async-done | bytes 1048592 | tf_op jit(solution)/shard_map/psum | solution.py:52
  863.0 20.1 %all_to_all.11 = f32[1,4,256,256]{3,2,0,1:T(8,128)S(1)} all-to-all(f32[1,4,256,256]{3,2,0,1:T(8,128)} %all-reduce.6.cloned.1.call-done), channel_id=1, replica_groups=mesh['op'=32,'blk'=4] {'blk'}, dimensions={1} | all-to-all | bytes 2097152 | tf_op jit(solution)/shard_map/all_to_all | solution.py:54
  (104 shorter events, 30.9 us)
Async XLA Ops:
  7.2 32.4 %all-gather.3.cloned.1.call-start = ((), (), s32[]{:S(2)}) async-start(), calls=%async_computation.2 | async-start | bytes 2621440 | tf_op jit(solution)/shard_map/all_gather | solution.py:16
  10.2 406.8 %all-reduce.4.cloned.1.call-start = ((), (), s32[]{:S(2)}) async-start(), calls=%async_computation.3 | async-start | bytes 2097152 | tf_op jit(solution)/shard_map/psum | solution.py:52
  39.6 397.5 %copy-start.3 = (bf16[4,256,256]{2,1,0:T(8,128)(2,1)S(1)}, bf16[4,256,256]{2,1,0:T(8,128)(2,1)}, u32[]{:S(2)}) copy-start(bf16[4,256,256]{2,1,0:T(8,128)(2,1)} %param.12) | copy-start | bytes 1572868
  39.6 397.5 %copy-start.5 = (f32[4]{0:T(128)S(1)}, f32[4]{0:T(128)}, u32[]{:S(2)}) copy-start(f32[4]{0:T(128)} %param.17) | copy-start | bytes 52
  107.3 1.0 copy-start
  108.3 377.2 %all-gather.5.cloned.1.call-start = ((), (), s32[]{:S(2)}) async-start(), calls=%async_computation.4 | async-start | bytes 2621440 | tf_op jit(solution)/shard_map/all_gather | solution.py:16
  438.3 47.3 %copy-start.2 = (f32[4,256,256]{2,1,0:T(8,128)}, f32[4,256,256]{2,1,0:T(8,128)S(1)}, u32[]{:S(2)}) copy-start(f32[4,256,256]{2,1,0:T(8,128)S(1)} %get-tuple-element.167) | copy-start | bytes 3145732
  458.3 404.8 %all-reduce.6.cloned.1.call-start = ((), (), s32[]{:S(2)}) async-start(), calls=%async_computation.5 | async-start | bytes 2097152 | tf_op jit(solution)/shard_map/psum | solution.py:52
  485.5 397.6 %copy-start.4 = (bf16[4,256,256]{2,1,0:T(8,128)(2,1)S(1)}, bf16[4,256,256]{2,1,0:T(8,128)(2,1)}, u32[]{:S(2)}) copy-start(bf16[4,256,256]{2,1,0:T(8,128)(2,1)} %multiply_convert_fusion) | copy-start | bytes 1572868
  553.3 1.0 copy-start.1
Sparse Core Ops, SparseCore 0:
  10.3 29.2 all-gather.2
  108.5 308.4 all-reduce.3
  458.4 27.0 all-gather.4
  554.4 308.5 all-reduce.5
where the time goes:
time: 893 us; the launch traced here: 891 us
  waiting for transfers between devices  673 us (75%)
  local copies, waits for them, and re-layouts  73 us (8%)
  matrix products  63.8 us (7%)
  blocking collectives  55.9 us (6%)
  between operations  15.9 us (2%)
    psum x2, waiting for transfers between devices, apply_hamiltonian(): summed = lax.psum(partial_value, 'op')  617 us
    gather x32, local copies, waits for them, and re-layouts, add_term(): chosen = jnp.take(whole, source_term, axis=0)  69.6 us
    dot_general x32, matrix products, add_term(): jnp.einsum('eik,elk->eil', inner, right_term, preferred_element_type=jnp....  63.8 us
    all_gather x2, waiting for transfers between devices, gather_blocks(): return lax.all_gather(vector, 'blk', axis=0, tiled=True)  55.8 us
    all_to_all x2, blocking collectives, apply_hamiltonian(): lax.all_to_all(grouped, 'blk', split_axis=1, concat_axis=1, tiled=True)  40.2 us
  transfers between devices with their start and end apart: 4, of which 4 were waited for; matrix products, arithmetic and copies ran while one was open for 0% of the time, Pallas kernels for 0%

commit v1 on v0

v1 whole, which is shorter than its diff:
```python
import functools

import jax
import jax.numpy as jnp
from jax import lax
from jax.experimental import pallas as pl
from jax.experimental.pallas import tpu as pltpu
from jax.sharding import PartitionSpec as P

BF = jnp.bfloat16
F32 = jnp.float32
BD = 256
INFO = 32
ROWS = 4 * BD + INFO
STEP = 2
MIB = 1 << 20
ALL = ("op", "blk")

SMEM = pl.BlockSpec(memory_space=pltpu.SMEM)
VMEM = pl.BlockSpec(memory_space=pltpu.VMEM)


def device(op, blk):
    return op * 4 + blk


def cross_pairs():
    return [(device(o, b), device(o ^ 16, b ^ 2)) for o in range(32) for b in range(4)]


def core_pairs():
    return [(b, b ^ 1) for b in range(4)]


def core_groups():
    return [[device(o, zh * 2 + c) for zh in range(2) for o in range(32)] for c in range(2)]


def live(rows, cols, shape):
    row_ids = lax.broadcasted_iota(jnp.int32, shape, 0).astype(F32)
    col_ids = lax.broadcasted_iota(jnp.int32, shape, 1).astype(F32)
    return (row_ids < rows) & (col_ids < cols)


def pack_kernel(dims, energy, wave, out):
    for b in range(4):
        mask = live(dims[0, b].astype(F32), dims[1, b].astype(F32), (BD, BD))
        block = jnp.where(mask, wave[b].astype(F32), 0.0)
        out[b * BD:(b + 1) * BD, :] = block.astype(BF)
    row = lax.broadcasted_iota(jnp.int32, (INFO, BD), 0)
    info = jnp.zeros((INFO, BD), F32)
    for b in range(4):
        value = jnp.full((INFO, BD), energy[b], F32)
        high = value.astype(BF).astype(F32)
        middle = (value - high).astype(BF).astype(F32)
        low = value - high - middle
        parts = (dims[0, b].astype(F32), dims[1, b].astype(F32), high, middle, low)
        for j, part in enumerate(parts):
            info = jnp.where(row == b * 8 + j, part, info)
    out[4 * BD:, :] = info.astype(BF)


def add_terms(step, src, vec, left, right, acc):
    for e in range(4):
        total = None
        for t in range(STEP):
            chosen = vec[src[step * STEP + t, e]]
            inner = jnp.dot(left[t, e], chosen, preferred_element_type=F32).astype(BF)
            term = lax.dot_general(
                inner, right[t, e], (((1,), (1,)), ((), ())), preferred_element_type=F32
            )
            total = term if total is None else total + term
        acc[e] += total


def wave_kernel(src, ids, own, far, core, far_core, left, right, out, vec, acc):
    step = pl.program_id(0)

    @pl.when(step == 0)
    def _():
        acc[...] = jnp.zeros_like(acc)
        for flip, piece in ((0, own), (2, far), (1, core), (3, far_core)):
            group = ids[0] ^ flip
            for b in range(4):
                vec[group * 4 + b] = piece[b * BD:(b + 1) * BD, :]

    add_terms(step, src, vec, left, right, acc)

    @pl.when(step == pl.num_programs(0) - 1)
    def _():
        out[...] = acc[...].astype(BF)


def fold(x):
    return jnp.sum(x.reshape(BD // 8, 8, BD), axis=0)


def total_of(x):
    return jnp.sum(jnp.sum(x, axis=1, keepdims=True), axis=0, keepdims=True)


def corr_kernel(
    src, ids, own, far, core, far_core, same, other, left, right,
    applied_out, corr_out, out, vec, acc, work,
):
    step = pl.program_id(0)
    entries = 16 * BD * BD

    @pl.when(step == 0)
    def _():
        me = ids[0]
        pieces = ((0, own), (2, far), (1, core), (3, far_core))
        cross = jnp.zeros((8, BD), F32)
        square = jnp.zeros((8, BD), F32)
        for flip, piece in pieces:
            group = me ^ flip
            for turn in range(4):
                b = me ^ turn
                summed = (same if turn % 2 == 0 else other)[b >> 1, group].astype(F32)
                info = piece[4 * BD:, :].astype(F32)
                pick = lax.broadcasted_iota(jnp.int32, (INFO, BD), 0)

                def entry(j):
                    return jnp.sum(jnp.where(pick == b * 8 + j, info, 0.0), axis=0, keepdims=True)

                mask = live(entry(0), entry(1), (BD, BD))
                level = entry(2) + entry(3) + entry(4)
                wave = piece[pl.ds(pl.multiple_of(b * BD, BD), BD), :].astype(F32)
                applied = jnp.where(mask, summed, 0.0) + level * wave
                work[group * 4 + b] = applied
                if flip == 0:
                    applied_out[b] = applied
                cross += fold(applied * wave)
                square += fold(wave * wave)
        rayleigh = total_of(cross) / entries / (total_of(square) / entries + 1e-06)
        resid = jnp.zeros((8, BD), F32)
        for flip, piece in pieces:
            group = me ^ flip
            for b in range(4):
                wave = piece[b * BD:(b + 1) * BD, :].astype(F32)
                left_over = work[group * 4 + b] - rayleigh * wave
                work[group * 4 + b] = left_over
                resid += fold(left_over * left_over)
        scale = lax.rsqrt(total_of(resid) / entries + 1e-06)
        for b in range(16):
            vec[b] = (work[b] * scale).astype(BF)
        for b in range(4):
            corr_out[b] = vec[me * 4 + b]
        acc[...] = jnp.zeros_like(acc)

    add_terms(step, src, vec, left, right, acc)

    @pl.when(step == pl.num_programs(0) - 1)
    def _():
        for e in range(4):
            for i in range(16):
                for j in range(2):
                    tile = acc[e, i * 16:(i + 1) * 16, j * 128:(j + 1) * 128]
                    out[i * 2 + j, e] = tile.astype(BF)


def reduce_kernel(parts, out):
    total = jnp.sum(parts[...].astype(F32), axis=0).astype(BF)
    for i in range(out.shape[0]):
        out[i] = total


def reduce_blocks_kernel(parts, out):
    total = jnp.sum(parts[...].astype(F32), axis=0).astype(BF)
    for i in range(out.shape[0]):
        out[i] = total


def final_kernel(dims, energy, parts, corr, out):
    for b in range(4):
        mask = live(dims[0, b].astype(F32), dims[1, b].astype(F32), (BD, BD))
        base = energy[b] * corr[b].astype(F32)
        rows = []
        for i in range(16):
            rows.append(jnp.concatenate([parts[2 * i, b], parts[2 * i + 1, b]], axis=1))
        summed = jnp.concatenate(rows, axis=0).astype(F32)
        out[b] = jnp.where(mask, summed + base, 0.0)


def params(mib):
    return pltpu.CompilerParams(vmem_limit_bytes=mib * MIB)


def shape(dims, kind=BF):
    return jax.ShapeDtypeStruct(dims, kind)


def shards(wave_blocks, left_env, right_env, source, block_dims, energy):
    blk = lax.axis_index("blk").astype(jnp.int32)
    ids = blk[None]
    steps = left_env.shape[0] // STEP
    env = pl.BlockSpec((STEP, 4, BD, BD), lambda s: (s, 0, 0, 0))

    own = pl.pallas_call(
        pack_kernel,
        out_shape=shape((ROWS, BD)),
        in_specs=[SMEM, SMEM, VMEM],
        out_specs=VMEM,
        compiler_params=params(16),
        name="pack",
    )(block_dims, energy, wave_blocks)
    far = lax.ppermute(own, ALL, cross_pairs())
    core = lax.ppermute(own, "blk", core_pairs())
    far_core = lax.ppermute(far, "blk", core_pairs())

    partial = pl.pallas_call(
        wave_kernel,
        grid=(steps,),
        out_shape=shape((4, BD, BD)),
        in_specs=[SMEM, SMEM, VMEM, VMEM, VMEM, VMEM, env, env],
        out_specs=VMEM,
        scratch_shapes=[pltpu.VMEM((16, BD, BD), BF), pltpu.VMEM((4, BD, BD), F32)],
        compiler_params=params(32),
        name="wave_terms",
    )(source, ids, own, far, core, far_core, left_env, right_env)

    pieces = lax.all_to_all(partial.reshape(32, 32, BD), "op", 0, 0, tiled=True)
    copies = pl.pallas_call(
        reduce_kernel,
        out_shape=shape((64, 32, BD)),
        in_specs=[VMEM],
        out_specs=VMEM,
        compiler_params=params(16),
        name="sum_wave",
    )(pieces)
    same = lax.all_to_all(
        copies, ALL, 0, 0, tiled=True, axis_index_groups=core_groups()
    )
    other = lax.ppermute(same, "blk", core_pairs())

    applied_wave, corr, partial = pl.pallas_call(
        corr_kernel,
        grid=(steps,),
        out_shape=(shape((4, BD, BD), F32), shape((4, BD, BD)), shape((32, 4, 16, 128))),
        in_specs=[SMEM, SMEM] + [VMEM] * 6 + [env, env],
        out_specs=(VMEM, VMEM, VMEM),
        scratch_shapes=[
            pltpu.VMEM((16, BD, BD), BF),
            pltpu.VMEM((4, BD, BD), F32),
            pltpu.VMEM((16, BD, BD), F32),
        ],
        compiler_params=params(40),
        name="corr_terms",
    )(
        source, ids, own, far, core, far_core,
        same.reshape(2, 4, BD, BD), other.reshape(2, 4, BD, BD), left_env, right_env,
    )

    pieces = lax.all_to_all(partial.reshape(128, 16, 128), ALL, 0, 0, tiled=True)
    copies = pl.pallas_call(
        reduce_blocks_kernel,
        out_shape=shape((32, 4, 16, 128)),
        in_specs=[VMEM],
        out_specs=VMEM,
        compiler_params=params(16),
        name="sum_corr",
    )(pieces.reshape(32, 4, 16, 128))
    gathered = lax.all_to_all(copies, "op", 0, 0, tiled=True)
    applied_corr = pl.pallas_call(
        final_kernel,
        out_shape=shape((4, BD, BD), F32),
        in_specs=[SMEM, SMEM, VMEM, VMEM],
        out_specs=VMEM,
        compiler_params=params(16),
        name="finish",
    )(block_dims, energy, gathered, corr)
    return (applied_wave, applied_corr)


def solution(mesh):
    placed = (
        P("blk", None, None),
        P("op", "blk", None, None),
        P("op", "blk", None, None),
        P("op", "blk"),
        P(None, "blk"),
        P("blk"),
    )
    return jax.shard_map(
        shards,
        mesh=mesh,
        in_specs=placed,
        out_specs=(P("blk", None, None), P("blk", None, None)),
        check_vma=False,
    )
```

time: 893 us -> 134 us (0.15)
  waiting for transfers between devices: 673 us -> 16.1 us
  matrix products: 63.8 us -> 0 us
  local copies, waits for them, and re-layouts: 73 us -> 9.9 us
  Pallas kernels: 0 us -> 26.2 us
  blocking collectives: 55.9 us -> 76.5 us
  between operations: 15.9 us -> 0.68 us
    psum x2 -> x0, waiting for transfers between devices: 617 us -> none  [apply_hamiltonian(): summed = lax.psum(partial_value, 'op')]
    gather x32 -> x0, local copies, waits for them, and re-layouts: 69.6 us -> none  [add_term(): chosen = jnp.take(whole, source_term, axis=0)]
    dot_general x32 -> x0, matrix products: 63.8 us -> none  [add_term(): jnp.einsum('eik,elk->eil', inner, right_term, preferred_element_type=jnp....]
    all_gather x2 -> x0, waiting for transfers between devices: 55.8 us -> none  [gather_blocks(): return lax.all_gather(vector, 'blk', axis=0, tiled=True)]
    all_to_all x2 -> x4, blocking collectives: 40.2 us -> 76.5 us  [the longest x1 25.8 us: shards(): lax.all_to_all(copies, ALL, 0, 0, tiled=True, axis_index_groups=core_grou...]
    pallas_call x0 -> x6, Pallas kernels: none -> 26.2 us  [the longest x1 14.6 us: shards(): pl.pallas_call(corr_kernel, grid=(steps,), out_shape=(shape((4, BD, BD),...]
    ppermute x0 -> x4, waiting for transfers between devices: none -> 16.1 us  [the longest x1 12.3 us: shards(): far = lax.ppermute(own, ALL, cross_pairs())]
    psum x2 -> x0, blocking collectives: 15.7 us -> none  [the longest x1 7.95 us: shards(): lax.psum((jnp.sum(wave_float * applied_wave), jnp.sum(wave_float * wave_f...]
  transfers between devices with their start and end apart: 4 -> 4, of which waited for: 4 -> 3; matrix products, arithmetic and copies ran while one was open for 0% -> 1% of each run, Pallas kernels for 0% -> 0%
where the time goes in v1:
time: 134 us
  blocking collectives  76.5 us (57%)
  Pallas kernels  26.2 us (20%)
  waiting for transfers between devices  16.1 us (12%)
  local copies, waits for them, and re-layouts  9.9 us (7%)
  starting transfers between devices  4.21 us (3%)
    all_to_all x1, blocking collectives, shards(): lax.all_to_all(copies, ALL, 0, 0, tiled=True, axis_index_groups=core_grou...  25.8 us
    all_to_all x1, blocking collectives, shards(): pieces = lax.all_to_all(partial.reshape(32, 32, BD), 'op', 0, 0, tiled=True)  18.7 us
    all_to_all x1, blocking collectives, shards(): lax.all_to_all(partial.reshape(128, 16, 128), ALL, 0, 0, tiled=True)  16.7 us
    all_to_all x1, blocking collectives, shards(): gathered = lax.all_to_all(copies, 'op', 0, 0, tiled=True)  15.3 us
    pallas_call x1, Pallas kernels, shards(): pl.pallas_call(corr_kernel, grid=(steps,), out_shape=(shape((4, BD, BD),...  14.6 us
    ppermute x1, waiting for transfers between devices, shards(): far = lax.ppermute(own, ALL, cross_pairs())  12.3 us
    unnamed x17, local copies, waits for them, and re-layouts  9.9 us
    pallas_call x1, Pallas kernels, shards(): pl.pallas_call(wave_kernel, grid=(steps,), out_shape=shape((4, BD, BD)),...  8.84 us
  transfers between devices with their start and end apart: 4, of which 3 were waited for; matrix products, arithmetic and copies ran while one was open for 1% of the time, Pallas kernels for 0%

profile of v1, /device:TPU:0, one launch (start us, length us, event | category | flops | bytes accessed | tf_op | source)
XLA Modules:
  0.0 133.6 jit_solution(14423153683915462020)
XLA Ops:
  0.6 0.0 copy-start.3
  0.6 1.0 copy-done.3
  1.7 0.0 copy-start.4
  1.7 0.7 copy-done.4
  2.4 0.0 copy-start.6
  2.4 0.7 copy-done.6
  3.0 0.7 pack.1.own
  3.7 4.2 %collective-permute-start = (bf16[1056,256]{1,0:T(8,128)(2,1)S(1)}, bf16[1056,256]{1,0:T(8,128)(2,1)S(1)}, u32[]{:S(2)}, u32[]{:S(2)}) collective-permute-start(bf16[1056,256]{1,0:T(8,128)(2,1)S(1)} %pack.1.own), channel_id=1, source_target_pairs={{0,66},{1,67},{2,64},{3,65},{4,70},{5,71},{6,68},{7,69},{8,74},{9,... | collective-permute-start | bytes 1622024 | tf_op jit(solution)/shard_map/ppermute | solution.py:207
  7.9 0.0 collective-permute-start.1
  7.9 12.3 %collective-permute-done.far = bf16[1056,256]{1,0:T(8,128)(2,1)S(1)} collective-permute-done((bf16[1056,256]{1,0:T(8,128)(2,1)S(1)}, bf16[1056,256]{1,0:T(8,128)(2,1)S(1)}, u32[]{:S(2)}, u32[]{:S(2)}) %collective-permute-start) | collective-permute-done | bytes 540704 | tf_op jit(solution)/shard_map/ppermute | solution.py:207
  20.2 0.0 collective-permute-start.2
  20.2 0.8 copy.9.src
  21.0 0.0 collective-permute-done.1.core
  21.0 1.2 collective-permute-done.2.far_core
  22.1 0.0 copy-start
  22.1 3.4 %copy-done = bf16[16,4,256,256]{3,2,1,0:T(8,128)(2,1)S(1)} copy-done((bf16[16,4,256,256]{3,2,1,0:T(8,128)(2,1)S(1)}, bf16[16,4,256,256]{3,2,1,0:T(8,128)(2,1)}, u32[]{:S(2)}) %copy-start) | copy-done | bytes 8388632
  25.5 0.0 copy-start.2
  25.5 3.4 %copy-done.2 = bf16[16,4,256,256]{3,2,1,0:T(8,128)(2,1)S(1)} copy-done((bf16[16,4,256,256]{3,2,1,0:T(8,128)(2,1)S(1)}, bf16[16,4,256,256]{3,2,1,0:T(8,128)(2,1)}, u32[]{:S(2)}) %copy-start.2) | copy-done | bytes 8388632
  28.9 0.0 copy-start.1
  28.9 8.8 %wave_terms.1 = bf16[4,256,256]{2,1,0:T(8,128)(2,1)S(1)} custom-call(s32[16,4]{1,0:T(8,128)S(1)} %copy.9.src, s32[1]{0:T(128)} %bitcast.ids, bf16[1056,256]{1,0:T(8,128)(2,1)S(1)} %pack.1.own, bf16[1056,256]{1,0:T(8,128)(2,1)S(1)} %collective-permute-done.far, bf16[1056,256]{1,0:T(8,128)(2,1)S(1)} %collective-permute-done.1.core, ...), custom_call_target="tpu_custom_call" | custom-call | tf_op jit(solution)/shard_map/wave_terms/pallas_call | solution.py:211
  37.7 18.7 %all_to_all.20.parts = bf16[32,32,256]{2,1,0:T(8,128)(2,1)S(1)} all-to-all(bf16[32,32,256]{2,1,0:T(8,128)(2,1)S(1)} %bitcast.8), channel_id=1, replica_groups=mesh['op'=32,'blk'=4] {'op'}, dimensions={0} | all-to-all | bytes 1048576 | tf_op jit(solution)/shard_map/all_to_all | solution.py:222
  56.4 0.2 sum_wave.1
  56.6 25.8 %all_to_all.21 = bf16[64,32,256]{2,1,0:T(8,128)(2,1)S(1)} all-to-all(bf16[64,32,256]{2,1,0:T(8,128)(2,1)S(1)} %sum_wave.1), channel_id=1, replica_groups={{0,4,8,12,16,20,24,28,32,36,40,44,48,52,56,60,64,68,72,76,80,84,88,92,9..., dimensions={0} | all-to-all | bytes 2097152 | tf_op jit(solution)/shard_map/all_to_all | solution.py:231
  82.4 0.0 collective-permute-start.3
  82.4 2.7 %collective-permute-done.3 = bf16[64,32,256]{2,1,0:T(8,128)(2,1)S(1)} collective-permute-done((bf16[64,32,256]{2,1,0:T(8,128)(2,1)S(1)}, bf16[64,32,256]{2,1,0:T(8,128)(2,1)S(1)}, u32[]{:S(2)}, u32[]{:S(2)}) %collective-permute-start.3) | collective-permute-done | bytes 1048608 | tf_op jit(solution)/shard_map/ppermute | solution.py:234
  85.0 0.0 copy-done.1
  85.0 0.0 copy-start.5
  85.0 0.0 copy-start.7
  85.1 14.6 %corr_terms.1 = (f32[4,256,256]{2,1,0:T(8,128)}, bf16[4,256,256]{2,1,0:T(8,128)(2,1)S(1)}, bf16[32,4,16,128]{3,2,1,0:T(8,128)(2,1)S(1)}) custom-call(s32[16,4]{1,0:T(8,128)S(1)} %copy.9.src, s32[1]{0:T(128)} %bitcast.ids, bf16[1056,256]{1,0:T(8,128)(2,1)S(1)} %pack.1.own, bf16[1056,256]{1,0:T(8,128)(2,1)S(1)} %collective-permute-done.far, ...), custom_call_target="tpu_custom_call" | custom-call | tf_op jit(solution)/shard_map/corr_terms/pallas_call | solution.py:236
  99.7 16.7 %all_to_all.22 = bf16[128,16,128]{2,1,0:T(8,128)(2,1)S(1)} all-to-all(bf16[128,16,128]{2,1,0:T(8,128)(2,1)S(1)} %bitcast.10), channel_id=1, replica_groups=mesh['op'=32,'blk'=4] {'op','blk'}, dimensions={0} | all-to-all | bytes 1048576 | tf_op jit(solution)/shard_map/all_to_all | solution.py:254
  116.4 0.1 sum_corr.1
  116.5 15.3 %all_to_all.23.parts = bf16[32,4,16,128]{3,2,1,0:T(8,128)(2,1)S(1)} all-to-all(bf16[32,4,16,128]{3,2,1,0:T(8,128)(2,1)S(1)} %sum_corr.1), channel_id=1, replica_groups=mesh['op'=32,'blk'=4] {'op'}, dimensions={0} | all-to-all | bytes 1048576 | tf_op jit(solution)/shard_map/all_to_all | solution.py:263
  131.8 0.0 copy-done.5
  131.8 0.0 copy-done.7
  131.8 1.8 %finish.1 = f32[4,256,256]{2,1,0:T(8,128)} custom-call(s32[2,4]{1,0:T(2,128)S(1)} %copy-done.5, f32[4]{0:T(128)S(1)} %copy-done.7, bf16[32,4,16,128]{3,2,1,0:T(8,128)(2,1)S(1)} %all_to_all.23.parts, bf16[4,256,256]{2,1,0:T(8,128)(2,1)S(1)} %get-tuple-element.7.corr), custom_call_target="tpu_custom_call" | custom-call | tf_op jit(solution)/shard_map/finish/pallas_call | solution.py:264
Async XLA Ops:
  0.6 1.0 copy-start.3
  1.7 0.7 copy-start.4
  2.4 0.7 copy-start.6
  3.7 16.5 %collective-permute-start = (bf16[1056,256]{1,0:T(8,128)(2,1)S(1)}, bf16[1056,256]{1,0:T(8,128)(2,1)S(1)}, u32[]{:S(2)}, u32[]{:S(2)}) collective-permute-start(bf16[1056,256]{1,0:T(8,128)(2,1)S(1)} %pack.1.own), channel_id=1, source_target_pairs={{0,66},{1,67},{2,64},{3,65},{4,70},{5,71},{6,68},{7,69},{8,74},{9,... | collective-permute-start | bytes 1622024 | tf_op jit(solution)/shard_map/ppermute | solution.py:207
  7.9 13.0 %collective-permute-start.1 = (bf16[1056,256]{1,0:T(8,128)(2,1)S(1)}, bf16[1056,256]{1,0:T(8,128)(2,1)S(1)}, u32[]{:S(2)}, u32[]{:S(2)}) collective-permute-start(bf16[1056,256]{1,0:T(8,128)(2,1)S(1)} %pack.1.own), channel_id=1, source_target_pairs={{0,1},{1,0},{2,3},{3,2},{4,5},{5,4},{6,7},{7,6},{8,9},{9,8},{10,11... | collective-permute-start | bytes 1622024 | tf_op jit(solution)/shard_map/ppermute | solution.py:208
  20.2 1.9 %collective-permute-start.2 = (bf16[1056,256]{1,0:T(8,128)(2,1)S(1)}, bf16[1056,256]{1,0:T(8,128)(2,1)S(1)}, u32[]{:S(2)}, u32[]{:S(2)}) collective-permute-start(bf16[1056,256]{1,0:T(8,128)(2,1)S(1)} %collective-permute-done.far), channel_id=1, source_target_pairs={{0,1},{1,0},{2,3},{3,2},{4,5},{5,4},{6,7},{7,6},{8,9},{9,8},{10,11... | collective-permute-start | bytes 1622024 | tf_op jit(solution)/shard_map/ppermute | solution.py:209
  22.1 3.4 %copy-start = (bf16[16,4,256,256]{3,2,1,0:T(8,128)(2,1)S(1)}, bf16[16,4,256,256]{3,2,1,0:T(8,128)(2,1)}, u32[]{:S(2)}) copy-start(bf16[16,4,256,256]{3,2,1,0:T(8,128)(2,1)} %left.3) | copy-start | bytes 25165828
  25.5 3.4 %copy-start.2 = (bf16[16,4,256,256]{3,2,1,0:T(8,128)(2,1)S(1)}, bf16[16,4,256,256]{3,2,1,0:T(8,128)(2,1)}, u32[]{:S(2)}) copy-start(bf16[16,4,256,256]{3,2,1,0:T(8,128)(2,1)} %right.3) | copy-start | bytes 25165828
  28.9 56.1 %copy-start.1 = (bf16[16,4,256,256]{3,2,1,0:T(8,128)(2,1)S(1)}, bf16[16,4,256,256]{3,2,1,0:T(8,128)(2,1)}, u32[]{:S(2)}) copy-start(bf16[16,4,256,256]{3,2,1,0:T(8,128)(2,1)} %left.3) | copy-start | bytes 25165828
  82.4 2.7 %collective-permute-start.3 = (bf16[64,32,256]{2,1,0:T(8,128)(2,1)S(1)}, bf16[64,32,256]{2,1,0:T(8,128)(2,1)S(1)}, u32[]{:S(2)}, u32[]{:S(2)}) collective-permute-start(bf16[64,32,256]{2,1,0:T(8,128)(2,1)S(1)} %all_to_all.21), channel_id=1, source_target_pairs={{0,1},{1,0},{2,3},{3,2},{4,5},{5,4},{6,7},{7,6},{8,9},{9,8},{10,11... | collective-permute-start | bytes 3145736 | tf_op jit(solution)/shard_map/ppermute | solution.py:234
  85.0 46.8 %copy-start.5 = (s32[2,4]{1,0:T(2,128)S(1)}, s32[2,4]{1,0:T(2,128)}, u32[]{:S(2)}) copy-start(s32[2,4]{1,0:T(2,128)} %dims.3) | copy-start | bytes 100
  85.0 46.8 %copy-start.7 = (f32[4]{0:T(128)S(1)}, f32[4]{0:T(128)}, u32[]{:S(2)}) copy-start(f32[4]{0:T(128)} %energy.3) | copy-start | bytes 52

commit v2 on v1

v2 whole, which is shorter than its diff:
```python
import jax
import jax.numpy as jnp
from jax import lax
from jax.experimental import pallas as pl
from jax.experimental.pallas import tpu as pltpu
from jax.sharding import PartitionSpec as P

BF = jnp.bfloat16
F32 = jnp.float32
BD = 256
INFO = 32
ROWS = 4 * BD + INFO
BATCH = 8
CHUNKS = (4, 4, 4, 2, 2)
STRIP = 32
MIB = 1 << 20
ALL = ("op", "blk")

SMEM = pl.BlockSpec(memory_space=pltpu.SMEM)
VMEM = pl.BlockSpec(memory_space=pltpu.VMEM)
HBM = pl.BlockSpec(memory_space=pltpu.HBM)


def device(op, blk):
    return op * 4 + blk


def cross_pairs():
    return [(device(o, b), device(o ^ 16, b ^ 2)) for o in range(32) for b in range(4)]


def core_pairs():
    return [(b, b ^ 1) for b in range(4)]


def core_groups():
    return [[device(o, zh * 2 + c) for zh in range(2) for o in range(32)] for c in range(2)]


def live(rows, cols, shape, first_row=0, first_col=0):
    row_ids = lax.broadcasted_iota(jnp.int32, shape, 0) + first_row
    col_ids = lax.broadcasted_iota(jnp.int32, shape, 1) + first_col
    return (row_ids < rows) & (col_ids < cols)


def pack_kernel(dims_in, energy_in, wave_in, out, dims, energy, wave, sems):
    copies = [
        pltpu.make_async_copy(dims_in, dims, sems.at[0]),
        pltpu.make_async_copy(energy_in, energy, sems.at[1]),
        pltpu.make_async_copy(wave_in, wave, sems.at[2]),
    ]
    for copy in copies:
        copy.start()
    for copy in copies:
        copy.wait()
    for b in range(4):
        mask = live(dims[0, b], dims[1, b], (BD, BD))
        block = jnp.where(mask, wave[b].astype(F32), 0.0)
        out[b * BD:(b + 1) * BD, :] = block.astype(BF)
    row = lax.broadcasted_iota(jnp.int32, (INFO, BD), 0)
    info = jnp.zeros((INFO, BD), F32)
    for b in range(4):
        value = jnp.full((INFO, BD), energy[b], F32)
        high = value.astype(BF).astype(F32)
        middle = (value - high).astype(BF).astype(F32)
        low = value - high - middle
        parts = (dims[0, b].astype(F32), dims[1, b].astype(F32), high, middle, low)
        for j, part in enumerate(parts):
            info = jnp.where(row == b * 8 + j, part, info)
    out[4 * BD:, :] = info.astype(BF)


def slot_terms(src, vec, left, right, e, terms):
    inner = [
        jnp.dot(left[t, e], vec[src[e, t]], preferred_element_type=F32).astype(BF)
        for t in terms
    ]
    return lax.dot_general(
        jnp.concatenate(inner, axis=1),
        jnp.concatenate([right[t, e] for t in terms], axis=1),
        (((1,), (1,)), ((), ())),
        preferred_element_type=F32,
    )


def add_terms(src, vec, left, right, acc):
    acc[...] = jnp.zeros_like(acc)

    @pl.loop(0, left.shape[0] // BATCH)
    def _(step):
        terms = [step * BATCH + t for t in range(BATCH)]
        for e in range(4):
            acc[e] += slot_terms(src, vec, left, right, e, terms)


def wave_kernel(
    src_in, ids, own, far, core, far_core, left_in, right_in,
    out, vec, info, left, right, src, acc, src_sem, sems,
):
    src_copy = pltpu.make_async_copy(src_in, src, src_sem)
    src_copy.start()
    starts = [sum(CHUNKS[:i]) for i in range(len(CHUNKS))]
    chunks = []
    for i, (start, size) in enumerate(zip(starts, CHUNKS)):
        terms = pl.ds(start, size)
        chunks.append([
            pltpu.make_async_copy(left_in.at[terms], left.at[terms], sems.at[0, i]),
            pltpu.make_async_copy(right_in.at[terms], right.at[terms], sems.at[1, i]),
        ])
    for copies in chunks:
        for copy in copies:
            copy.start()
    for flip, piece in ((0, own), (2, far), (1, core), (3, far_core)):
        group = ids[0] ^ flip
        rows = piece[4 * BD:, :].astype(F32)
        for b in range(4):
            vec[group * 4 + b] = piece[b * BD:(b + 1) * BD, :]
            entry = rows[b * 8:(b + 1) * 8, :]
            level = entry[2:3] + entry[3:4] + entry[4:5]
            info[group * 4 + b, 0:2] = entry[0:2]
            info[group * 4 + b, 2:3] = level
    src_copy.wait()
    for i, copies in enumerate(chunks):
        for copy in copies:
            copy.wait()
        terms = range(starts[i], starts[i] + CHUNKS[i])
        for e in range(4):
            product = slot_terms(src, vec, left, right, e, terms)
            total = product if i == 0 else acc[e] + product
            if i == len(chunks) - 1:
                out[e] = total.astype(BF)
            else:
                acc[e] = total


def total_of(x):
    return jnp.sum(jnp.sum(x, axis=1, keepdims=True), axis=0, keepdims=True)


def fold(x):
    return jnp.sum(x.reshape(STRIP // 8, 8, BD), axis=0)


def corr_kernel(
    src, ids, wave, info, same, other, left, right,
    applied_out, corr_out, out, vec, acc, work,
):
    entries = 16 * BD * BD
    me = ids[0]
    zero = jnp.zeros((8, BD), F32)
    strips = [pl.ds(r, STRIP) for r in range(0, BD, STRIP)]

    def apply(group, sums):
        cross, square = sums
        for turn in range(4):
            b = me ^ turn
            summed = same if turn % 2 == 0 else other
            block = group * 4 + b
            level = info[block, 2:3]
            for rows in strips:
                vector = wave[block, rows].astype(F32)
                applied = summed[b >> 1, group, rows].astype(F32) + level * vector
                work[block, rows] = applied
                cross += fold(applied * vector)
                square += fold(vector * vector)
        return cross, square

    cross, square = lax.fori_loop(0, 4, apply, (zero, zero))
    for b in range(4):
        applied_out[b] = work[me * 4 + b]
    rayleigh = total_of(cross) / entries / (total_of(square) / entries + 1e-06)

    def subtract(group, resid):
        for b in range(4):
            for rows in strips:
                vector = wave[group * 4 + b, rows].astype(F32)
                rest = work[group * 4 + b, rows] - rayleigh * vector
                work[group * 4 + b, rows] = rest
                resid += fold(rest * rest)
        return resid

    resid = lax.fori_loop(0, 4, subtract, zero)
    scale = lax.rsqrt(total_of(resid) / entries + 1e-06)

    @pl.loop(0, 4)
    def _(group):
        for b in range(4):
            for rows in strips:
                vec[group * 4 + b, rows] = (work[group * 4 + b, rows] * scale).astype(BF)

    for b in range(4):
        corr_out[b] = vec[me * 4 + b]

    add_terms(src, vec, left, right, acc)
    for e in range(4):
        for i in range(16):
            for j in range(2):
                tile = acc[e, i * 16:(i + 1) * 16, j * 128:(j + 1) * 128]
                out[i * 2 + j, e] = tile.astype(BF)


def sum_wave_kernel(ids, info, parts, out):
    part = ids[1]
    entry = info[(part >> 3) * 4 + ids[0]]
    mask = live(entry[0:1], entry[1:2], (STRIP, BD), (part & 7) * STRIP)
    total = jnp.sum(parts[...].astype(F32), axis=0)
    total = jnp.where(mask, total, 0.0).astype(BF)
    for i in range(out.shape[0]):
        out[i] = total


def sum_corr_kernel(ids, info, parts, out):
    part = ids[1]
    totals = []
    for b in range(4):
        entry = info[ids[0] * 4 + b][:, :128]
        total = jnp.sum(parts[:, b].astype(F32), axis=0)
        mask = live(entry[0:1], entry[1:2], (16, 128), (part >> 1) * 16, (part & 1) * 128)
        totals.append(jnp.where(mask, total, 0.0).astype(BF))
    for i in range(out.shape[0]):
        for b in range(4):
            out[i, b] = totals[b]


def final_kernel(ids, info, parts, corr, out):
    for b in range(4):
        level = info[ids[0] * 4 + b, 2:3]
        for i in range(16):
            rows = pl.ds(i * 16, 16)
            summed = jnp.concatenate([parts[2 * i, b], parts[2 * i + 1, b]], axis=1)
            out[b, rows] = summed.astype(F32) + level * corr[b, rows].astype(F32)


def params(mib):
    return pltpu.CompilerParams(vmem_limit_bytes=mib * MIB)


def shape(dims, kind=BF):
    return jax.ShapeDtypeStruct(dims, kind)


def shards(wave_blocks, left_env, right_env, source, block_dims, energy):
    ids = jnp.stack([lax.axis_index("blk"), lax.axis_index("op")]).astype(jnp.int32)
    src = source.T

    own = pl.pallas_call(
        pack_kernel,
        out_shape=shape((ROWS, BD)),
        in_specs=[HBM, HBM, HBM],
        out_specs=VMEM,
        scratch_shapes=[
            pltpu.SMEM((2, 4), jnp.int32),
            pltpu.SMEM((4,), F32),
            pltpu.VMEM((4, BD, BD), BF),
            pltpu.SemaphoreType.DMA((3,)),
        ],
        compiler_params=params(8),
        name="pack",
    )(*(pltpu.with_memory_space_constraint(x, pltpu.HBM) for x in (block_dims, energy, wave_blocks)))
    far = lax.ppermute(own, ALL, cross_pairs())
    core = lax.ppermute(own, "blk", core_pairs())
    far_core = lax.ppermute(far, "blk", core_pairs())

    partial, wave, info, left, right = pl.pallas_call(
        wave_kernel,
        out_shape=(
            shape((4, BD, BD)), shape((16, BD, BD)), shape((16, 8, BD), F32),
            pltpu.VMEM(left_env.shape, BF), pltpu.VMEM(right_env.shape, BF),
        ),
        in_specs=[HBM, SMEM] + [VMEM] * 4 + [HBM, HBM],
        out_specs=(VMEM,) * 5,
        scratch_shapes=[
            pltpu.SMEM((4, 16), jnp.int32),
            pltpu.VMEM((4, BD, BD), F32),
            pltpu.SemaphoreType.DMA,
            pltpu.SemaphoreType.DMA((2, len(CHUNKS))),
        ],
        compiler_params=params(14),
        name="wave_terms",
    )(
        pltpu.with_memory_space_constraint(src, pltpu.HBM), ids, own, far, core, far_core,
        pltpu.with_memory_space_constraint(left_env, pltpu.HBM),
        pltpu.with_memory_space_constraint(right_env, pltpu.HBM),
    )

    pieces = lax.all_to_all(partial.reshape(32, 32, BD), "op", 0, 0, tiled=True)
    copies = pl.pallas_call(
        sum_wave_kernel,
        out_shape=shape((64, 32, BD)),
        in_specs=[SMEM, VMEM, VMEM],
        out_specs=VMEM,
        compiler_params=params(8),
        name="sum_wave",
    )(ids, info, pieces)
    same = lax.all_to_all(
        copies, ALL, 0, 0, tiled=True, axis_index_groups=core_groups()
    )
    other = lax.ppermute(same, "blk", core_pairs())

    applied_wave, corr, partial = pl.pallas_call(
        corr_kernel,
        out_shape=(shape((4, BD, BD), F32), shape((4, BD, BD)), shape((32, 4, 16, 128))),
        in_specs=[SMEM, SMEM] + [VMEM] * 6,
        out_specs=(VMEM, VMEM, VMEM),
        scratch_shapes=[
            pltpu.VMEM((16, BD, BD), BF),
            pltpu.VMEM((4, BD, BD), F32),
            pltpu.VMEM((16, BD, BD), F32),
        ],
        compiler_params=params(14),
        name="corr_terms",
    )(
        src, ids, wave, info,
        same.reshape(2, 4, BD, BD), other.reshape(2, 4, BD, BD), left, right,
    )

    pieces = lax.all_to_all(partial.reshape(128, 16, 128), ALL, 0, 0, tiled=True)
    copies = pl.pallas_call(
        sum_corr_kernel,
        out_shape=shape((32, 4, 16, 128)),
        in_specs=[SMEM, VMEM, VMEM],
        out_specs=VMEM,
        compiler_params=params(8),
        name="sum_corr",
    )(ids, info, pieces.reshape(32, 4, 16, 128))
    gathered = lax.all_to_all(copies, "op", 0, 0, tiled=True)
    applied_corr = pl.pallas_call(
        final_kernel,
        out_shape=shape((4, BD, BD), F32),
        in_specs=[SMEM, VMEM, VMEM, VMEM],
        out_specs=VMEM,
        compiler_params=params(8),
        name="finish",
    )(ids, info, gathered, corr)
    return (applied_wave, applied_corr)


def solution(mesh):
    placed = (
        P("blk", None, None),
        P("op", "blk", None, None),
        P("op", "blk", None, None),
        P("op", "blk"),
        P(None, "blk"),
        P("blk"),
    )
    return jax.shard_map(
        shards,
        mesh=mesh,
        in_specs=placed,
        out_specs=(P("blk", None, None), P("blk", None, None)),
        check_vma=False,
    )
```

time: 134 us -> 120 us (0.90)
  local copies, waits for them, and re-layouts: 9.9 us -> 0.01 us
  Pallas kernels: 26.2 us -> 21.1 us
    unnamed x17 -> x2, local copies, waits for them, and re-layouts: 9.9 us -> 0.01 us
    pallas_call x5, Pallas kernels: 24.4 us -> 19.4 us  [the longest x1 8.67 us: shards(): pl.pallas_call(corr_kernel, out_shape=(shape((4, BD, BD), F32), shape((4,...]
  transfers between devices with their start and end apart: 4 -> 4, of which waited for: 3 -> 3; matrix products, arithmetic and copies ran while one was open for 1% -> 0% of each run, Pallas kernels for 0% -> 0%
where the time goes in v2:
time: 120 us; the launch traced here: 119 us
  blocking collectives  76.5 us (64%)
  Pallas kernels  21.1 us (18%)
  waiting for transfers between devices  16.8 us (14%)
  starting transfers between devices  4.21 us (4%)
    all_to_all x1, blocking collectives, shards(): lax.all_to_all(copies, ALL, 0, 0, tiled=True, axis_index_groups=core_grou...  25.8 us
    all_to_all x1, blocking collectives, shards(): pieces = lax.all_to_all(partial.reshape(32, 32, BD), 'op', 0, 0, tiled=True)  18.7 us
    all_to_all x1, blocking collectives, shards(): lax.all_to_all(partial.reshape(128, 16, 128), ALL, 0, 0, tiled=True)  16.7 us
    all_to_all x1, blocking collectives, shards(): gathered = lax.all_to_all(copies, 'op', 0, 0, tiled=True)  15.3 us
    ppermute x1, waiting for transfers between devices, shards(): far = lax.ppermute(own, ALL, cross_pairs())  12.3 us
    pallas_call x1, Pallas kernels, shards(): pl.pallas_call(corr_kernel, out_shape=(shape((4, BD, BD), F32), shape((4,...  8.67 us
    pallas_call x1, Pallas kernels, shards(): pl.pallas_call(wave_kernel, out_shape=(shape((4, BD, BD)), shape((16, BD,...  8.15 us
    ppermute x1, starting transfers between devices, shards(): far = lax.ppermute(own, ALL, cross_pairs())  4.2 us
  transfers between devices with their start and end apart: 4, of which 3 were waited for; matrix products, arithmetic and copies ran while one was open for 0% of the time, Pallas kernels for 0%

profile of v2, /device:TPU:0, one launch (start us, length us, event | category | flops | bytes accessed | tf_op | source)
XLA Modules:
  0.0 119.3 jit_solution(11892898699510496577)
XLA Ops:
  0.6 1.2 %pack.1.own = bf16[1056,256]{1,0:T(8,128)(2,1)S(1)} custom-call(s32[2,4]{1,0:T(2,128)} %dims_in.1, f32[4]{0:T(128)} %energy_in.1, bf16[4,256,256]{2,1,0:T(8,128)(2,1)} %wave_in.1), custom_call_target="tpu_custom_call" | custom-call | tf_op jit(solution)/shard_map/pack/pallas_call | solution.py:246
  1.9 4.2 %collective-permute-start = (bf16[1056,256]{1,0:T(8,128)(2,1)S(1)}, bf16[1056,256]{1,0:T(8,128)(2,1)S(1)}, u32[]{:S(2)}, u32[]{:S(2)}) collective-permute-start(bf16[1056,256]{1,0:T(8,128)(2,1)S(1)} %pack.1.own), channel_id=1, source_target_pairs={{0,66},{1,67},{2,64},{3,65},{4,70},{5,71},{6,68},{7,69},{8,74},{9,... | collective-permute-start | bytes 1622024 | tf_op jit(solution)/shard_map/ppermute | solution.py:260
  6.1 0.0 collective-permute-start.1
  6.1 12.3 %collective-permute-done.far = bf16[1056,256]{1,0:T(8,128)(2,1)S(1)} collective-permute-done((bf16[1056,256]{1,0:T(8,128)(2,1)S(1)}, bf16[1056,256]{1,0:T(8,128)(2,1)S(1)}, u32[]{:S(2)}, u32[]{:S(2)}) %collective-permute-start) | collective-permute-done | bytes 540704 | tf_op jit(solution)/shard_map/ppermute | solution.py:260
  18.3 0.0 collective-permute-start.2
  18.3 0.1 pad_add_fusion.ids
  18.4 0.0 collective-permute-done.1.core
  18.4 1.9 %collective-permute-done.2.far_core = bf16[1056,256]{1,0:T(8,128)(2,1)S(1)} collective-permute-done((bf16[1056,256]{1,0:T(8,128)(2,1)S(1)}, bf16[1056,256]{1,0:T(8,128)(2,1)S(1)}, u32[]{:S(2)}, u32[]{:S(2)}) %collective-permute-start.2) | collective-permute-done | bytes 540704 | tf_op jit(solution)/shard_map/ppermute | solution.py:262
  20.3 0.0 copy-start
  20.3 8.2 %wave_terms.1 = (bf16[4,256,256]{2,1,0:T(8,128)(2,1)S(1)}, bf16[16,256,256]{2,1,0:T(8,128)(2,1)S(1)}, f32[16,8,256]{2,1,0:T(8,128)S(1)}, bf16[16,4,256,256]{3,2,...) custom-call(s32[4,16]{1,0:T(4,128)} %bitcast.13, s32[2]{0:T(128)S(1)} %pad_add_fusion.ids, bf16[1056,256]{1,0:T(8,128)(2,1)S(1)} %pack.1.own, ...), custom_call_target="tpu_custom_call" | custom-call | tf_op jit(solution)/shard_map/wave_terms/pallas_call | solution.py:264
  28.4 18.7 %all_to_all.20.parts = bf16[32,32,256]{2,1,0:T(8,128)(2,1)S(1)} all-to-all(bf16[32,32,256]{2,1,0:T(8,128)(2,1)S(1)} %bitcast.11), channel_id=1, replica_groups=mesh['op'=32,'blk'=4] {'op'}, dimensions={0} | all-to-all | bytes 1048576 | tf_op jit(solution)/shard_map/all_to_all | solution.py:286
  47.1 0.7 sum_wave.1
  47.9 25.8 %all_to_all.21 = bf16[64,32,256]{2,1,0:T(8,128)(2,1)S(1)} all-to-all(bf16[64,32,256]{2,1,0:T(8,128)(2,1)S(1)} %sum_wave.1), channel_id=1, replica_groups={{0,4,8,12,16,20,24,28,32,36,40,44,48,52,56,60,64,68,72,76,80,84,88,92,9..., dimensions={0} | all-to-all | bytes 2097152 | tf_op jit(solution)/shard_map/all_to_all | solution.py:295
  73.6 0.0 collective-permute-start.3
  73.6 2.7 %collective-permute-done.3 = bf16[64,32,256]{2,1,0:T(8,128)(2,1)S(1)} collective-permute-done((bf16[64,32,256]{2,1,0:T(8,128)(2,1)S(1)}, bf16[64,32,256]{2,1,0:T(8,128)(2,1)S(1)}, u32[]{:S(2)}, u32[]{:S(2)}) %collective-permute-start.3) | collective-permute-done | bytes 1048608 | tf_op jit(solution)/shard_map/ppermute | solution.py:298
  76.3 0.0 copy-done
  76.3 8.7 %corr_terms.1 = (f32[4,256,256]{2,1,0:T(8,128)}, bf16[4,256,256]{2,1,0:T(8,128)(2,1)S(1)}, bf16[32,4,16,128]{3,2,1,0:T(8,128)(2,1)S(1)}) custom-call(s32[4,16]{1,0:T(4,128)S(1)} %bitcast.14, s32[2]{0:T(128)S(1)} %pad_add_fusion.ids, bf16[16,256,256]{2,1,0:T(8,128)(2,1)S(1)} %get-tuple-element.10.wave, f32[16,8,256]{2,1,0:T(8,128)S(1)} %get-tuple-element.11.info, ...), custom_call_target="tpu_custom_call" | custom-call | tf_op jit(solution)/shard_map/corr_terms/pallas_call | solution.py:300
  85.0 16.7 %all_to_all.22 = bf16[128,16,128]{2,1,0:T(8,128)(2,1)S(1)} all-to-all(bf16[128,16,128]{2,1,0:T(8,128)(2,1)S(1)} %bitcast.12), channel_id=1, replica_groups=mesh['op'=32,'blk'=4] {'op','blk'}, dimensions={0} | all-to-all | bytes 1048576 | tf_op jit(solution)/shard_map/all_to_all | solution.py:317
  101.7 0.7 sum_corr.1
  102.4 15.3 %all_to_all.23.parts = bf16[32,4,16,128]{3,2,1,0:T(8,128)(2,1)S(1)} all-to-all(bf16[32,4,16,128]{3,2,1,0:T(8,128)(2,1)S(1)} %sum_corr.1), channel_id=1, replica_groups=mesh['op'=32,'blk'=4] {'op'}, dimensions={0} | all-to-all | bytes 1048576 | tf_op jit(solution)/shard_map/all_to_all | solution.py:326
  117.7 1.7 %finish.1 = f32[4,256,256]{2,1,0:T(8,128)} custom-call(s32[2]{0:T(128)S(1)} %pad_add_fusion.ids, f32[16,8,256]{2,1,0:T(8,128)S(1)} %get-tuple-element.11.info, bf16[32,4,16,128]{3,2,1,0:T(8,128)(2,1)S(1)} %all_to_all.23.parts, bf16[4,256,256]{2,1,0:T(8,128)(2,1)S(1)} %get-tuple-element.17.corr), custom_call_target="tpu_custom_call" | custom-call | tf_op jit(solution)/shard_map/finish/pallas_call | solution.py:327
Async XLA Ops:
  1.9 16.5 %collective-permute-start = (bf16[1056,256]{1,0:T(8,128)(2,1)S(1)}, bf16[1056,256]{1,0:T(8,128)(2,1)S(1)}, u32[]{:S(2)}, u32[]{:S(2)}) collective-permute-start(bf16[1056,256]{1,0:T(8,128)(2,1)S(1)} %pack.1.own), channel_id=1, source_target_pairs={{0,66},{1,67},{2,64},{3,65},{4,70},{5,71},{6,68},{7,69},{8,74},{9,... | collective-permute-start | bytes 1622024 | tf_op jit(solution)/shard_map/ppermute | solution.py:260
  6.1 12.4 %collective-permute-start.1 = (bf16[1056,256]{1,0:T(8,128)(2,1)S(1)}, bf16[1056,256]{1,0:T(8,128)(2,1)S(1)}, u32[]{:S(2)}, u32[]{:S(2)}) collective-permute-start(bf16[1056,256]{1,0:T(8,128)(2,1)S(1)} %pack.1.own), channel_id=1, source_target_pairs={{0,1},{1,0},{2,3},{3,2},{4,5},{5,4},{6,7},{7,6},{8,9},{9,8},{10,11... | collective-permute-start | bytes 1622024 | tf_op jit(solution)/shard_map/ppermute | solution.py:261
  18.3 1.9 %collective-permute-start.2 = (bf16[1056,256]{1,0:T(8,128)(2,1)S(1)}, bf16[1056,256]{1,0:T(8,128)(2,1)S(1)}, u32[]{:S(2)}, u32[]{:S(2)}) collective-permute-start(bf16[1056,256]{1,0:T(8,128)(2,1)S(1)} %collective-permute-done.far), channel_id=1, source_target_pairs={{0,1},{1,0},{2,3},{3,2},{4,5},{5,4},{6,7},{7,6},{8,9},{9,8},{10,11... | collective-permute-start | bytes 1622024 | tf_op jit(solution)/shard_map/ppermute | solution.py:262
  20.3 56.0 %copy-start = (s32[16,4]{0,1:T(4,128)S(1)}, s32[16,4]{0,1:T(4,128)}, u32[]{:S(2)}) copy-start(s32[16,4]{0,1:T(4,128)} %param.9) | copy-start | bytes 772
  73.6 2.7 %collective-permute-start.3 = (bf16[64,32,256]{2,1,0:T(8,128)(2,1)S(1)}, bf16[64,32,256]{2,1,0:T(8,128)(2,1)S(1)}, u32[]{:S(2)}, u32[]{:S(2)}) collective-permute-start(bf16[64,32,256]{2,1,0:T(8,128)(2,1)S(1)} %all_to_all.21), channel_id=1, source_target_pairs={{0,1},{1,0},{2,3},{3,2},{4,5},{5,4},{6,7},{7,6},{8,9},{9,8},{10,11... | collective-permute-start | bytes 3145736 | tf_op jit(solution)/shard_map/ppermute | solution.py:298

commit v3 on v2

--- a/solution.py
+++ b/solution.py
@@ -8,8 +8,8 @@
 BF = jnp.bfloat16
 F32 = jnp.float32
 BD = 256
-INFO = 32
-ROWS = 4 * BD + INFO
+INFO = 16
+ROWS = BD + INFO
 BATCH = 8
 CHUNKS = (4, 4, 4, 2, 2)
 STRIP = 32
@@ -29,6 +29,15 @@
     return [(device(o, b), device(o ^ 16, b ^ 2)) for o in range(32) for b in range(4)]
 
 
+def flip_pairs(bit):
+    return [(o, o ^ bit) for o in range(32)]
+
+
+def color_of(op):
+    x, y, z = op & 1, (op >> 2) & 1, op >> 4
+    return (x ^ z) + 2 * (y ^ z)
+
+
 def core_pairs():
     return [(b, b ^ 1) for b in range(4)]
 
@@ -43,7 +52,7 @@
     return (row_ids < rows) & (col_ids < cols)
 
 
-def pack_kernel(dims_in, energy_in, wave_in, out, dims, energy, wave, sems):
+def pack_kernel(dims_in, energy_in, wave_in, out, first, dims, energy, wave, sems):
     copies = [
         pltpu.make_async_copy(dims_in, dims, sems.at[0]),
         pltpu.make_async_copy(energy_in, energy, sems.at[1]),
@@ -53,21 +62,20 @@
         copy.start()
     for copy in copies:
         copy.wait()
+    row = lax.broadcasted_iota(jnp.int32, (INFO, BD), 0)
     for b in range(4):
         mask = live(dims[0, b], dims[1, b], (BD, BD))
-        block = jnp.where(mask, wave[b].astype(F32), 0.0)
-        out[b * BD:(b + 1) * BD, :] = block.astype(BF)
-    row = lax.broadcasted_iota(jnp.int32, (INFO, BD), 0)
-    info = jnp.zeros((INFO, BD), F32)
-    for b in range(4):
+        out[b, :BD] = jnp.where(mask, wave[b].astype(F32), 0.0).astype(BF)
         value = jnp.full((INFO, BD), energy[b], F32)
         high = value.astype(BF).astype(F32)
         middle = (value - high).astype(BF).astype(F32)
         low = value - high - middle
+        info = jnp.zeros((INFO, BD), F32)
         parts = (dims[0, b].astype(F32), dims[1, b].astype(F32), high, middle, low)
         for j, part in enumerate(parts):
-            info = jnp.where(row == b * 8 + j, part, info)
-    out[4 * BD:, :] = info.astype(BF)
+            info = jnp.where(row == j, part, info)
+        out[b, BD:] = info.astype(BF)
+    first[...] = out[color_of(lax.axis_index("op")) ^ 3]
 
 
 def slot_terms(src, vec, left, right, e, terms):
@@ -94,8 +102,8 @@
 
 
 def wave_kernel(
-    src_in, ids, own, far, core, far_core, left_in, right_in,
-    out, vec, info, left, right, src, acc, src_sem, sems,
+    src_in, own, core, far0, far1, far2, far3, near0, near1, near2, near3,
+    left_in, right_in, out, vec, info, left, right, src, acc, src_sem, sems,
 ):
     src_copy = pltpu.make_async_copy(src_in, src, src_sem)
     src_copy.start()
@@ -110,15 +118,18 @@
     for copies in chunks:
         for copy in copies:
             copy.start()
-    for flip, piece in ((0, own), (2, far), (1, core), (3, far_core)):
-        group = ids[0] ^ flip
-        rows = piece[4 * BD:, :].astype(F32)
-        for b in range(4):
-            vec[group * 4 + b] = piece[b * BD:(b + 1) * BD, :]
-            entry = rows[b * 8:(b + 1) * 8, :]
-            level = entry[2:3] + entry[3:4] + entry[4:5]
-            info[group * 4 + b, 0:2] = entry[0:2]
-            info[group * 4 + b, 2:3] = level
+    blocks = []
+    for b in range(4):
+        blocks.append((lax.axis_index("blk") * 4 + b, own.at[b]))
+        blocks.append(((lax.axis_index("blk") ^ 1) * 4 + b, core.at[b]))
+    for flip, pieces in ((2, (far0, far1, far2, far3)), (3, (near0, near1, near2, near3))):
+        for b, piece in enumerate(pieces):
+            blocks.append(((lax.axis_index("blk") ^ flip) * 4 + (color_of(lax.axis_index("op")) ^ b), piece))
+    for block, piece in blocks:
+        vec[block] = piece[:BD]
+        entry = piece[BD:].astype(F32)
+        info[block, 0:2] = entry[0:2]
+        info[block, 2:3] = entry[2:3] + entry[3:4] + entry[4:5]
     src_copy.wait()
     for i, copies in enumerate(chunks):
         for copy in copies:
@@ -142,45 +153,57 @@
 
 
 def corr_kernel(
-    src, ids, wave, info, same, other, left, right,
-    applied_out, corr_out, out, vec, acc, work,
+    src, wave, info, same, other, left, right,
+    applied_out, corr_out, out, vec, acc, work, applied, applied_sem,
 ):
     entries = 16 * BD * BD
-    me = ids[0]
+    me = lax.axis_index("blk")
     zero = jnp.zeros((8, BD), F32)
     strips = [pl.ds(r, STRIP) for r in range(0, BD, STRIP)]
 
-    def apply(group, sums):
+    def summed(group, turn):
+        b = me ^ turn
+        return b, (same if turn % 2 == 0 else other).at[b >> 1, group]
+
+    def cross_sums(group, sums):
         cross, square = sums
         for turn in range(4):
-            b = me ^ turn
-            summed = same if turn % 2 == 0 else other
+            b, values = summed(group, turn)
             block = group * 4 + b
-            level = info[block, 2:3]
+            part, own_part = zero, zero
             for rows in strips:
                 vector = wave[block, rows].astype(F32)
-                applied = summed[b >> 1, group, rows].astype(F32) + level * vector
-                work[block, rows] = applied
-                cross += fold(applied * vector)
-                square += fold(vector * vector)
+                part += fold(values[rows].astype(F32) * vector)
+                own_part += fold(vector * vector)
+            cross += part + info[block, 2:3] * own_part
+            square += own_part
         return cross, square
 
-    cross, square = lax.fori_loop(0, 4, apply, (zero, zero))
-    for b in range(4):
-        applied_out[b] = work[me * 4 + b]
+    cross, square = lax.fori_loop(0, 4, cross_sums, (zero, zero))
     rayleigh = total_of(cross) / entries / (total_of(square) / entries + 1e-06)
 
     def subtract(group, resid):
-        for b in range(4):
+        for turn in range(4):
+            b, values = summed(group, turn)
+            block = group * 4 + b
+            level = info[block, 2:3] - rayleigh
             for rows in strips:
-                vector = wave[group * 4 + b, rows].astype(F32)
-                rest = work[group * 4 + b, rows] - rayleigh * vector
-                work[group * 4 + b, rows] = rest
+                rest = values[rows].astype(F32) + level * wave[block, rows].astype(F32)
+                work[block, rows] = rest
                 resid += fold(rest * rest)
         return resid
 
     resid = lax.fori_loop(0, 4, subtract, zero)
     scale = lax.rsqrt(total_of(resid) / entries + 1e-06)
+    for turn in range(4):
+        b, values = summed(me, turn)
+        level = info[me * 4 + b, 2:3]
+        for rows in strips:
+            vector = wave[me * 4 + b, rows].astype(F32)
+            applied[b, rows] = values[rows].astype(F32) + level * vector
+
+    applied_copy = pltpu.make_async_copy(applied, applied_out, applied_sem)
+    applied_copy.start()
 
     @pl.loop(0, 4)
     def _(group):
@@ -197,11 +220,12 @@
             for j in range(2):
                 tile = acc[e, i * 16:(i + 1) * 16, j * 128:(j + 1) * 128]
                 out[i * 2 + j, e] = tile.astype(BF)
-
-
-def sum_wave_kernel(ids, info, parts, out):
-    part = ids[1]
-    entry = info[(part >> 3) * 4 + ids[0]]
+    applied_copy.wait()
+
+
+def sum_wave_kernel(info, parts, out):
+    part = lax.axis_index("op")
+    entry = info[(part >> 3) * 4 + lax.axis_index("blk")]
     mask = live(entry[0:1], entry[1:2], (STRIP, BD), (part & 7) * STRIP)
     total = jnp.sum(parts[...].astype(F32), axis=0)
     total = jnp.where(mask, total, 0.0).astype(BF)
@@ -209,11 +233,11 @@
         out[i] = total
 
 
-def sum_corr_kernel(ids, info, parts, out):
-    part = ids[1]
+def sum_corr_kernel(info, parts, out):
+    part = lax.axis_index("op")
     totals = []
     for b in range(4):
-        entry = info[ids[0] * 4 + b][:, :128]
+        entry = info[lax.axis_index("blk") * 4 + b][:, :128]
         total = jnp.sum(parts[:, b].astype(F32), axis=0)
         mask = live(entry[0:1], entry[1:2], (16, 128), (part >> 1) * 16, (part & 1) * 128)
         totals.append(jnp.where(mask, total, 0.0).astype(BF))
@@ -222,13 +246,18 @@
             out[i, b] = totals[b]
 
 
-def final_kernel(ids, info, parts, corr, out):
-    for b in range(4):
-        level = info[ids[0] * 4 + b, 2:3]
+def final_kernel(info, parts, corr, out, blocks, sems):
+    copies = []
+    for b in range(4):
+        level = info[lax.axis_index("blk") * 4 + b, 2:3]
         for i in range(16):
             rows = pl.ds(i * 16, 16)
             summed = jnp.concatenate([parts[2 * i, b], parts[2 * i + 1, b]], axis=1)
-            out[b, rows] = summed.astype(F32) + level * corr[b, rows].astype(F32)
+            blocks[b, rows] = summed.astype(F32) + level * corr[b, rows].astype(F32)
+        copies.append(pltpu.make_async_copy(blocks.at[b], out.at[b], sems.at[b]))
+        copies[b].start()
+    for copy in copies:
+        copy.wait()
 
 
 def params(mib):
@@ -240,14 +269,13 @@
 
 
 def shards(wave_blocks, left_env, right_env, source, block_dims, energy):
-    ids = jnp.stack([lax.axis_index("blk"), lax.axis_index("op")]).astype(jnp.int32)
     src = source.T
 
-    own = pl.pallas_call(
+    own, first = pl.pallas_call(
         pack_kernel,
-        out_shape=shape((ROWS, BD)),
+        out_shape=(shape((4, ROWS, BD)), shape((ROWS, BD))),
         in_specs=[HBM, HBM, HBM],
-        out_specs=VMEM,
+        out_specs=(VMEM, VMEM),
         scratch_shapes=[
             pltpu.SMEM((2, 4), jnp.int32),
             pltpu.SMEM((4,), F32),
@@ -257,9 +285,11 @@
         compiler_params=params(8),
         name="pack",
     )(*(pltpu.with_memory_space_constraint(x, pltpu.HBM) for x in (block_dims, energy, wave_blocks)))
-    far = lax.ppermute(own, ALL, cross_pairs())
+    far = [lax.ppermute(first, ALL, cross_pairs())]
     core = lax.ppermute(own, "blk", core_pairs())
-    far_core = lax.ppermute(far, "blk", core_pairs())
+    for bit in (1, 4, 16):
+        far.append(lax.ppermute(far[0], "op", flip_pairs(bit)))
+    near = [lax.ppermute(piece, "blk", core_pairs()) for piece in far]
 
     partial, wave, info, left, right = pl.pallas_call(
         wave_kernel,
@@ -267,7 +297,7 @@
             shape((4, BD, BD)), shape((16, BD, BD)), shape((16, 8, BD), F32),
             pltpu.VMEM(left_env.shape, BF), pltpu.VMEM(right_env.shape, BF),
         ),
-        in_specs=[HBM, SMEM] + [VMEM] * 4 + [HBM, HBM],
+        in_specs=[HBM] + [VMEM] * 10 + [HBM, HBM],
         out_specs=(VMEM,) * 5,
         scratch_shapes=[
             pltpu.SMEM((4, 16), jnp.int32),
@@ -278,7 +308,7 @@
         compiler_params=params(14),
         name="wave_terms",
     )(
-        pltpu.with_memory_space_constraint(src, pltpu.HBM), ids, own, far, core, far_core,
+        pltpu.with_memory_space_constraint(src, pltpu.HBM), own, core, *far, *near,
         pltpu.with_memory_space_constraint(left_env, pltpu.HBM),
         pltpu.with_memory_space_constraint(right_env, pltpu.HBM),
     )
@@ -287,11 +317,11 @@
     copies = pl.pallas_call(
         sum_wave_kernel,
         out_shape=shape((64, 32, BD)),
-        in_specs=[SMEM, VMEM, VMEM],
+        in_specs=[VMEM, VMEM],
         out_specs=VMEM,
         compiler_params=params(8),
         name="sum_wave",
-    )(ids, info, pieces)
+    )(info, pieces)
     same = lax.all_to_all(
         copies, ALL, 0, 0, tiled=True, axis_index_groups=core_groups()
     )
@@ -300,17 +330,19 @@
     applied_wave, corr, partial = pl.pallas_call(
         corr_kernel,
         out_shape=(shape((4, BD, BD), F32), shape((4, BD, BD)), shape((32, 4, 16, 128))),
-        in_specs=[SMEM, SMEM] + [VMEM] * 6,
-        out_specs=(VMEM, VMEM, VMEM),
+        in_specs=[SMEM] + [VMEM] * 6,
+        out_specs=(HBM, VMEM, VMEM),
         scratch_shapes=[
             pltpu.VMEM((16, BD, BD), BF),
             pltpu.VMEM((4, BD, BD), F32),
             pltpu.VMEM((16, BD, BD), F32),
+            pltpu.VMEM((4, BD, BD), F32),
+            pltpu.SemaphoreType.DMA,
         ],
         compiler_params=params(14),
         name="corr_terms",
     )(
-        src, ids, wave, info,
+        src, wave, info,
         same.reshape(2, 4, BD, BD), other.reshape(2, 4, BD, BD), left, right,
     )
 
@@ -318,20 +350,21 @@
     copies = pl.pallas_call(
         sum_corr_kernel,
         out_shape=shape((32, 4, 16, 128)),
-        in_specs=[SMEM, VMEM, VMEM],
+        in_specs=[VMEM, VMEM],
         out_specs=VMEM,
         compiler_params=params(8),
         name="sum_corr",
-    )(ids, info, pieces.reshape(32, 4, 16, 128))
+    )(info, pieces.reshape(32, 4, 16, 128))
     gathered = lax.all_to_all(copies, "op", 0, 0, tiled=True)
     applied_corr = pl.pallas_call(
         final_kernel,
         out_shape=shape((4, BD, BD), F32),
-        in_specs=[SMEM, VMEM, VMEM, VMEM],
-        out_specs=VMEM,
+        in_specs=[VMEM, VMEM, VMEM],
+        out_specs=HBM,
+        scratch_shapes=[pltpu.VMEM((4, BD, BD), F32), pltpu.SemaphoreType.DMA((4,))],
         compiler_params=params(8),
         name="finish",
-    )(ids, info, gathered, corr)
+    )(info, gathered, corr)
     return (applied_wave, applied_corr)
 
 

time: 120 us -> 115 us (0.958)
  waiting for transfers between devices: 16.8 us -> 11.4 us
  starting transfers between devices: 4.21 us -> 7.87 us
  Pallas kernels: 21.1 us -> 17.8 us
    ppermute x2 -> x8, waiting for transfers between devices: 14.1 us -> 8.73 us  [the longest x1 4.25 us: shards(): far = [lax.ppermute(first, ALL, cross_pairs())]]
    ppermute x2 -> x8, starting transfers between devices: 4.2 us -> 7.79 us  [the longest x1 4.2 us: shards(): far = [lax.ppermute(first, ALL, cross_pairs())]]
  transfers between devices with their start and end apart: 4 -> 10, of which waited for: 3 -> 7; matrix products, arithmetic and copies ran while one was open for 0% -> 0% of each run, Pallas kernels for 0% -> 0%
where the time goes in v3:
time: 115 us
  blocking collectives  76.7 us (67%)
  Pallas kernels  17.8 us (15%)
  waiting for transfers between devices  11.4 us (10%)
  starting transfers between devices  7.87 us (7%)
    all_to_all x1, blocking collectives, shards(): lax.all_to_all(copies, ALL, 0, 0, tiled=True, axis_index_groups=core_grou...  24.9 us
    all_to_all x1, blocking collectives, shards(): pieces = lax.all_to_all(partial.reshape(32, 32, BD), 'op', 0, 0, tiled=True)  19.8 us
    all_to_all x1, blocking collectives, shards(): lax.all_to_all(partial.reshape(128, 16, 128), ALL, 0, 0, tiled=True)  16.7 us
    all_to_all x1, blocking collectives, shards(): gathered = lax.all_to_all(copies, 'op', 0, 0, tiled=True)  15.3 us
    pallas_call x1, Pallas kernels, shards(): pl.pallas_call(wave_kernel, out_shape=(shape((4, BD, BD)), shape((16, BD,...  7.63 us
    pallas_call x1, Pallas kernels, shards(): pl.pallas_call(corr_kernel, out_shape=(shape((4, BD, BD), F32), shape((4,...  7.61 us
    ppermute x1, waiting for transfers between devices, shards(): far = [lax.ppermute(first, ALL, cross_pairs())]  4.25 us
    ppermute x1, starting transfers between devices, shards(): far = [lax.ppermute(first, ALL, cross_pairs())]  4.2 us
  transfers between devices with their start and end apart: 10, of which 7 were waited for; matrix products, arithmetic and copies ran while one was open for 0% of the time, Pallas kernels for 0%

profile of v3, /device:TPU:0, one launch (start us, length us, event | category | flops | bytes accessed | tf_op | source)
XLA Modules:
  0.0 114.7 jit_solution(14060645847920988302)
XLA Ops:
  0.6 1.3 %pack.1 = (bf16[4,272,256]{2,1,0:T(8,128)(2,1)S(1)}, bf16[272,256]{1,0:T(8,128)(2,1)S(1)}) custom-call(s32[2,4]{1,0:T(2,128)} %dims_in.1, f32[4]{0:T(128)} %energy_in.1, bf16[4,256,256]{2,1,0:T(8,128)(2,1)} %wave_in.1), custom_call_target="tpu_custom_call" | custom-call | tf_op jit(solution)/shard_map/pack/pallas_call | solution.py:274
  1.9 0.1 collective-permute-start
  2.0 4.2 %collective-permute-start.1 = (bf16[272,256]{1,0:T(8,128)(2,1)S(1)}, bf16[272,256]{1,0:T(8,128)(2,1)S(1)}, u32[]{:S(2)}, u32[]{:S(2)}) collective-permute-start(bf16[272,256]{1,0:T(8,128)(2,1)S(1)} %get-tuple-element.13), channel_id=1, source_target_pairs={{0,66},{1,67},{2,64},{3,65},{4,70},{5,71},{6,68},{7,69},{8,74},{9,... | collective-permute-start | bytes 417800 | tf_op jit(solution)/shard_map/ppermute | solution.py:288
  6.2 4.3 %collective-permute-done.1.far0 = bf16[272,256]{1,0:T(8,128)(2,1)S(1)} collective-permute-done((bf16[272,256]{1,0:T(8,128)(2,1)S(1)}, bf16[272,256]{1,0:T(8,128)(2,1)S(1)}, u32[]{:S(2)}, u32[]{:S(2)}) %collective-permute-start.1) | collective-permute-done | bytes 139296 | tf_op jit(solution)/shard_map/ppermute | solution.py:288
  10.5 0.0 collective-permute-start.4
  10.5 1.6 %collective-permute-start.3 = (bf16[272,256]{1,0:T(8,128)(2,1)S(1)}, bf16[272,256]{1,0:T(8,128)(2,1)S(1)}, u32[]{:S(2)}, u32[]{:S(2)}) collective-permute-start(bf16[272,256]{1,0:T(8,128)(2,1)S(1)} %collective-permute-done.1.far0), channel_id=1, source_target_pairs={{0,16},{4,20},{8,24},{12,28},{16,0},{20,4},{24,8},{28,12},{32,48},... | collective-permute-start | bytes 417800 | tf_op jit(solution)/shard_map/ppermute | solution.py:291
  12.0 1.5 %collective-permute-start.2 = (bf16[272,256]{1,0:T(8,128)(2,1)S(1)}, bf16[272,256]{1,0:T(8,128)(2,1)S(1)}, u32[]{:S(2)}, u32[]{:S(2)}) collective-permute-start(bf16[272,256]{1,0:T(8,128)(2,1)S(1)} %collective-permute-done.1.far0), channel_id=1, source_target_pairs={{0,4},{4,0},{8,12},{12,8},{16,20},{20,16},{24,28},{28,24},{32,36},... | collective-permute-start | bytes 417800 | tf_op jit(solution)/shard_map/ppermute | solution.py:291
  13.5 0.0 collective-permute-start.5
  13.5 2.3 %collective-permute-done.4.far3 = bf16[272,256]{1,0:T(8,128)(2,1)S(1)} collective-permute-done((bf16[272,256]{1,0:T(8,128)(2,1)S(1)}, bf16[272,256]{1,0:T(8,128)(2,1)S(1)}, u32[]{:S(2)}, u32[]{:S(2)}) %collective-permute-start.4) | collective-permute-done | bytes 139296 | tf_op jit(solution)/shard_map/ppermute | solution.py:291
  15.9 0.0 collective-permute-start.8
  15.9 0.0 collective-permute-done.3.far2
  15.9 0.5 collective-permute-start.7
  16.4 0.8 collective-permute-done.2.far1
  17.2 0.0 collective-permute-start.6
  17.2 0.0 collective-permute-done.5.near0
  17.2 0.1 collective-permute-done.8.near3
  17.2 0.2 collective-permute-done.7.near2
  17.4 1.1 collective-permute-done.6.near1
  18.5 0.0 collective-permute-done.core
  18.5 0.0 copy-start
  18.5 7.6 %wave_terms.1 = (bf16[4,256,256]{2,1,0:T(8,128)(2,1)S(1)}, bf16[16,256,256]{2,1,0:T(8,128)(2,1)S(1)}, f32[16,8,256]{2,1,0:T(8,128)S(1)}, bf16[16,4,256,256]{3,2,...) custom-call(s32[4,16]{1,0:T(4,128)} %bitcast.11, bf16[4,272,256]{2,1,0:T(8,128)(2,1)S(1)} %get-tuple-element.12.own, ...), custom_call_target="tpu_custom_call" | custom-call | tf_op jit(solution)/shard_map/wave_terms/pallas_call | solution.py:294
  26.2 19.8 %all_to_all.20.parts = bf16[32,32,256]{2,1,0:T(8,128)(2,1)S(1)} all-to-all(bf16[32,32,256]{2,1,0:T(8,128)(2,1)S(1)} %bitcast.9), channel_id=1, replica_groups=mesh['op'=32,'blk'=4] {'op'}, dimensions={0} | all-to-all | bytes 1048576 | tf_op jit(solution)/shard_map/all_to_all | solution.py:316
  46.0 0.2 sum_wave.1
  46.1 24.9 %all_to_all.21 = bf16[64,32,256]{2,1,0:T(8,128)(2,1)S(1)} all-to-all(bf16[64,32,256]{2,1,0:T(8,128)(2,1)S(1)} %sum_wave.1), channel_id=1, replica_groups={{0,4,8,12,16,20,24,28,32,36,40,44,48,52,56,60,64,68,72,76,80,84,88,92,9..., dimensions={0} | all-to-all | bytes 2097152 | tf_op jit(solution)/shard_map/all_to_all | solution.py:325
  71.0 0.0 collective-permute-start.9
  71.0 2.7 %collective-permute-done.9 = bf16[64,32,256]{2,1,0:T(8,128)(2,1)S(1)} collective-permute-done((bf16[64,32,256]{2,1,0:T(8,128)(2,1)S(1)}, bf16[64,32,256]{2,1,0:T(8,128)(2,1)S(1)}, u32[]{:S(2)}, u32[]{:S(2)}) %collective-permute-start.9) | collective-permute-done | bytes 1048608 | tf_op jit(solution)/shard_map/ppermute | solution.py:328
  73.7 0.0 copy-done
  73.7 7.6 %corr_terms.1 = (f32[4,256,256]{2,1,0:T(8,128)}, bf16[4,256,256]{2,1,0:T(8,128)(2,1)S(1)}, bf16[32,4,16,128]{3,2,1,0:T(8,128)(2,1)S(1)}) custom-call(s32[4,16]{1,0:T(4,128)S(1)} %bitcast.12, bf16[16,256,256]{2,1,0:T(8,128)(2,1)S(1)} %get-tuple-element.14.wave, f32[16,8,256]{2,1,0:T(8,128)S(1)} %get-tuple-element.15.info, ...), custom_call_target="tpu_custom_call" | custom-call | tf_op jit(solution)/shard_map/corr_terms/pallas_call | solution.py:330
  81.3 16.7 %all_to_all.22 = bf16[128,16,128]{2,1,0:T(8,128)(2,1)S(1)} all-to-all(bf16[128,16,128]{2,1,0:T(8,128)(2,1)S(1)} %bitcast.10), channel_id=1, replica_groups=mesh['op'=32,'blk'=4] {'op','blk'}, dimensions={0} | all-to-all | bytes 1048576 | tf_op jit(solution)/shard_map/all_to_all | solution.py:349
  98.1 0.1 sum_corr.1
  98.2 15.3 %all_to_all.23.parts = bf16[32,4,16,128]{3,2,1,0:T(8,128)(2,1)S(1)} all-to-all(bf16[32,4,16,128]{3,2,1,0:T(8,128)(2,1)S(1)} %sum_corr.1), channel_id=1, replica_groups=mesh['op'=32,'blk'=4] {'op'}, dimensions={0} | all-to-all | bytes 1048576 | tf_op jit(solution)/shard_map/all_to_all | solution.py:358
  113.5 1.0 finish.1
Async XLA Ops:
  1.9 16.6 %collective-permute-start = (bf16[4,272,256]{2,1,0:T(8,128)(2,1)S(1)}, bf16[4,272,256]{2,1,0:T(8,128)(2,1)S(1)}, u32[]{:S(2)}, u32[]{:S(2)}) collective-permute-start(bf16[4,272,256]{2,1,0:T(8,128)(2,1)S(1)} %get-tuple-element.12.own), channel_id=1, source_target_pairs={{0,1},{1,0},{2,3},{3,2},{4,5},{5,4},{6,7},{7,6},{8,9},{9,8},{10,11... | collective-permute-start | bytes 1671176 | tf_op jit(solution)/shard_map/ppermute | solution.py:289
  2.0 8.5 %collective-permute-start.1 = (bf16[272,256]{1,0:T(8,128)(2,1)S(1)}, bf16[272,256]{1,0:T(8,128)(2,1)S(1)}, u32[]{:S(2)}, u32[]{:S(2)}) collective-permute-start(bf16[272,256]{1,0:T(8,128)(2,1)S(1)} %get-tuple-element.13), channel_id=1, source_target_pairs={{0,66},{1,67},{2,64},{3,65},{4,70},{5,71},{6,68},{7,69},{8,74},{9,... | collective-permute-start | bytes 417800 | tf_op jit(solution)/shard_map/ppermute | solution.py:288
  10.5 5.4 %collective-permute-start.4 = (bf16[272,256]{1,0:T(8,128)(2,1)S(1)}, bf16[272,256]{1,0:T(8,128)(2,1)S(1)}, u32[]{:S(2)}, u32[]{:S(2)}) collective-permute-start(bf16[272,256]{1,0:T(8,128)(2,1)S(1)} %collective-permute-done.1.far0), channel_id=1, source_target_pairs={{0,64},{4,68},{8,72},{12,76},{16,80},{20,84},{24,88},{28,92},{32,9... | collective-permute-start | bytes 417800 | tf_op jit(solution)/shard_map/ppermute | solution.py:291
  10.5 5.4 %collective-permute-start.3 = (bf16[272,256]{1,0:T(8,128)(2,1)S(1)}, bf16[272,256]{1,0:T(8,128)(2,1)S(1)}, u32[]{:S(2)}, u32[]{:S(2)}) collective-permute-start(bf16[272,256]{1,0:T(8,128)(2,1)S(1)} %collective-permute-done.1.far0), channel_id=1, source_target_pairs={{0,16},{4,20},{8,24},{12,28},{16,0},{20,4},{24,8},{28,12},{32,48},... | collective-permute-start | bytes 417800 | tf_op jit(solution)/shard_map/ppermute | solution.py:291
  12.0 5.1 %collective-permute-start.2 = (bf16[272,256]{1,0:T(8,128)(2,1)S(1)}, bf16[272,256]{1,0:T(8,128)(2,1)S(1)}, u32[]{:S(2)}, u32[]{:S(2)}) collective-permute-start(bf16[272,256]{1,0:T(8,128)(2,1)S(1)} %collective-permute-done.1.far0), channel_id=1, source_target_pairs={{0,4},{4,0},{8,12},{12,8},{16,20},{20,16},{24,28},{28,24},{32,36},... | collective-permute-start | bytes 417800 | tf_op jit(solution)/shard_map/ppermute | solution.py:291
  13.5 3.6 %collective-permute-start.5 = (bf16[272,256]{1,0:T(8,128)(2,1)S(1)}, bf16[272,256]{1,0:T(8,128)(2,1)S(1)}, u32[]{:S(2)}, u32[]{:S(2)}) collective-permute-start(bf16[272,256]{1,0:T(8,128)(2,1)S(1)} %collective-permute-done.1.far0), channel_id=1, source_target_pairs={{0,1},{1,0},{2,3},{3,2},{4,5},{5,4},{6,7},{7,6},{8,9},{9,8},{10,11... | collective-permute-start | bytes 417800 | tf_op jit(solution)/shard_map/ppermute | solution.py:292
  15.9 1.4 %collective-permute-start.8 = (bf16[272,256]{1,0:T(8,128)(2,1)S(1)}, bf16[272,256]{1,0:T(8,128)(2,1)S(1)}, u32[]{:S(2)}, u32[]{:S(2)}) collective-permute-start(bf16[272,256]{1,0:T(8,128)(2,1)S(1)} %collective-permute-done.4.far3), channel_id=1, source_target_pairs={{0,1},{1,0},{2,3},{3,2},{4,5},{5,4},{6,7},{7,6},{8,9},{9,8},{10,11... | collective-permute-start | bytes 417800 | tf_op jit(solution)/shard_map/ppermute | solution.py:292
  15.9 1.6 %collective-permute-start.7 = (bf16[272,256]{1,0:T(8,128)(2,1)S(1)}, bf16[272,256]{1,0:T(8,128)(2,1)S(1)}, u32[]{:S(2)}, u32[]{:S(2)}) collective-permute-start(bf16[272,256]{1,0:T(8,128)(2,1)S(1)} %collective-permute-done.3.far2), channel_id=1, source_target_pairs={{0,1},{1,0},{2,3},{3,2},{4,5},{5,4},{6,7},{7,6},{8,9},{9,8},{10,11... | collective-permute-start | bytes 417800 | tf_op jit(solution)/shard_map/ppermute | solution.py:292
  17.2 1.4 %collective-permute-start.6 = (bf16[272,256]{1,0:T(8,128)(2,1)S(1)}, bf16[272,256]{1,0:T(8,128)(2,1)S(1)}, u32[]{:S(2)}, u32[]{:S(2)}) collective-permute-start(bf16[272,256]{1,0:T(8,128)(2,1)S(1)} %collective-permute-done.2.far1), channel_id=1, source_target_pairs={{0,1},{1,0},{2,3},{3,2},{4,5},{5,4},{6,7},{7,6},{8,9},{9,8},{10,11... | collective-permute-start | bytes 417800 | tf_op jit(solution)/shard_map/ppermute | solution.py:292
  18.5 55.2 %copy-start = (s32[16,4]{0,1:T(4,128)S(1)}, s32[16,4]{0,1:T(4,128)}, u32[]{:S(2)}) copy-start(s32[16,4]{0,1:T(4,128)} %param.9) | copy-start | bytes 772
  71.0 2.7 %collective-permute-start.9 = (bf16[64,32,256]{2,1,0:T(8,128)(2,1)S(1)}, bf16[64,32,256]{2,1,0:T(8,128)(2,1)S(1)}, u32[]{:S(2)}, u32[]{:S(2)}) collective-permute-start(bf16[64,32,256]{2,1,0:T(8,128)(2,1)S(1)} %all_to_all.21), channel_id=1, source_target_pairs={{0,1},{1,0},{2,3},{3,2},{4,5},{5,4},{6,7},{7,6},{8,9},{9,8},{10,11... | collective-permute-start | bytes 3145736 | tf_op jit(solution)/shard_map/ppermute | solution.py:328

commit v4 on v3

--- a/solution.py
+++ b/solution.py
@@ -10,8 +10,7 @@
 BD = 256
 INFO = 16
 ROWS = BD + INFO
-BATCH = 8
-CHUNKS = (4, 4, 4, 2, 2)
+HALF = 8
 STRIP = 32
 MIB = 1 << 20
 ALL = ("op", "blk")
@@ -78,70 +77,58 @@
     first[...] = out[color_of(lax.axis_index("op")) ^ 3]
 
 
-def slot_terms(src, vec, left, right, e, terms):
+def load_kernel(left, right, left_out, right_out, token, sems):
+    copies = [
+        pltpu.make_async_copy(left, left_out, sems.at[0]),
+        pltpu.make_async_copy(right.at[pl.ds(0, HALF)], right_out, sems.at[1]),
+    ]
+    for copy in copies:
+        copy.start()
+    token[...] = jnp.zeros_like(token)
+    for copy in copies:
+        copy.wait()
+
+
+def slot_terms(src, vec, left, right, e, first):
     inner = [
-        jnp.dot(left[t, e], vec[src[e, t]], preferred_element_type=F32).astype(BF)
-        for t in terms
+        jnp.dot(left[first + t, e], vec[src[e, first + t]], preferred_element_type=F32).astype(BF)
+        for t in range(HALF)
     ]
     return lax.dot_general(
         jnp.concatenate(inner, axis=1),
-        jnp.concatenate([right[t, e] for t in terms], axis=1),
+        jnp.concatenate([right[t, e] for t in range(HALF)], axis=1),
         (((1,), (1,)), ((), ())),
         preferred_element_type=F32,
     )
 
 
-def add_terms(src, vec, left, right, acc):
-    acc[...] = jnp.zeros_like(acc)
-
-    @pl.loop(0, left.shape[0] // BATCH)
-    def _(step):
-        terms = [step * BATCH + t for t in range(BATCH)]
-        for e in range(4):
-            acc[e] += slot_terms(src, vec, left, right, e, terms)
-
-
 def wave_kernel(
     src_in, own, core, far0, far1, far2, far3, near0, near1, near2, near3,
-    left_in, right_in, out, vec, info, left, right, src, acc, src_sem, sems,
+    left, right_a, right_in, token, out, vec, info, right_b, src, acc, src_sem, sem,
 ):
     src_copy = pltpu.make_async_copy(src_in, src, src_sem)
     src_copy.start()
-    starts = [sum(CHUNKS[:i]) for i in range(len(CHUNKS))]
-    chunks = []
-    for i, (start, size) in enumerate(zip(starts, CHUNKS)):
-        terms = pl.ds(start, size)
-        chunks.append([
-            pltpu.make_async_copy(left_in.at[terms], left.at[terms], sems.at[0, i]),
-            pltpu.make_async_copy(right_in.at[terms], right.at[terms], sems.at[1, i]),
-        ])
-    for copies in chunks:
-        for copy in copies:
-            copy.start()
+    right_copy = pltpu.make_async_copy(right_in.at[pl.ds(HALF, HALF)], right_b, sem)
+    right_copy.start()
+    me, color = lax.axis_index("blk"), color_of(lax.axis_index("op"))
     blocks = []
     for b in range(4):
-        blocks.append((lax.axis_index("blk") * 4 + b, own.at[b]))
-        blocks.append(((lax.axis_index("blk") ^ 1) * 4 + b, core.at[b]))
+        blocks.append((me * 4 + b, own.at[b]))
+        blocks.append(((me ^ 1) * 4 + b, core.at[b]))
     for flip, pieces in ((2, (far0, far1, far2, far3)), (3, (near0, near1, near2, near3))):
         for b, piece in enumerate(pieces):
-            blocks.append(((lax.axis_index("blk") ^ flip) * 4 + (color_of(lax.axis_index("op")) ^ b), piece))
+            blocks.append(((me ^ flip) * 4 + (color ^ b), piece))
     for block, piece in blocks:
         vec[block] = piece[:BD]
         entry = piece[BD:].astype(F32)
         info[block, 0:2] = entry[0:2]
         info[block, 2:3] = entry[2:3] + entry[3:4] + entry[4:5]
     src_copy.wait()
-    for i, copies in enumerate(chunks):
-        for copy in copies:
-            copy.wait()
-        terms = range(starts[i], starts[i] + CHUNKS[i])
-        for e in range(4):
-            product = slot_terms(src, vec, left, right, e, terms)
-            total = product if i == 0 else acc[e] + product
-            if i == len(chunks) - 1:
-                out[e] = total.astype(BF)
-            else:
-                acc[e] = total
+    for e in range(4):
+        acc[e] = slot_terms(src, vec, left, right_a, e, 0)
+    right_copy.wait()
+    for e in range(4):
+        out[e] = (acc[e] + slot_terms(src, vec, left, right_b, e, HALF)).astype(BF)
 
 
 def total_of(x):
@@ -153,7 +140,7 @@
 
 
 def corr_kernel(
-    src, wave, info, same, other, left, right,
+    src, wave, info, same, other, left, right_a, right_b,
     applied_out, corr_out, out, vec, acc, work, applied, applied_sem,
 ):
     entries = 16 * BD * BD
@@ -214,11 +201,13 @@
     for b in range(4):
         corr_out[b] = vec[me * 4 + b]
 
-    add_terms(src, vec, left, right, acc)
     for e in range(4):
+        acc[e] = slot_terms(src, vec, left, right_a, e, 0)
+    for e in range(4):
+        total = acc[e] + slot_terms(src, vec, left, right_b, e, HALF)
         for i in range(16):
             for j in range(2):
-                tile = acc[e, i * 16:(i + 1) * 16, j * 128:(j + 1) * 128]
+                tile = total[i * 16:(i + 1) * 16, j * 128:(j + 1) * 128]
                 out[i * 2 + j, e] = tile.astype(BF)
     applied_copy.wait()
 
@@ -286,31 +275,43 @@
         name="pack",
     )(*(pltpu.with_memory_space_constraint(x, pltpu.HBM) for x in (block_dims, energy, wave_blocks)))
     far = [lax.ppermute(first, ALL, cross_pairs())]
+    left_in, right_in = (
+        pltpu.with_memory_space_constraint(x, pltpu.HBM) for x in (left_env, right_env)
+    )
+    half = (HALF,) + right_env.shape[1:]
+    left, right_a, token = pl.pallas_call(
+        load_kernel,
+        out_shape=(pltpu.VMEM(left_env.shape, BF), pltpu.VMEM(half, BF), shape((8, 128), F32)),
+        in_specs=[HBM, HBM],
+        out_specs=(VMEM, VMEM, VMEM),
+        scratch_shapes=[pltpu.SemaphoreType.DMA((2,))],
+        compiler_params=params(1),
+        name="load",
+    )(left_in, right_in)
+    far[0], token = lax.optimization_barrier((far[0], token))
     core = lax.ppermute(own, "blk", core_pairs())
     for bit in (1, 4, 16):
         far.append(lax.ppermute(far[0], "op", flip_pairs(bit)))
     near = [lax.ppermute(piece, "blk", core_pairs()) for piece in far]
 
-    partial, wave, info, left, right = pl.pallas_call(
+    partial, wave, info, right_b = pl.pallas_call(
         wave_kernel,
         out_shape=(
-            shape((4, BD, BD)), shape((16, BD, BD)), shape((16, 8, BD), F32),
-            pltpu.VMEM(left_env.shape, BF), pltpu.VMEM(right_env.shape, BF),
+            shape((4, BD, BD)), shape((16, BD, BD)), shape((16, 8, BD), F32), pltpu.VMEM(half, BF),
         ),
-        in_specs=[HBM] + [VMEM] * 10 + [HBM, HBM],
-        out_specs=(VMEM,) * 5,
+        in_specs=[HBM] + [VMEM] * 12 + [HBM, VMEM],
+        out_specs=(VMEM,) * 4,
         scratch_shapes=[
             pltpu.SMEM((4, 16), jnp.int32),
             pltpu.VMEM((4, BD, BD), F32),
             pltpu.SemaphoreType.DMA,
-            pltpu.SemaphoreType.DMA((2, len(CHUNKS))),
+            pltpu.SemaphoreType.DMA,
         ],
-        compiler_params=params(14),
+        compiler_params=params(8),
         name="wave_terms",
     )(
         pltpu.with_memory_space_constraint(src, pltpu.HBM), own, core, *far, *near,
-        pltpu.with_memory_space_constraint(left_env, pltpu.HBM),
-        pltpu.with_memory_space_constraint(right_env, pltpu.HBM),
+        left, right_a, right_in, token,
     )
 
     pieces = lax.all_to_all(partial.reshape(32, 32, BD), "op", 0, 0, tiled=True)
@@ -330,7 +331,7 @@
     applied_wave, corr, partial = pl.pallas_call(
         corr_kernel,
         out_shape=(shape((4, BD, BD), F32), shape((4, BD, BD)), shape((32, 4, 16, 128))),
-        in_specs=[SMEM] + [VMEM] * 6,
+        in_specs=[SMEM] + [VMEM] * 7,
         out_specs=(HBM, VMEM, VMEM),
         scratch_shapes=[
             pltpu.VMEM((16, BD, BD), BF),
@@ -343,7 +344,7 @@
         name="corr_terms",
     )(
         src, wave, info,
-        same.reshape(2, 4, BD, BD), other.reshape(2, 4, BD, BD), left, right,
+        same.reshape(2, 4, BD, BD), other.reshape(2, 4, BD, BD), left, right_a, right_b,
     )
 
     pieces = lax.all_to_all(partial.reshape(128, 16, 128), ALL, 0, 0, tiled=True)

time: 115 us -> 113 us (0.983)
  waiting for transfers between devices: 11.4 us -> 7.54 us
  Pallas kernels: 17.8 us -> 20 us
    pallas_call x0 -> x1, Pallas kernels: none -> 4.59 us  [shards(): pl.pallas_call(load_kernel, out_shape=(pltpu.VMEM(left_env.shape, BF), pl...]
    ppermute x1, waiting for transfers between devices: 4.25 us -> 0.01 us  [shards(): far = [lax.ppermute(first, ALL, cross_pairs())]]
    pallas_call x1, Pallas kernels: 7.63 us -> 5.59 us  [shards(): pl.pallas_call(wave_kernel, out_shape=(shape((4, BD, BD)), shape((16, BD,...]
  transfers between devices with their start and end apart: 10 -> 10, of which waited for: 7 -> 6; matrix products, arithmetic and copies ran while one was open for 0% -> 0% of each run, Pallas kernels for 0% -> 4%
where the time goes in v4:
time: 113 us; the launch traced here: 112 us
  blocking collectives  75.9 us (67%)
  Pallas kernels  20 us (18%)
  starting transfers between devices  7.95 us (7%)
  waiting for transfers between devices  7.54 us (7%)
    all_to_all x1, blocking collectives, shards(): lax.all_to_all(copies, ALL, 0, 0, tiled=True, axis_index_groups=core_grou...  24.4 us
    all_to_all x1, blocking collectives, shards(): pieces = lax.all_to_all(partial.reshape(32, 32, BD), 'op', 0, 0, tiled=True)  19.5 us
    all_to_all x1, blocking collectives, shards(): lax.all_to_all(partial.reshape(128, 16, 128), ALL, 0, 0, tiled=True)  16.7 us
    all_to_all x1, blocking collectives, shards(): gathered = lax.all_to_all(copies, 'op', 0, 0, tiled=True)  15.3 us
    pallas_call x1, Pallas kernels, shards(): pl.pallas_call(corr_kernel, out_shape=(shape((4, BD, BD), F32), shape((4,...  7.22 us
    pallas_call x1, Pallas kernels, shards(): pl.pallas_call(wave_kernel, out_shape=(shape((4, BD, BD)), shape((16, BD,...  5.59 us
    pallas_call x1, Pallas kernels, shards(): pl.pallas_call(load_kernel, out_shape=(pltpu.VMEM(left_env.shape, BF), pl...  4.59 us
    ppermute x1, starting transfers between devices, shards(): far = [lax.ppermute(first, ALL, cross_pairs())]  4.2 us
  transfers between devices with their start and end apart: 10, of which 6 were waited for; matrix products, arithmetic and copies ran while one was open for 0% of the time, Pallas kernels for 4%

profile of v4, /device:TPU:0, one launch (start us, length us, event | category | flops | bytes accessed | tf_op | source)
XLA Modules:
  0.0 112.3 jit_solution(12652492429490611179)
XLA Ops:
  0.6 1.3 %pack.1 = (bf16[4,272,256]{2,1,0:T(8,128)(2,1)S(1)}, bf16[272,256]{1,0:T(8,128)(2,1)S(1)}) custom-call(s32[2,4]{1,0:T(2,128)} %dims_in.1, f32[4]{0:T(128)} %energy_in.1, bf16[4,256,256]{2,1,0:T(8,128)(2,1)} %wave_in.1), custom_call_target="tpu_custom_call" | custom-call | tf_op jit(solution)/shard_map/pack/pallas_call | solution.py:263
  1.9 0.1 collective-permute-start
  2.0 4.2 %collective-permute-start.1 = (bf16[272,256]{1,0:T(8,128)(2,1)S(1)}, bf16[272,256]{1,0:T(8,128)(2,1)S(1)}, u32[]{:S(2)}, u32[]{:S(2)}) collective-permute-start(bf16[272,256]{1,0:T(8,128)(2,1)S(1)} %get-tuple-element.17), channel_id=1, source_target_pairs={{0,66},{1,67},{2,64},{3,65},{4,70},{5,71},{6,68},{7,69},{8,74},{9,... | collective-permute-start | bytes 417800 | tf_op jit(solution)/shard_map/ppermute | solution.py:277
  6.2 4.6 %load.1 = (bf16[16,4,256,256]{3,2,1,0:T(8,128)(2,1)S(1)}, bf16[8,4,256,256]{3,2,1,0:T(8,128)(2,1)S(1)}, f32[8,128]{1,0:T(8,128)S(1)}) custom-call(bf16[16,4,256,256]{3,2,1,0:T(8,128)(2,1)} %left.1, bf16[16,4,256,256]{3,2,1,0:T(8,128)(2,1)} %right_in.1), custom_call_target="tpu_custom_call" | custom-call | tf_op jit(solution)/shard_map/load/pallas_call | solution.py:282
  10.8 0.0 collective-permute-done.1.far0
  10.8 0.1 collective-permute-start.4
  10.9 1.7 %collective-permute-start.3 = (bf16[272,256]{1,0:T(8,128)(2,1)S(1)}, bf16[272,256]{1,0:T(8,128)(2,1)S(1)}, u32[]{:S(2)}, u32[]{:S(2)}) collective-permute-start(bf16[272,256]{1,0:T(8,128)(2,1)S(1)} %collective-permute-done.1.far0), channel_id=1, source_target_pairs={{0,16},{4,20},{8,24},{12,28},{16,0},{20,4},{24,8},{28,12},{32,48},... | collective-permute-start | bytes 417800 | tf_op jit(solution)/shard_map/ppermute | solution.py:294
  12.6 1.5 %collective-permute-start.2 = (bf16[272,256]{1,0:T(8,128)(2,1)S(1)}, bf16[272,256]{1,0:T(8,128)(2,1)S(1)}, u32[]{:S(2)}, u32[]{:S(2)}) collective-permute-start(bf16[272,256]{1,0:T(8,128)(2,1)S(1)} %collective-permute-done.1.far0), channel_id=1, source_target_pairs={{0,4},{4,0},{8,12},{12,8},{16,20},{20,16},{24,28},{28,24},{32,36},... | collective-permute-start | bytes 417800 | tf_op jit(solution)/shard_map/ppermute | solution.py:294
  14.1 0.0 collective-permute-start.5
  14.1 2.6 %collective-permute-done.4.far3 = bf16[272,256]{1,0:T(8,128)(2,1)S(1)} collective-permute-done((bf16[272,256]{1,0:T(8,128)(2,1)S(1)}, bf16[272,256]{1,0:T(8,128)(2,1)S(1)}, u32[]{:S(2)}, u32[]{:S(2)}) %collective-permute-start.4) | collective-permute-done | bytes 139296 | tf_op jit(solution)/shard_map/ppermute | solution.py:294
  16.6 0.0 collective-permute-start.8
  16.6 0.1 collective-permute-done.3.far2
  16.7 0.4 collective-permute-start.7
  17.1 0.9 collective-permute-done.2.far1
  18.0 0.0 collective-permute-start.6
  18.0 0.0 collective-permute-done.5.near0
  18.0 0.0 collective-permute-done.8.near3
  18.0 0.2 collective-permute-done.7.near2
  18.2 1.2 %collective-permute-done.6.near1 = bf16[272,256]{1,0:T(8,128)(2,1)S(1)} collective-permute-done((bf16[272,256]{1,0:T(8,128)(2,1)S(1)}, bf16[272,256]{1,0:T(8,128)(2,1)S(1)}, u32[]{:S(2)}, u32[]{:S(2)}) %collective-permute-start.6) | collective-permute-done | bytes 139296 | tf_op jit(solution)/shard_map/ppermute | solution.py:295
  19.4 0.0 collective-permute-done.core
  19.4 0.0 copy-start
  19.4 5.6 %wave_terms.1 = (bf16[4,256,256]{2,1,0:T(8,128)(2,1)S(1)}, bf16[16,256,256]{2,1,0:T(8,128)(2,1)S(1)}, f32[16,8,256]{2,1,0:T(8,128)S(1)}, bf16[8,4,256,256]{3,2,1,0:T(8,128)(2,1)S(1)}) custom-call(s32[4,16]{1,0:T(4,128)} %bitcast.11, bf16[4,272,256]{2,1,0:T(8,128)(2,1)S(1)} %get-tuple-element.16.own, bf16[4,272,256]{2,1,0:T(8,128)(2,1)S(1)} %collective-permute-done.core, ...), custom_call_target="tpu_custom_call" | custom-call | tf_op jit(solution)/shard_map/wave_terms/pallas_call | solution.py:297
  25.0 19.5 %all_to_all.20.parts = bf16[32,32,256]{2,1,0:T(8,128)(2,1)S(1)} all-to-all(bf16[32,32,256]{2,1,0:T(8,128)(2,1)S(1)} %bitcast.9), channel_id=1, replica_groups=mesh['op'=32,'blk'=4] {'op'}, dimensions={0} | all-to-all | bytes 1048576 | tf_op jit(solution)/shard_map/all_to_all | solution.py:317
  44.5 0.2 sum_wave.1
  44.7 24.4 %all_to_all.21 = bf16[64,32,256]{2,1,0:T(8,128)(2,1)S(1)} all-to-all(bf16[64,32,256]{2,1,0:T(8,128)(2,1)S(1)} %sum_wave.1), channel_id=1, replica_groups={{0,4,8,12,16,20,24,28,32,36,40,44,48,52,56,60,64,68,72,76,80,84,88,92,9..., dimensions={0} | all-to-all | bytes 2097152 | tf_op jit(solution)/shard_map/all_to_all | solution.py:326
  69.0 0.0 collective-permute-start.9
  69.0 2.7 %collective-permute-done.9 = bf16[64,32,256]{2,1,0:T(8,128)(2,1)S(1)} collective-permute-done((bf16[64,32,256]{2,1,0:T(8,128)(2,1)S(1)}, bf16[64,32,256]{2,1,0:T(8,128)(2,1)S(1)}, u32[]{:S(2)}, u32[]{:S(2)}) %collective-permute-start.9) | collective-permute-done | bytes 1048608 | tf_op jit(solution)/shard_map/ppermute | solution.py:329
  71.7 0.0 copy-done
  71.7 7.2 %corr_terms.1 = (f32[4,256,256]{2,1,0:T(8,128)}, bf16[4,256,256]{2,1,0:T(8,128)(2,1)S(1)}, bf16[32,4,16,128]{3,2,1,0:T(8,128)(2,1)S(1)}) custom-call(s32[4,16]{1,0:T(4,128)S(1)} %bitcast.12, bf16[16,256,256]{2,1,0:T(8,128)(2,1)S(1)} %get-tuple-element.23.wave, f32[16,8,256]{2,1,0:T(8,128)S(1)} %get-tuple-element.24.info, ...), custom_call_target="tpu_custom_call" | custom-call | tf_op jit(solution)/shard_map/corr_terms/pallas_call | solution.py:331
  78.9 16.7 %all_to_all.22 = bf16[128,16,128]{2,1,0:T(8,128)(2,1)S(1)} all-to-all(bf16[128,16,128]{2,1,0:T(8,128)(2,1)S(1)} %bitcast.10), channel_id=1, replica_groups=mesh['op'=32,'blk'=4] {'op','blk'}, dimensions={0} | all-to-all | bytes 1048576 | tf_op jit(solution)/shard_map/all_to_all | solution.py:350
  95.7 0.1 sum_corr.1
  95.8 15.3 %all_to_all.23.parts = bf16[32,4,16,128]{3,2,1,0:T(8,128)(2,1)S(1)} all-to-all(bf16[32,4,16,128]{3,2,1,0:T(8,128)(2,1)S(1)} %sum_corr.1), channel_id=1, replica_groups=mesh['op'=32,'blk'=4] {'op'}, dimensions={0} | all-to-all | bytes 1048576 | tf_op jit(solution)/shard_map/all_to_all | solution.py:359
  111.1 1.0 finish.1
Async XLA Ops:
  1.9 17.5 %collective-permute-start = (bf16[4,272,256]{2,1,0:T(8,128)(2,1)S(1)}, bf16[4,272,256]{2,1,0:T(8,128)(2,1)S(1)}, u32[]{:S(2)}, u32[]{:S(2)}) collective-permute-start(bf16[4,272,256]{2,1,0:T(8,128)(2,1)S(1)} %get-tuple-element.16.own), channel_id=1, source_target_pairs={{0,1},{1,0},{2,3},{3,2},{4,5},{5,4},{6,7},{7,6},{8,9},{9,8},{10,11... | collective-permute-start | bytes 1671176 | tf_op jit(solution)/shard_map/ppermute | solution.py:292
  2.0 8.8 %collective-permute-start.1 = (bf16[272,256]{1,0:T(8,128)(2,1)S(1)}, bf16[272,256]{1,0:T(8,128)(2,1)S(1)}, u32[]{:S(2)}, u32[]{:S(2)}) collective-permute-start(bf16[272,256]{1,0:T(8,128)(2,1)S(1)} %get-tuple-element.17), channel_id=1, source_target_pairs={{0,66},{1,67},{2,64},{3,65},{4,70},{5,71},{6,68},{7,69},{8,74},{9,... | collective-permute-start | bytes 417800 | tf_op jit(solution)/shard_map/ppermute | solution.py:277
  10.8 5.8 %collective-permute-start.4 = (bf16[272,256]{1,0:T(8,128)(2,1)S(1)}, bf16[272,256]{1,0:T(8,128)(2,1)S(1)}, u32[]{:S(2)}, u32[]{:S(2)}) collective-permute-start(bf16[272,256]{1,0:T(8,128)(2,1)S(1)} %collective-permute-done.1.far0), channel_id=1, source_target_pairs={{0,64},{4,68},{8,72},{12,76},{16,80},{20,84},{24,88},{28,92},{32,9... | collective-permute-start | bytes 417800 | tf_op jit(solution)/shard_map/ppermute | solution.py:294
  10.9 5.8 %collective-permute-start.3 = (bf16[272,256]{1,0:T(8,128)(2,1)S(1)}, bf16[272,256]{1,0:T(8,128)(2,1)S(1)}, u32[]{:S(2)}, u32[]{:S(2)}) collective-permute-start(bf16[272,256]{1,0:T(8,128)(2,1)S(1)} %collective-permute-done.1.far0), channel_id=1, source_target_pairs={{0,16},{4,20},{8,24},{12,28},{16,0},{20,4},{24,8},{28,12},{32,48},... | collective-permute-start | bytes 417800 | tf_op jit(solution)/shard_map/ppermute | solution.py:294
  12.6 5.4 %collective-permute-start.2 = (bf16[272,256]{1,0:T(8,128)(2,1)S(1)}, bf16[272,256]{1,0:T(8,128)(2,1)S(1)}, u32[]{:S(2)}, u32[]{:S(2)}) collective-permute-start(bf16[272,256]{1,0:T(8,128)(2,1)S(1)} %collective-permute-done.1.far0), channel_id=1, source_target_pairs={{0,4},{4,0},{8,12},{12,8},{16,20},{20,16},{24,28},{28,24},{32,36},... | collective-permute-start | bytes 417800 | tf_op jit(solution)/shard_map/ppermute | solution.py:294
  14.1 4.0 %collective-permute-start.5 = (bf16[272,256]{1,0:T(8,128)(2,1)S(1)}, bf16[272,256]{1,0:T(8,128)(2,1)S(1)}, u32[]{:S(2)}, u32[]{:S(2)}) collective-permute-start(bf16[272,256]{1,0:T(8,128)(2,1)S(1)} %collective-permute-done.1.far0), channel_id=1, source_target_pairs={{0,1},{1,0},{2,3},{3,2},{4,5},{5,4},{6,7},{7,6},{8,9},{9,8},{10,11... | collective-permute-start | bytes 417800 | tf_op jit(solution)/shard_map/ppermute | solution.py:295
  16.6 1.4 %collective-permute-start.8 = (bf16[272,256]{1,0:T(8,128)(2,1)S(1)}, bf16[272,256]{1,0:T(8,128)(2,1)S(1)}, u32[]{:S(2)}, u32[]{:S(2)}) collective-permute-start(bf16[272,256]{1,0:T(8,128)(2,1)S(1)} %collective-permute-done.4.far3), channel_id=1, source_target_pairs={{0,1},{1,0},{2,3},{3,2},{4,5},{5,4},{6,7},{7,6},{8,9},{9,8},{10,11... | collective-permute-start | bytes 417800 | tf_op jit(solution)/shard_map/ppermute | solution.py:295
  16.7 1.5 %collective-permute-start.7 = (bf16[272,256]{1,0:T(8,128)(2,1)S(1)}, bf16[272,256]{1,0:T(8,128)(2,1)S(1)}, u32[]{:S(2)}, u32[]{:S(2)}) collective-permute-start(bf16[272,256]{1,0:T(8,128)(2,1)S(1)} %collective-permute-done.3.far2), channel_id=1, source_target_pairs={{0,1},{1,0},{2,3},{3,2},{4,5},{5,4},{6,7},{7,6},{8,9},{9,8},{10,11... | collective-permute-start | bytes 417800 | tf_op jit(solution)/shard_map/ppermute | solution.py:295
  18.0 1.4 %collective-permute-start.6 = (bf16[272,256]{1,0:T(8,128)(2,1)S(1)}, bf16[272,256]{1,0:T(8,128)(2,1)S(1)}, u32[]{:S(2)}, u32[]{:S(2)}) collective-permute-start(bf16[272,256]{1,0:T(8,128)(2,1)S(1)} %collective-permute-done.2.far1), channel_id=1, source_target_pairs={{0,1},{1,0},{2,3},{3,2},{4,5},{5,4},{6,7},{7,6},{8,9},{9,8},{10,11... | collective-permute-start | bytes 417800 | tf_op jit(solution)/shard_map/ppermute | solution.py:295
  19.4 52.3 %copy-start = (s32[16,4]{0,1:T(4,128)S(1)}, s32[16,4]{0,1:T(4,128)}, u32[]{:S(2)}) copy-start(s32[16,4]{0,1:T(4,128)} %param.9) | copy-start | bytes 772
  69.0 2.7 %collective-permute-start.9 = (bf16[64,32,256]{2,1,0:T(8,128)(2,1)S(1)}, bf16[64,32,256]{2,1,0:T(8,128)(2,1)S(1)}, u32[]{:S(2)}, u32[]{:S(2)}) collective-permute-start(bf16[64,32,256]{2,1,0:T(8,128)(2,1)S(1)} %all_to_all.21), channel_id=1, source_target_pairs={{0,1},{1,0},{2,3},{3,2},{4,5},{5,4},{6,7},{7,6},{8,9},{9,8},{10,11... | collective-permute-start | bytes 3145736 | tf_op jit(solution)/shard_map/ppermute | solution.py:329

commit v5 on v4

--- a/solution.py
+++ b/solution.py
@@ -51,41 +51,52 @@
     return (row_ids < rows) & (col_ids < cols)
 
 
-def pack_kernel(dims_in, energy_in, wave_in, out, first, dims, energy, wave, sems):
+def pack(rows, cols, energy, wave):
+    row = lax.broadcasted_iota(jnp.int32, (INFO, BD), 0)
+    block = jnp.where(live(rows, cols, (BD, BD)), wave.astype(F32), 0.0)
+    value = jnp.full((INFO, BD), energy, F32)
+    high = value.astype(BF).astype(F32)
+    middle = (value - high).astype(BF).astype(F32)
+    low = value - high - middle
+    info = jnp.zeros((INFO, BD), F32)
+    for j, part in enumerate((rows.astype(F32), cols.astype(F32), high, middle, low)):
+        info = jnp.where(row == j, part, info)
+    return block.astype(BF), info.astype(BF)
+
+
+def first_kernel(dims_in, energy_in, wave_in, out, dims, energy, wave, sems):
+    b = color_of(lax.axis_index("op")) ^ 3
     copies = [
         pltpu.make_async_copy(dims_in, dims, sems.at[0]),
         pltpu.make_async_copy(energy_in, energy, sems.at[1]),
-        pltpu.make_async_copy(wave_in, wave, sems.at[2]),
+        pltpu.make_async_copy(wave_in.at[b], wave, sems.at[2]),
     ]
     for copy in copies:
         copy.start()
     for copy in copies:
         copy.wait()
-    row = lax.broadcasted_iota(jnp.int32, (INFO, BD), 0)
-    for b in range(4):
-        mask = live(dims[0, b], dims[1, b], (BD, BD))
-        out[b, :BD] = jnp.where(mask, wave[b].astype(F32), 0.0).astype(BF)
-        value = jnp.full((INFO, BD), energy[b], F32)
-        high = value.astype(BF).astype(F32)
-        middle = (value - high).astype(BF).astype(F32)
-        low = value - high - middle
-        info = jnp.zeros((INFO, BD), F32)
-        parts = (dims[0, b].astype(F32), dims[1, b].astype(F32), high, middle, low)
-        for j, part in enumerate(parts):
-            info = jnp.where(row == j, part, info)
-        out[b, BD:] = info.astype(BF)
-    first[...] = out[color_of(lax.axis_index("op")) ^ 3]
-
-
-def load_kernel(left, right, left_out, right_out, token, sems):
+    out[:BD], out[BD:] = pack(dims[0, b], dims[1, b], energy[b], wave[...])
+
+
+def load_kernel(
+    first, dims_in, energy_in, wave_in, left, right,
+    own, left_out, right_out, token, dims, energy, wave, sems,
+):
     copies = [
-        pltpu.make_async_copy(left, left_out, sems.at[0]),
-        pltpu.make_async_copy(right.at[pl.ds(0, HALF)], right_out, sems.at[1]),
+        pltpu.make_async_copy(dims_in, dims, sems.at[0]),
+        pltpu.make_async_copy(energy_in, energy, sems.at[1]),
+        pltpu.make_async_copy(wave_in, wave, sems.at[2]),
+        pltpu.make_async_copy(left, left_out, sems.at[3]),
+        pltpu.make_async_copy(right.at[pl.ds(0, HALF)], right_out, sems.at[4]),
     ]
     for copy in copies:
         copy.start()
     token[...] = jnp.zeros_like(token)
-    for copy in copies:
+    for copy in copies[:3]:
+        copy.wait()
+    for b in range(4):
+        own[b, :BD], own[b, BD:] = pack(dims[0, b], dims[1, b], energy[b], wave[b])
+    for copy in copies[3:]:
         copy.wait()
 
 
@@ -104,7 +115,7 @@
 
 def wave_kernel(
     src_in, own, core, far0, far1, far2, far3, near0, near1, near2, near3,
-    left, right_a, right_in, token, out, vec, info, right_b, src, acc, src_sem, sem,
+    left, right_a, right_in, token, out, vec, info, squares, right_b, src, acc, src_sem, sem,
 ):
     src_copy = pltpu.make_async_copy(src_in, src, src_sem)
     src_copy.start()
@@ -124,8 +135,17 @@
         info[block, 0:2] = entry[0:2]
         info[block, 2:3] = entry[2:3] + entry[3:4] + entry[4:5]
     src_copy.wait()
+    plain, weighted = jnp.zeros((8, BD), F32), jnp.zeros((8, BD), F32)
     for e in range(4):
         acc[e] = slot_terms(src, vec, left, right_a, e, 0)
+        for block in range(e * 4, e * 4 + 4):
+            part = jnp.zeros((8, BD), F32)
+            for r in range(0, BD, STRIP):
+                vector = vec[block, r:r + STRIP].astype(F32)
+                part += fold(vector * vector)
+            plain += part
+            weighted += info[block, 2:3] * part
+    squares[0], squares[1] = plain, weighted
     right_copy.wait()
     for e in range(4):
         out[e] = (acc[e] + slot_terms(src, vec, left, right_b, e, HALF)).astype(BF)
@@ -140,7 +160,7 @@
 
 
 def corr_kernel(
-    src, wave, info, same, other, left, right_a, right_b,
+    src, wave, info, squares, same, other, left, right_a, right_b,
     applied_out, corr_out, out, vec, acc, work, applied, applied_sem,
 ):
     entries = 16 * BD * BD
@@ -152,21 +172,15 @@
         b = me ^ turn
         return b, (same if turn % 2 == 0 else other).at[b >> 1, group]
 
-    def cross_sums(group, sums):
-        cross, square = sums
+    def cross_sums(group, cross):
         for turn in range(4):
             b, values = summed(group, turn)
-            block = group * 4 + b
-            part, own_part = zero, zero
             for rows in strips:
-                vector = wave[block, rows].astype(F32)
-                part += fold(values[rows].astype(F32) * vector)
-                own_part += fold(vector * vector)
-            cross += part + info[block, 2:3] * own_part
-            square += own_part
-        return cross, square
-
-    cross, square = lax.fori_loop(0, 4, cross_sums, (zero, zero))
+                cross += fold(values[rows].astype(F32) * wave[group * 4 + b, rows].astype(F32))
+        return cross
+
+    square = squares[0]
+    cross = lax.fori_loop(0, 4, cross_sums, squares[1])
     rayleigh = total_of(cross) / entries / (total_of(square) / entries + 1e-06)
 
     def subtract(group, resid):
@@ -260,47 +274,48 @@
 def shards(wave_blocks, left_env, right_env, source, block_dims, energy):
     src = source.T
 
-    own, first = pl.pallas_call(
-        pack_kernel,
-        out_shape=(shape((4, ROWS, BD)), shape((ROWS, BD))),
-        in_specs=[HBM, HBM, HBM],
-        out_specs=(VMEM, VMEM),
-        scratch_shapes=[
-            pltpu.SMEM((2, 4), jnp.int32),
-            pltpu.SMEM((4,), F32),
-            pltpu.VMEM((4, BD, BD), BF),
-            pltpu.SemaphoreType.DMA((3,)),
-        ],
-        compiler_params=params(8),
-        name="pack",
-    )(*(pltpu.with_memory_space_constraint(x, pltpu.HBM) for x in (block_dims, energy, wave_blocks)))
+    dims_in, energy_in, wave_in, left_in, right_in = (
+        pltpu.with_memory_space_constraint(x, pltpu.HBM)
+        for x in (block_dims, energy, wave_blocks, left_env, right_env)
+    )
+    half = (HALF,) + right_env.shape[1:]
+    small = [pltpu.SMEM((2, 4), jnp.int32), pltpu.SMEM((4,), F32)]
+    first = pl.pallas_call(
+        first_kernel,
+        out_shape=shape((ROWS, BD)),
+        in_specs=[HBM] * 3,
+        out_specs=VMEM,
+        scratch_shapes=small + [pltpu.VMEM((BD, BD), BF), pltpu.SemaphoreType.DMA((3,))],
+        compiler_params=params(2),
+        name="pack_first",
+    )(dims_in, energy_in, wave_in)
     far = [lax.ppermute(first, ALL, cross_pairs())]
-    left_in, right_in = (
-        pltpu.with_memory_space_constraint(x, pltpu.HBM) for x in (left_env, right_env)
-    )
-    half = (HALF,) + right_env.shape[1:]
-    left, right_a, token = pl.pallas_call(
+    own, left, right_a, token = pl.pallas_call(
         load_kernel,
-        out_shape=(pltpu.VMEM(left_env.shape, BF), pltpu.VMEM(half, BF), shape((8, 128), F32)),
-        in_specs=[HBM, HBM],
-        out_specs=(VMEM, VMEM, VMEM),
-        scratch_shapes=[pltpu.SemaphoreType.DMA((2,))],
-        compiler_params=params(1),
+        out_shape=(
+            shape((4, ROWS, BD)), pltpu.VMEM(left_env.shape, BF), pltpu.VMEM(half, BF),
+            shape((8, 128), F32),
+        ),
+        in_specs=[VMEM] + [HBM] * 5,
+        out_specs=(VMEM,) * 4,
+        scratch_shapes=small + [pltpu.VMEM((4, BD, BD), BF), pltpu.SemaphoreType.DMA((5,))],
+        compiler_params=params(4),
         name="load",
-    )(left_in, right_in)
-    far[0], token = lax.optimization_barrier((far[0], token))
+    )(first, dims_in, energy_in, wave_in, left_in, right_in)
+    far[0], own, token = lax.optimization_barrier((far[0], own, token))
     core = lax.ppermute(own, "blk", core_pairs())
     for bit in (1, 4, 16):
         far.append(lax.ppermute(far[0], "op", flip_pairs(bit)))
     near = [lax.ppermute(piece, "blk", core_pairs()) for piece in far]
 
-    partial, wave, info, right_b = pl.pallas_call(
+    partial, wave, info, squares, right_b = pl.pallas_call(
         wave_kernel,
         out_shape=(
-            shape((4, BD, BD)), shape((16, BD, BD)), shape((16, 8, BD), F32), pltpu.VMEM(half, BF),
+            shape((4, BD, BD)), shape((16, BD, BD)), shape((16, 8, BD), F32),
+            shape((2, 8, BD), F32), pltpu.VMEM(half, BF),
         ),
         in_specs=[HBM] + [VMEM] * 12 + [HBM, VMEM],
-        out_specs=(VMEM,) * 4,
+        out_specs=(VMEM,) * 5,
         scratch_shapes=[
             pltpu.SMEM((4, 16), jnp.int32),
             pltpu.VMEM((4, BD, BD), F32),
@@ -331,7 +346,7 @@
     applied_wave, corr, partial = pl.pallas_call(
         corr_kernel,
         out_shape=(shape((4, BD, BD), F32), shape((4, BD, BD)), shape((32, 4, 16, 128))),
-        in_specs=[SMEM] + [VMEM] * 7,
+        in_specs=[SMEM] + [VMEM] * 8,
         out_specs=(HBM, VMEM, VMEM),
         scratch_shapes=[
             pltpu.VMEM((16, BD, BD), BF),
@@ -343,7 +358,7 @@
         compiler_params=params(14),
         name="corr_terms",
     )(
-        src, wave, info,
+        src, wave, info, squares,
         same.reshape(2, 4, BD, BD), other.reshape(2, 4, BD, BD), left, right_a, right_b,
     )
 

time: 113 us -> 112 us (level)
  no operation moved by 1% of the time
where the time goes in v5:
time: 112 us
  blocking collectives  75.3 us (67%)
  Pallas kernels  19.7 us (18%)
  starting transfers between devices  8.04 us (7%)
  waiting for transfers between devices  7.64 us (7%)
    all_to_all x1, blocking collectives, shards(): lax.all_to_all(copies, ALL, 0, 0, tiled=True, axis_index_groups=core_grou...  23.6 us
    all_to_all x1, blocking collectives, shards(): pieces = lax.all_to_all(partial.reshape(32, 32, BD), 'op', 0, 0, tiled=True)  19.6 us
    all_to_all x1, blocking collectives, shards(): lax.all_to_all(partial.reshape(128, 16, 128), ALL, 0, 0, tiled=True)  16.7 us
    all_to_all x1, blocking collectives, shards(): gathered = lax.all_to_all(copies, 'op', 0, 0, tiled=True)  15.3 us
    pallas_call x1, Pallas kernels, shards(): pl.pallas_call(corr_kernel, out_shape=(shape((4, BD, BD), F32), shape((4,...  6.94 us
    pallas_call x1, Pallas kernels, shards(): pl.pallas_call(wave_kernel, out_shape=(shape((4, BD, BD)), shape((16, BD,...  5.62 us
    pallas_call x1, Pallas kernels, shards(): pl.pallas_call(load_kernel, out_shape=(shape((4, ROWS, BD)), pltpu.VMEM(l...  4.8 us
    ppermute x1, starting transfers between devices, shards(): far = [lax.ppermute(first, ALL, cross_pairs())]  4.2 us
  transfers between devices with their start and end apart: 10, of which 6 were waited for; matrix products, arithmetic and copies ran while one was open for 0% of the time, Pallas kernels for 4%

profile of v5, /device:TPU:0, one launch (start us, length us, event | category | flops | bytes accessed | tf_op | source)
XLA Modules:
  0.0 111.5 jit_solution(9190075757556472621)
XLA Ops:
  0.6 1.0 pack_first.1.first
  1.6 4.2 %collective-permute-start = (bf16[272,256]{1,0:T(8,128)(2,1)S(1)}, bf16[272,256]{1,0:T(8,128)(2,1)S(1)}, u32[]{:S(2)}, u32[]{:S(2)}) collective-permute-start(bf16[272,256]{1,0:T(8,128)(2,1)S(1)} %pack_first.1.first), channel_id=1, source_target_pairs={{0,66},{1,67},{2,64},{3,65},{4,70},{5,71},{6,68},{7,69},{8,74},{9,... | collective-permute-start | bytes 417800 | tf_op jit(solution)/shard_map/ppermute | solution.py:292
  5.8 4.8 %load.1 = (bf16[4,272,256]{2,1,0:T(8,128)(2,1)S(1)}, bf16[16,4,256,256]{3,2,1,0:T(8,128)(2,1)S(1)}, bf16[8,4,256,256]{3,2,1,0:T(8,128)(2,1)S(1)}, f32[8,128]{1,0:T(8,128)S(1)}) custom-call(bf16[272,256]{1,0:T(8,128)(2,1)S(1)} %pack_first.1.first, s32[2,4]{1,0:T(2,128)} %dims_in.3, f32[4]{0:T(128)} %energy_in.3, bf16[4,256,256]{2,1,0:T(8,128)(2,1)} %wave_in.3, ...), custom_call_target="tpu_custom_call" | custom-call | tf_op jit(solution)/shard_map/load/pallas_call | solution.py:293
  10.6 0.0 collective-permute-done.far0
  10.7 0.1 collective-permute-start.1
  10.7 0.1 collective-permute-start.4
  10.8 1.7 %collective-permute-start.3 = (bf16[272,256]{1,0:T(8,128)(2,1)S(1)}, bf16[272,256]{1,0:T(8,128)(2,1)S(1)}, u32[]{:S(2)}, u32[]{:S(2)}) collective-permute-start(bf16[272,256]{1,0:T(8,128)(2,1)S(1)} %collective-permute-done.far0), channel_id=1, source_target_pairs={{0,16},{4,20},{8,24},{12,28},{16,0},{20,4},{24,8},{28,12},{32,48},... | collective-permute-start | bytes 417800 | tf_op jit(solution)/shard_map/ppermute | solution.py:308
  12.5 1.5 %collective-permute-start.2 = (bf16[272,256]{1,0:T(8,128)(2,1)S(1)}, bf16[272,256]{1,0:T(8,128)(2,1)S(1)}, u32[]{:S(2)}, u32[]{:S(2)}) collective-permute-start(bf16[272,256]{1,0:T(8,128)(2,1)S(1)} %collective-permute-done.far0), channel_id=1, source_target_pairs={{0,4},{4,0},{8,12},{12,8},{16,20},{20,16},{24,28},{28,24},{32,36},... | collective-permute-start | bytes 417800 | tf_op jit(solution)/shard_map/ppermute | solution.py:308
  14.0 0.0 collective-permute-start.5
  14.0 2.8 %collective-permute-done.4.far3 = bf16[272,256]{1,0:T(8,128)(2,1)S(1)} collective-permute-done((bf16[272,256]{1,0:T(8,128)(2,1)S(1)}, bf16[272,256]{1,0:T(8,128)(2,1)S(1)}, u32[]{:S(2)}, u32[]{:S(2)}) %collective-permute-start.4) | collective-permute-done | bytes 139296 | tf_op jit(solution)/shard_map/ppermute | solution.py:308
  16.8 0.0 collective-permute-start.8
  16.8 0.0 collective-permute-done.3.far2
  16.8 0.5 collective-permute-start.7
  17.4 0.8 collective-permute-done.2.far1
  18.1 0.0 collective-permute-start.6
  18.1 0.0 collective-permute-done.5.near0
  18.1 0.1 collective-permute-done.8.near3
  18.2 0.2 collective-permute-done.7.near2
  18.4 1.1 collective-permute-done.6.near1
  19.5 0.0 collective-permute-done.1.core
  19.5 0.0 copy-start
  19.5 5.6 %wave_terms.1 = (bf16[4,256,256]{2,1,0:T(8,128)(2,1)S(1)}, bf16[16,256,256]{2,1,0:T(8,128)(2,1)S(1)}, f32[16,8,256]{2,1,0:T(8,128)S(1)}, f32[2,8,256]{2,1,0:T(8,128)S(1)}, bf16[8,4,256,256]{3,2,1,0:T(8,128)(2,1)S(1)}) custom-call(s32[4,16]{1,0:T(4,128)} %bitcast.11, bf16[4,272,256]{2,1,0:T(8,128)(2,1)S(1)} %get-tuple-element.19.own, ...), custom_call_target="tpu_custom_call" | custom-call | tf_op jit(solution)/shard_map/wave_terms/pallas_call | solution.py:311
  25.1 19.6 %all_to_all.20.parts = bf16[32,32,256]{2,1,0:T(8,128)(2,1)S(1)} all-to-all(bf16[32,32,256]{2,1,0:T(8,128)(2,1)S(1)} %bitcast.9), channel_id=1, replica_groups=mesh['op'=32,'blk'=4] {'op'}, dimensions={0} | all-to-all | bytes 1048576 | tf_op jit(solution)/shard_map/all_to_all | solution.py:332
  44.7 0.2 sum_wave.1
  44.9 23.6 %all_to_all.21 = bf16[64,32,256]{2,1,0:T(8,128)(2,1)S(1)} all-to-all(bf16[64,32,256]{2,1,0:T(8,128)(2,1)S(1)} %sum_wave.1), channel_id=1, replica_groups={{0,4,8,12,16,20,24,28,32,36,40,44,48,52,56,60,64,68,72,76,80,84,88,92,9..., dimensions={0} | all-to-all | bytes 2097152 | tf_op jit(solution)/shard_map/all_to_all | solution.py:341
  68.6 0.0 collective-permute-start.9
  68.6 2.7 %collective-permute-done.9 = bf16[64,32,256]{2,1,0:T(8,128)(2,1)S(1)} collective-permute-done((bf16[64,32,256]{2,1,0:T(8,128)(2,1)S(1)}, bf16[64,32,256]{2,1,0:T(8,128)(2,1)S(1)}, u32[]{:S(2)}, u32[]{:S(2)}) %collective-permute-start.9) | collective-permute-done | bytes 1048608 | tf_op jit(solution)/shard_map/ppermute | solution.py:344
  71.2 0.0 copy-done
  71.2 6.9 %corr_terms.1 = (f32[4,256,256]{2,1,0:T(8,128)}, bf16[4,256,256]{2,1,0:T(8,128)(2,1)S(1)}, bf16[32,4,16,128]{3,2,1,0:T(8,128)(2,1)S(1)}) custom-call(s32[4,16]{1,0:T(4,128)S(1)} %bitcast.12, bf16[16,256,256]{2,1,0:T(8,128)(2,1)S(1)} %get-tuple-element.24.wave, f32[16,8,256]{2,1,0:T(8,128)S(1)} %get-tuple-element.25.info, ...), custom_call_target="tpu_custom_call" | custom-call | tf_op jit(solution)/shard_map/corr_terms/pallas_call | solution.py:346
  78.2 16.7 %all_to_all.22 = bf16[128,16,128]{2,1,0:T(8,128)(2,1)S(1)} all-to-all(bf16[128,16,128]{2,1,0:T(8,128)(2,1)S(1)} %bitcast.10), channel_id=1, replica_groups=mesh['op'=32,'blk'=4] {'op','blk'}, dimensions={0} | all-to-all | bytes 1048576 | tf_op jit(solution)/shard_map/all_to_all | solution.py:365
  94.9 0.1 sum_corr.1
  95.0 15.3 %all_to_all.23.parts = bf16[32,4,16,128]{3,2,1,0:T(8,128)(2,1)S(1)} all-to-all(bf16[32,4,16,128]{3,2,1,0:T(8,128)(2,1)S(1)} %sum_corr.1), channel_id=1, replica_groups=mesh['op'=32,'blk'=4] {'op'}, dimensions={0} | all-to-all | bytes 1048576 | tf_op jit(solution)/shard_map/all_to_all | solution.py:374
  110.3 1.0 finish.1
Async XLA Ops:
  1.6 9.0 %collective-permute-start = (bf16[272,256]{1,0:T(8,128)(2,1)S(1)}, bf16[272,256]{1,0:T(8,128)(2,1)S(1)}, u32[]{:S(2)}, u32[]{:S(2)}) collective-permute-start(bf16[272,256]{1,0:T(8,128)(2,1)S(1)} %pack_first.1.first), channel_id=1, source_target_pairs={{0,66},{1,67},{2,64},{3,65},{4,70},{5,71},{6,68},{7,69},{8,74},{9,... | collective-permute-start | bytes 417800 | tf_op jit(solution)/shard_map/ppermute | solution.py:292
  10.7 8.8 %collective-permute-start.1 = (bf16[4,272,256]{2,1,0:T(8,128)(2,1)S(1)}, bf16[4,272,256]{2,1,0:T(8,128)(2,1)S(1)}, u32[]{:S(2)}, u32[]{:S(2)}) collective-permute-start(bf16[4,272,256]{2,1,0:T(8,128)(2,1)S(1)} %get-tuple-element.19.own), channel_id=1, source_target_pairs={{0,1},{1,0},{2,3},{3,2},{4,5},{5,4},{6,7},{7,6},{8,9},{9,8},{10,11... | collective-permute-start | bytes 1671176 | tf_op jit(solution)/shard_map/ppermute | solution.py:306
  10.7 6.1 %collective-permute-start.4 = (bf16[272,256]{1,0:T(8,128)(2,1)S(1)}, bf16[272,256]{1,0:T(8,128)(2,1)S(1)}, u32[]{:S(2)}, u32[]{:S(2)}) collective-permute-start(bf16[272,256]{1,0:T(8,128)(2,1)S(1)} %collective-permute-done.far0), channel_id=1, source_target_pairs={{0,64},{4,68},{8,72},{12,76},{16,80},{20,84},{24,88},{28,92},{32,9... | collective-permute-start | bytes 417800 | tf_op jit(solution)/shard_map/ppermute | solution.py:308
  10.8 6.0 %collective-permute-start.3 = (bf16[272,256]{1,0:T(8,128)(2,1)S(1)}, bf16[272,256]{1,0:T(8,128)(2,1)S(1)}, u32[]{:S(2)}, u32[]{:S(2)}) collective-permute-start(bf16[272,256]{1,0:T(8,128)(2,1)S(1)} %collective-permute-done.far0), channel_id=1, source_target_pairs={{0,16},{4,20},{8,24},{12,28},{16,0},{20,4},{24,8},{28,12},{32,48},... | collective-permute-start | bytes 417800 | tf_op jit(solution)/shard_map/ppermute | solution.py:308
  12.5 5.6 %collective-permute-start.2 = (bf16[272,256]{1,0:T(8,128)(2,1)S(1)}, bf16[272,256]{1,0:T(8,128)(2,1)S(1)}, u32[]{:S(2)}, u32[]{:S(2)}) collective-permute-start(bf16[272,256]{1,0:T(8,128)(2,1)S(1)} %collective-permute-done.far0), channel_id=1, source_target_pairs={{0,4},{4,0},{8,12},{12,8},{16,20},{20,16},{24,28},{28,24},{32,36},... | collective-permute-start | bytes 417800 | tf_op jit(solution)/shard_map/ppermute | solution.py:308
  14.0 4.1 %collective-permute-start.5 = (bf16[272,256]{1,0:T(8,128)(2,1)S(1)}, bf16[272,256]{1,0:T(8,128)(2,1)S(1)}, u32[]{:S(2)}, u32[]{:S(2)}) collective-permute-start(bf16[272,256]{1,0:T(8,128)(2,1)S(1)} %collective-permute-done.far0), channel_id=1, source_target_pairs={{0,1},{1,0},{2,3},{3,2},{4,5},{5,4},{6,7},{7,6},{8,9},{9,8},{10,11... | collective-permute-start | bytes 417800 | tf_op jit(solution)/shard_map/ppermute | solution.py:309
  16.8 1.4 %collective-permute-start.8 = (bf16[272,256]{1,0:T(8,128)(2,1)S(1)}, bf16[272,256]{1,0:T(8,128)(2,1)S(1)}, u32[]{:S(2)}, u32[]{:S(2)}) collective-permute-start(bf16[272,256]{1,0:T(8,128)(2,1)S(1)} %collective-permute-done.4.far3), channel_id=1, source_target_pairs={{0,1},{1,0},{2,3},{3,2},{4,5},{5,4},{6,7},{7,6},{8,9},{9,8},{10,11... | collective-permute-start | bytes 417800 | tf_op jit(solution)/shard_map/ppermute | solution.py:309
  16.8 1.6 %collective-permute-start.7 = (bf16[272,256]{1,0:T(8,128)(2,1)S(1)}, bf16[272,256]{1,0:T(8,128)(2,1)S(1)}, u32[]{:S(2)}, u32[]{:S(2)}) collective-permute-start(bf16[272,256]{1,0:T(8,128)(2,1)S(1)} %collective-permute-done.3.far2), channel_id=1, source_target_pairs={{0,1},{1,0},{2,3},{3,2},{4,5},{5,4},{6,7},{7,6},{8,9},{9,8},{10,11... | collective-permute-start | bytes 417800 | tf_op jit(solution)/shard_map/ppermute | solution.py:309
  18.1 1.4 %collective-permute-start.6 = (bf16[272,256]{1,0:T(8,128)(2,1)S(1)}, bf16[272,256]{1,0:T(8,128)(2,1)S(1)}, u32[]{:S(2)}, u32[]{:S(2)}) collective-permute-start(bf16[272,256]{1,0:T(8,128)(2,1)S(1)} %collective-permute-done.2.far1), channel_id=1, source_target_pairs={{0,1},{1,0},{2,3},{3,2},{4,5},{5,4},{6,7},{7,6},{8,9},{9,8},{10,11... | collective-permute-start | bytes 417800 | tf_op jit(solution)/shard_map/ppermute | solution.py:309
  19.5 51.7 %copy-start = (s32[16,4]{0,1:T(4,128)S(1)}, s32[16,4]{0,1:T(4,128)}, u32[]{:S(2)}) copy-start(s32[16,4]{0,1:T(4,128)} %param.9) | copy-start | bytes 772
  68.6 2.7 %collective-permute-start.9 = (bf16[64,32,256]{2,1,0:T(8,128)(2,1)S(1)}, bf16[64,32,256]{2,1,0:T(8,128)(2,1)S(1)}, u32[]{:S(2)}, u32[]{:S(2)}) collective-permute-start(bf16[64,32,256]{2,1,0:T(8,128)(2,1)S(1)} %all_to_all.21), channel_id=1, source_target_pairs={{0,1},{1,0},{2,3},{3,2},{4,5},{5,4},{6,7},{7,6},{8,9},{9,8},{10,11... | collective-permute-start | bytes 3145736 | tf_op jit(solution)/shard_map/ppermute | solution.py:344

commit v6 on v5

--- a/solution.py
+++ b/solution.py
@@ -13,6 +13,9 @@
 HALF = 8
 STRIP = 32
 MIB = 1 << 20
+UNIT = 2.0 ** 20
+SLOPE = 5.8
+LN2 = 0.6931471805599453
 ALL = ("op", "blk")
 
 SMEM = pl.BlockSpec(memory_space=pltpu.SMEM)
@@ -148,7 +151,21 @@
     squares[0], squares[1] = plain, weighted
     right_copy.wait()
     for e in range(4):
-        out[e] = (acc[e] + slot_terms(src, vec, left, right_b, e, HALF)).astype(BF)
+        out[e] = encode(acc[e] + slot_terms(src, vec, left, right_b, e, HALF))
+
+
+def encode(x):
+    level = jnp.log(1.0 + jnp.abs(x) * UNIT) * (SLOPE / LN2)
+    size = jnp.exp2(level - 120.0)
+    return jnp.where(x < 0.0, -size, size).astype(BF)
+
+
+def decode(code):
+    code = code.astype(F32)
+    size = jnp.abs(code)
+    level = (jnp.log(size) * (1.0 / LN2) + 120.0) * (1.0 / SLOPE)
+    value = jnp.where(size > 2.0 ** -120, (jnp.exp2(level) - 1.0) * (1.0 / UNIT), 0.0)
+    return jnp.where(code < 0.0, -value, value)
 
 
 def total_of(x):
@@ -176,7 +193,9 @@
         for turn in range(4):
             b, values = summed(group, turn)
             for rows in strips:
-                cross += fold(values[rows].astype(F32) * wave[group * 4 + b, rows].astype(F32))
+                value = decode(values[rows])
+                work[group * 4 + b, rows] = value
+                cross += fold(value * wave[group * 4 + b, rows].astype(F32))
         return cross
 
     square = squares[0]
@@ -184,24 +203,20 @@
     rayleigh = total_of(cross) / entries / (total_of(square) / entries + 1e-06)
 
     def subtract(group, resid):
-        for turn in range(4):
-            b, values = summed(group, turn)
+        for b in range(4):
             block = group * 4 + b
             level = info[block, 2:3] - rayleigh
             for rows in strips:
-                rest = values[rows].astype(F32) + level * wave[block, rows].astype(F32)
+                rest = work[block, rows] + level * wave[block, rows].astype(F32)
                 work[block, rows] = rest
                 resid += fold(rest * rest)
         return resid
 
     resid = lax.fori_loop(0, 4, subtract, zero)
     scale = lax.rsqrt(total_of(resid) / entries + 1e-06)
-    for turn in range(4):
-        b, values = summed(me, turn)
-        level = info[me * 4 + b, 2:3]
+    for b in range(4):
         for rows in strips:
-            vector = wave[me * 4 + b, rows].astype(F32)
-            applied[b, rows] = values[rows].astype(F32) + level * vector
+            applied[b, rows] = work[me * 4 + b, rows] + rayleigh * wave[me * 4 + b, rows].astype(F32)
 
     applied_copy = pltpu.make_async_copy(applied, applied_out, applied_sem)
     applied_copy.start()
@@ -230,8 +245,10 @@
     part = lax.axis_index("op")
     entry = info[(part >> 3) * 4 + lax.axis_index("blk")]
     mask = live(entry[0:1], entry[1:2], (STRIP, BD), (part & 7) * STRIP)
-    total = jnp.sum(parts[...].astype(F32), axis=0)
-    total = jnp.where(mask, total, 0.0).astype(BF)
+    total = jnp.zeros((STRIP, BD), F32)
+    for i in range(parts.shape[0]):
+        total += decode(parts[i])
+    total = encode(jnp.where(mask, total, 0.0))
     for i in range(out.shape[0]):
         out[i] = total
 

time: 112 us -> 115 us (1.027)
  Pallas kernels: 19.7 us -> 22.5 us
    pallas_call x1, Pallas kernels: 6.94 us -> 9.08 us  [shards(): pl.pallas_call(corr_kernel, out_shape=(shape((4, BD, BD), F32), shape((4,...]
where the time goes in v6:
time: 115 us; the launch traced here: 114 us
  blocking collectives  75.3 us (65%)
  Pallas kernels  22.5 us (20%)
  starting transfers between devices  8.04 us (7%)
  waiting for transfers between devices  7.64 us (7%)
    all_to_all x1, blocking collectives, shards(): lax.all_to_all(copies, ALL, 0, 0, tiled=True, axis_index_groups=core_grou...  23.6 us
    all_to_all x1, blocking collectives, shards(): pieces = lax.all_to_all(partial.reshape(32, 32, BD), 'op', 0, 0, tiled=True)  19.6 us
    all_to_all x1, blocking collectives, shards(): lax.all_to_all(partial.reshape(128, 16, 128), ALL, 0, 0, tiled=True)  16.7 us
    all_to_all x1, blocking collectives, shards(): gathered = lax.all_to_all(copies, 'op', 0, 0, tiled=True)  15.3 us
    pallas_call x1, Pallas kernels, shards(): pl.pallas_call(corr_kernel, out_shape=(shape((4, BD, BD), F32), shape((4,...  9.08 us
    pallas_call x1, Pallas kernels, shards(): pl.pallas_call(wave_kernel, out_shape=(shape((4, BD, BD)), shape((16, BD,...  5.79 us
    pallas_call x1, Pallas kernels, shards(): pl.pallas_call(load_kernel, out_shape=(shape((4, ROWS, BD)), pltpu.VMEM(l...  4.8 us
    ppermute x1, starting transfers between devices, shards(): far = [lax.ppermute(first, ALL, cross_pairs())]  4.2 us
  transfers between devices with their start and end apart: 10, of which 6 were waited for; matrix products, arithmetic and copies ran while one was open for 0% of the time, Pallas kernels for 4%

profile of v6, /device:TPU:0, one launch (start us, length us, event | category | flops | bytes accessed | tf_op | source)
XLA Modules:
  0.0 114.4 jit_solution(10327245210031026318)
XLA Ops:
  0.6 1.0 pack_first.1.first
  1.6 4.2 %collective-permute-start = (bf16[272,256]{1,0:T(8,128)(2,1)S(1)}, bf16[272,256]{1,0:T(8,128)(2,1)S(1)}, u32[]{:S(2)}, u32[]{:S(2)}) collective-permute-start(bf16[272,256]{1,0:T(8,128)(2,1)S(1)} %pack_first.1.first), channel_id=1, source_target_pairs={{0,66},{1,67},{2,64},{3,65},{4,70},{5,71},{6,68},{7,69},{8,74},{9,... | collective-permute-start | bytes 417800 | tf_op jit(solution)/shard_map/ppermute | solution.py:309
  5.8 4.8 %load.1 = (bf16[4,272,256]{2,1,0:T(8,128)(2,1)S(1)}, bf16[16,4,256,256]{3,2,1,0:T(8,128)(2,1)S(1)}, bf16[8,4,256,256]{3,2,1,0:T(8,128)(2,1)S(1)}, f32[8,128]{1,0:T(8,128)S(1)}) custom-call(bf16[272,256]{1,0:T(8,128)(2,1)S(1)} %pack_first.1.first, s32[2,4]{1,0:T(2,128)} %dims_in.3, f32[4]{0:T(128)} %energy_in.3, bf16[4,256,256]{2,1,0:T(8,128)(2,1)} %wave_in.3, ...), custom_call_target="tpu_custom_call" | custom-call | tf_op jit(solution)/shard_map/load/pallas_call | solution.py:310
  10.6 0.0 collective-permute-done.far0
  10.7 0.1 collective-permute-start.1
  10.7 0.1 collective-permute-start.4
  10.8 1.7 %collective-permute-start.3 = (bf16[272,256]{1,0:T(8,128)(2,1)S(1)}, bf16[272,256]{1,0:T(8,128)(2,1)S(1)}, u32[]{:S(2)}, u32[]{:S(2)}) collective-permute-start(bf16[272,256]{1,0:T(8,128)(2,1)S(1)} %collective-permute-done.far0), channel_id=1, source_target_pairs={{0,16},{4,20},{8,24},{12,28},{16,0},{20,4},{24,8},{28,12},{32,48},... | collective-permute-start | bytes 417800 | tf_op jit(solution)/shard_map/ppermute | solution.py:325
  12.5 1.5 %collective-permute-start.2 = (bf16[272,256]{1,0:T(8,128)(2,1)S(1)}, bf16[272,256]{1,0:T(8,128)(2,1)S(1)}, u32[]{:S(2)}, u32[]{:S(2)}) collective-permute-start(bf16[272,256]{1,0:T(8,128)(2,1)S(1)} %collective-permute-done.far0), channel_id=1, source_target_pairs={{0,4},{4,0},{8,12},{12,8},{16,20},{20,16},{24,28},{28,24},{32,36},... | collective-permute-start | bytes 417800 | tf_op jit(solution)/shard_map/ppermute | solution.py:325
  14.0 0.0 collective-permute-start.5
  14.0 2.8 %collective-permute-done.4.far3 = bf16[272,256]{1,0:T(8,128)(2,1)S(1)} collective-permute-done((bf16[272,256]{1,0:T(8,128)(2,1)S(1)}, bf16[272,256]{1,0:T(8,128)(2,1)S(1)}, u32[]{:S(2)}, u32[]{:S(2)}) %collective-permute-start.4) | collective-permute-done | bytes 139296 | tf_op jit(solution)/shard_map/ppermute | solution.py:325
  16.8 0.0 collective-permute-start.8
  16.8 0.0 collective-permute-done.3.far2
  16.8 0.5 collective-permute-start.7
  17.4 0.8 collective-permute-done.2.far1
  18.1 0.0 collective-permute-start.6
  18.1 0.0 collective-permute-done.5.near0
  18.1 0.1 collective-permute-done.8.near3
  18.2 0.2 collective-permute-done.7.near2
  18.4 1.1 collective-permute-done.6.near1
  19.5 0.0 collective-permute-done.1.core
  19.5 0.0 copy-start
  19.5 5.8 %wave_terms.1 = (bf16[4,256,256]{2,1,0:T(8,128)(2,1)S(1)}, bf16[16,256,256]{2,1,0:T(8,128)(2,1)S(1)}, f32[16,8,256]{2,1,0:T(8,128)S(1)}, f32[2,8,256]{2,1,0:T(8,128)S(1)}, bf16[8,4,256,256]{3,2,1,0:T(8,128)(2,1)S(1)}) custom-call(s32[4,16]{1,0:T(4,128)} %bitcast.11, bf16[4,272,256]{2,1,0:T(8,128)(2,1)S(1)} %get-tuple-element.19.own, ...), custom_call_target="tpu_custom_call" | custom-call | tf_op jit(solution)/shard_map/wave_terms/pallas_call | solution.py:328
  25.3 19.6 %all_to_all.20.parts = bf16[32,32,256]{2,1,0:T(8,128)(2,1)S(1)} all-to-all(bf16[32,32,256]{2,1,0:T(8,128)(2,1)S(1)} %bitcast.9), channel_id=1, replica_groups=mesh['op'=32,'blk'=4] {'op'}, dimensions={0} | all-to-all | bytes 1048576 | tf_op jit(solution)/shard_map/all_to_all | solution.py:349
  44.9 0.7 sum_wave.1
  45.6 23.6 %all_to_all.21 = bf16[64,32,256]{2,1,0:T(8,128)(2,1)S(1)} all-to-all(bf16[64,32,256]{2,1,0:T(8,128)(2,1)S(1)} %sum_wave.1), channel_id=1, replica_groups={{0,4,8,12,16,20,24,28,32,36,40,44,48,52,56,60,64,68,72,76,80,84,88,92,9..., dimensions={0} | all-to-all | bytes 2097152 | tf_op jit(solution)/shard_map/all_to_all | solution.py:358
  69.3 0.0 collective-permute-start.9
  69.3 2.7 %collective-permute-done.9 = bf16[64,32,256]{2,1,0:T(8,128)(2,1)S(1)} collective-permute-done((bf16[64,32,256]{2,1,0:T(8,128)(2,1)S(1)}, bf16[64,32,256]{2,1,0:T(8,128)(2,1)S(1)}, u32[]{:S(2)}, u32[]{:S(2)}) %collective-permute-start.9) | collective-permute-done | bytes 1048608 | tf_op jit(solution)/shard_map/ppermute | solution.py:361
  71.9 0.0 copy-done
  71.9 9.1 %corr_terms.1 = (f32[4,256,256]{2,1,0:T(8,128)}, bf16[4,256,256]{2,1,0:T(8,128)(2,1)S(1)}, bf16[32,4,16,128]{3,2,1,0:T(8,128)(2,1)S(1)}) custom-call(s32[4,16]{1,0:T(4,128)S(1)} %bitcast.12, bf16[16,256,256]{2,1,0:T(8,128)(2,1)S(1)} %get-tuple-element.24.wave, f32[16,8,256]{2,1,0:T(8,128)S(1)} %get-tuple-element.25.info, ...), custom_call_target="tpu_custom_call" | custom-call | tf_op jit(solution)/shard_map/corr_terms/pallas_call | solution.py:363
  81.0 16.7 %all_to_all.22 = bf16[128,16,128]{2,1,0:T(8,128)(2,1)S(1)} all-to-all(bf16[128,16,128]{2,1,0:T(8,128)(2,1)S(1)} %bitcast.10), channel_id=1, replica_groups=mesh['op'=32,'blk'=4] {'op','blk'}, dimensions={0} | all-to-all | bytes 1048576 | tf_op jit(solution)/shard_map/all_to_all | solution.py:382
  97.8 0.1 sum_corr.1
  97.9 15.3 %all_to_all.23.parts = bf16[32,4,16,128]{3,2,1,0:T(8,128)(2,1)S(1)} all-to-all(bf16[32,4,16,128]{3,2,1,0:T(8,128)(2,1)S(1)} %sum_corr.1), channel_id=1, replica_groups=mesh['op'=32,'blk'=4] {'op'}, dimensions={0} | all-to-all | bytes 1048576 | tf_op jit(solution)/shard_map/all_to_all | solution.py:391
  113.2 1.0 finish.1
Async XLA Ops:
  1.6 9.0 %collective-permute-start = (bf16[272,256]{1,0:T(8,128)(2,1)S(1)}, bf16[272,256]{1,0:T(8,128)(2,1)S(1)}, u32[]{:S(2)}, u32[]{:S(2)}) collective-permute-start(bf16[272,256]{1,0:T(8,128)(2,1)S(1)} %pack_first.1.first), channel_id=1, source_target_pairs={{0,66},{1,67},{2,64},{3,65},{4,70},{5,71},{6,68},{7,69},{8,74},{9,... | collective-permute-start | bytes 417800 | tf_op jit(solution)/shard_map/ppermute | solution.py:309
  10.7 8.8 %collective-permute-start.1 = (bf16[4,272,256]{2,1,0:T(8,128)(2,1)S(1)}, bf16[4,272,256]{2,1,0:T(8,128)(2,1)S(1)}, u32[]{:S(2)}, u32[]{:S(2)}) collective-permute-start(bf16[4,272,256]{2,1,0:T(8,128)(2,1)S(1)} %get-tuple-element.19.own), channel_id=1, source_target_pairs={{0,1},{1,0},{2,3},{3,2},{4,5},{5,4},{6,7},{7,6},{8,9},{9,8},{10,11... | collective-permute-start | bytes 1671176 | tf_op jit(solution)/shard_map/ppermute | solution.py:323
  10.7 6.1 %collective-permute-start.4 = (bf16[272,256]{1,0:T(8,128)(2,1)S(1)}, bf16[272,256]{1,0:T(8,128)(2,1)S(1)}, u32[]{:S(2)}, u32[]{:S(2)}) collective-permute-start(bf16[272,256]{1,0:T(8,128)(2,1)S(1)} %collective-permute-done.far0), channel_id=1, source_target_pairs={{0,64},{4,68},{8,72},{12,76},{16,80},{20,84},{24,88},{28,92},{32,9... | collective-permute-start | bytes 417800 | tf_op jit(solution)/shard_map/ppermute | solution.py:325
  10.8 6.0 %collective-permute-start.3 = (bf16[272,256]{1,0:T(8,128)(2,1)S(1)}, bf16[272,256]{1,0:T(8,128)(2,1)S(1)}, u32[]{:S(2)}, u32[]{:S(2)}) collective-permute-start(bf16[272,256]{1,0:T(8,128)(2,1)S(1)} %collective-permute-done.far0), channel_id=1, source_target_pairs={{0,16},{4,20},{8,24},{12,28},{16,0},{20,4},{24,8},{28,12},{32,48},... | collective-permute-start | bytes 417800 | tf_op jit(solution)/shard_map/ppermute | solution.py:325
  12.5 5.6 %collective-permute-start.2 = (bf16[272,256]{1,0:T(8,128)(2,1)S(1)}, bf16[272,256]{1,0:T(8,128)(2,1)S(1)}, u32[]{:S(2)}, u32[]{:S(2)}) collective-permute-start(bf16[272,256]{1,0:T(8,128)(2,1)S(1)} %collective-permute-done.far0), channel_id=1, source_target_pairs={{0,4},{4,0},{8,12},{12,8},{16,20},{20,16},{24,28},{28,24},{32,36},... | collective-permute-start | bytes 417800 | tf_op jit(solution)/shard_map/ppermute | solution.py:325
  14.0 4.1 %collective-permute-start.5 = (bf16[272,256]{1,0:T(8,128)(2,1)S(1)}, bf16[272,256]{1,0:T(8,128)(2,1)S(1)}, u32[]{:S(2)}, u32[]{:S(2)}) collective-permute-start(bf16[272,256]{1,0:T(8,128)(2,1)S(1)} %collective-permute-done.far0), channel_id=1, source_target_pairs={{0,1},{1,0},{2,3},{3,2},{4,5},{5,4},{6,7},{7,6},{8,9},{9,8},{10,11... | collective-permute-start | bytes 417800 | tf_op jit(solution)/shard_map/ppermute | solution.py:326
  16.8 1.4 %collective-permute-start.8 = (bf16[272,256]{1,0:T(8,128)(2,1)S(1)}, bf16[272,256]{1,0:T(8,128)(2,1)S(1)}, u32[]{:S(2)}, u32[]{:S(2)}) collective-permute-start(bf16[272,256]{1,0:T(8,128)(2,1)S(1)} %collective-permute-done.4.far3), channel_id=1, source_target_pairs={{0,1},{1,0},{2,3},{3,2},{4,5},{5,4},{6,7},{7,6},{8,9},{9,8},{10,11... | collective-permute-start | bytes 417800 | tf_op jit(solution)/shard_map/ppermute | solution.py:326
  16.8 1.6 %collective-permute-start.7 = (bf16[272,256]{1,0:T(8,128)(2,1)S(1)}, bf16[272,256]{1,0:T(8,128)(2,1)S(1)}, u32[]{:S(2)}, u32[]{:S(2)}) collective-permute-start(bf16[272,256]{1,0:T(8,128)(2,1)S(1)} %collective-permute-done.3.far2), channel_id=1, source_target_pairs={{0,1},{1,0},{2,3},{3,2},{4,5},{5,4},{6,7},{7,6},{8,9},{9,8},{10,11... | collective-permute-start | bytes 417800 | tf_op jit(solution)/shard_map/ppermute | solution.py:326
  18.1 1.4 %collective-permute-start.6 = (bf16[272,256]{1,0:T(8,128)(2,1)S(1)}, bf16[272,256]{1,0:T(8,128)(2,1)S(1)}, u32[]{:S(2)}, u32[]{:S(2)}) collective-permute-start(bf16[272,256]{1,0:T(8,128)(2,1)S(1)} %collective-permute-done.2.far1), channel_id=1, source_target_pairs={{0,1},{1,0},{2,3},{3,2},{4,5},{5,4},{6,7},{7,6},{8,9},{9,8},{10,11... | collective-permute-start | bytes 417800 | tf_op jit(solution)/shard_map/ppermute | solution.py:326
  19.5 52.4 %copy-start = (s32[16,4]{0,1:T(4,128)S(1)}, s32[16,4]{0,1:T(4,128)}, u32[]{:S(2)}) copy-start(s32[16,4]{0,1:T(4,128)} %param.9) | copy-start | bytes 772
  69.3 2.7 %collective-permute-start.9 = (bf16[64,32,256]{2,1,0:T(8,128)(2,1)S(1)}, bf16[64,32,256]{2,1,0:T(8,128)(2,1)S(1)}, u32[]{:S(2)}, u32[]{:S(2)}) collective-permute-start(bf16[64,32,256]{2,1,0:T(8,128)(2,1)S(1)} %all_to_all.21), channel_id=1, source_target_pairs={{0,1},{1,0},{2,3},{3,2},{4,5},{5,4},{6,7},{7,6},{8,9},{9,8},{10,11... | collective-permute-start | bytes 3145736 | tf_op jit(solution)/shard_map/ppermute | solution.py:361

commit v7 on v6

--- a/solution.py
+++ b/solution.py
@@ -176,30 +176,36 @@
     return jnp.sum(x.reshape(STRIP // 8, 8, BD), axis=0)
 
 
+def decode_sums(work, codes, wave, me, turns, start):
+    def add_group(group, cross):
+        for turn in turns:
+            b = me ^ turn
+            for r in range(0, BD, STRIP):
+                rows = pl.ds(r, STRIP)
+                value = decode(codes[b >> 1, group, rows])
+                work[group * 4 + b, rows] = value
+                cross += fold(value * wave[group * 4 + b, rows].astype(F32))
+        return cross
+
+    return lax.fori_loop(0, 4, add_group, start)
+
+
+def half_kernel(wave, squares, same, sums, work):
+    sums[0] = squares[0]
+    sums[1] = decode_sums(work, same, wave, lax.axis_index("blk"), (0, 2), squares[1])
+
+
 def corr_kernel(
-    src, wave, info, squares, same, other, left, right_a, right_b,
-    applied_out, corr_out, out, vec, acc, work, applied, applied_sem,
+    src, wave, info, sums, work_in, other, left, right_a, right_b,
+    applied_out, corr_out, out, work, vec, acc, applied, applied_sem,
 ):
     entries = 16 * BD * BD
     me = lax.axis_index("blk")
     zero = jnp.zeros((8, BD), F32)
     strips = [pl.ds(r, STRIP) for r in range(0, BD, STRIP)]
 
-    def summed(group, turn):
-        b = me ^ turn
-        return b, (same if turn % 2 == 0 else other).at[b >> 1, group]
-
-    def cross_sums(group, cross):
-        for turn in range(4):
-            b, values = summed(group, turn)
-            for rows in strips:
-                value = decode(values[rows])
-                work[group * 4 + b, rows] = value
-                cross += fold(value * wave[group * 4 + b, rows].astype(F32))
-        return cross
-
-    square = squares[0]
-    cross = lax.fori_loop(0, 4, cross_sums, squares[1])
+    square = sums[0]
+    cross = decode_sums(work, other, wave, me, (1, 3), sums[1])
     rayleigh = total_of(cross) / entries / (total_of(square) / entries + 1e-06)
 
     def subtract(group, resid):
@@ -359,24 +365,37 @@
         copies, ALL, 0, 0, tiled=True, axis_index_groups=core_groups()
     )
     other = lax.ppermute(same, "blk", core_pairs())
-
-    applied_wave, corr, partial = pl.pallas_call(
+    sums, work = pl.pallas_call(
+        half_kernel,
+        out_shape=(shape((2, 8, BD), F32), shape((16, BD, BD), F32)),
+        in_specs=[VMEM] * 3,
+        out_specs=(VMEM, VMEM),
+        compiler_params=params(2),
+        cost_estimate=pl.CostEstimate(
+            flops=16 * MIB, bytes_accessed=4 * MIB, transcendentals=MIB
+        ),
+        name="decode_half",
+    )(wave, squares, same.reshape(2, 4, BD, BD))
+
+    applied_wave, corr, partial, work = pl.pallas_call(
         corr_kernel,
-        out_shape=(shape((4, BD, BD), F32), shape((4, BD, BD)), shape((32, 4, 16, 128))),
+        out_shape=(
+            shape((4, BD, BD), F32), shape((4, BD, BD)), shape((32, 4, 16, 128)),
+            shape((16, BD, BD), F32),
+        ),
         in_specs=[SMEM] + [VMEM] * 8,
-        out_specs=(HBM, VMEM, VMEM),
+        out_specs=(HBM, VMEM, VMEM, VMEM),
+        input_output_aliases={4: 3},
         scratch_shapes=[
             pltpu.VMEM((16, BD, BD), BF),
             pltpu.VMEM((4, BD, BD), F32),
-            pltpu.VMEM((16, BD, BD), F32),
             pltpu.VMEM((4, BD, BD), F32),
             pltpu.SemaphoreType.DMA,
         ],
         compiler_params=params(14),
         name="corr_terms",
     )(
-        src, wave, info, squares,
-        same.reshape(2, 4, BD, BD), other.reshape(2, 4, BD, BD), left, right_a, right_b,
+        src, wave, info, sums, work, other.reshape(2, 4, BD, BD), left, right_a, right_b,
     )
 
     pieces = lax.all_to_all(partial.reshape(128, 16, 128), ALL, 0, 0, tiled=True)

time: 115 us -> 113 us (0.983)
  waiting for transfers between devices: 7.64 us -> 6.32 us
    pallas_call x1, Pallas kernels: 9.08 us -> 7.75 us  [shards(): pl.pallas_call(corr_kernel, out_shape=(shape((4, BD, BD), F32), shape((4,...]
    ppermute x1, waiting for transfers between devices: 2.66 us -> 1.34 us  [shards(): other = lax.ppermute(same, 'blk', core_pairs())]
    pallas_call x0 -> x1, Pallas kernels: none -> 1.31 us  [shards(): pl.pallas_call(half_kernel, out_shape=(shape((2, 8, BD), F32), shape((16,...]
  transfers between devices with their start and end apart: 10 -> 10, of which waited for: 6 -> 6; matrix products, arithmetic and copies ran while one was open for 0% -> 0% of each run, Pallas kernels for 4% -> 5%
where the time goes in v7:
time: 113 us
  blocking collectives  75.3 us (67%)
  Pallas kernels  22.5 us (20%)
  starting transfers between devices  8.04 us (7%)
  waiting for transfers between devices  6.32 us (6%)
    all_to_all x1, blocking collectives, shards(): lax.all_to_all(copies, ALL, 0, 0, tiled=True, axis_index_groups=core_grou...  23.6 us
    all_to_all x1, blocking collectives, shards(): pieces = lax.all_to_all(partial.reshape(32, 32, BD), 'op', 0, 0, tiled=True)  19.6 us
    all_to_all x1, blocking collectives, shards(): lax.all_to_all(partial.reshape(128, 16, 128), ALL, 0, 0, tiled=True)  16.7 us
    all_to_all x1, blocking collectives, shards(): gathered = lax.all_to_all(copies, 'op', 0, 0, tiled=True)  15.3 us
    pallas_call x1, Pallas kernels, shards(): pl.pallas_call(corr_kernel, out_shape=(shape((4, BD, BD), F32), shape((4,...  7.75 us
    pallas_call x1, Pallas kernels, shards(): pl.pallas_call(wave_kernel, out_shape=(shape((4, BD, BD)), shape((16, BD,...  5.75 us
    pallas_call x1, Pallas kernels, shards(): pl.pallas_call(load_kernel, out_shape=(shape((4, ROWS, BD)), pltpu.VMEM(l...  4.8 us
    ppermute x1, starting transfers between devices, shards(): far = [lax.ppermute(first, ALL, cross_pairs())]  4.2 us
  transfers between devices with their start and end apart: 10, of which 6 were waited for; matrix products, arithmetic and copies ran while one was open for 0% of the time, Pallas kernels for 5%

profile of v7, /device:TPU:0, one launch (start us, length us, event | category | flops | bytes accessed | tf_op | source)
XLA Modules:
  0.0 113.0 jit_solution(6319459456536554626)
XLA Ops:
  0.6 1.0 pack_first.1.first
  1.6 4.2 %collective-permute-start = (bf16[272,256]{1,0:T(8,128)(2,1)S(1)}, bf16[272,256]{1,0:T(8,128)(2,1)S(1)}, u32[]{:S(2)}, u32[]{:S(2)}) collective-permute-start(bf16[272,256]{1,0:T(8,128)(2,1)S(1)} %pack_first.1.first), channel_id=1, source_target_pairs={{0,66},{1,67},{2,64},{3,65},{4,70},{5,71},{6,68},{7,69},{8,74},{9,... | collective-permute-start | bytes 417800 | tf_op jit(solution)/shard_map/ppermute | solution.py:315
  5.8 4.8 %load.1 = (bf16[4,272,256]{2,1,0:T(8,128)(2,1)S(1)}, bf16[16,4,256,256]{3,2,1,0:T(8,128)(2,1)S(1)}, bf16[8,4,256,256]{3,2,1,0:T(8,128)(2,1)S(1)}, f32[8,128]{1,0:T(8,128)S(1)}) custom-call(bf16[272,256]{1,0:T(8,128)(2,1)S(1)} %pack_first.1.first, s32[2,4]{1,0:T(2,128)} %dims_in.3, f32[4]{0:T(128)} %energy_in.3, bf16[4,256,256]{2,1,0:T(8,128)(2,1)} %wave_in.3, ...), custom_call_target="tpu_custom_call" | custom-call | tf_op jit(solution)/shard_map/load/pallas_call | solution.py:316
  10.6 0.0 collective-permute-done.far0
  10.7 0.1 collective-permute-start.1
  10.7 0.1 collective-permute-start.4
  10.8 1.7 %collective-permute-start.3 = (bf16[272,256]{1,0:T(8,128)(2,1)S(1)}, bf16[272,256]{1,0:T(8,128)(2,1)S(1)}, u32[]{:S(2)}, u32[]{:S(2)}) collective-permute-start(bf16[272,256]{1,0:T(8,128)(2,1)S(1)} %collective-permute-done.far0), channel_id=1, source_target_pairs={{0,16},{4,20},{8,24},{12,28},{16,0},{20,4},{24,8},{28,12},{32,48},... | collective-permute-start | bytes 417800 | tf_op jit(solution)/shard_map/ppermute | solution.py:331
  12.5 1.5 %collective-permute-start.2 = (bf16[272,256]{1,0:T(8,128)(2,1)S(1)}, bf16[272,256]{1,0:T(8,128)(2,1)S(1)}, u32[]{:S(2)}, u32[]{:S(2)}) collective-permute-start(bf16[272,256]{1,0:T(8,128)(2,1)S(1)} %collective-permute-done.far0), channel_id=1, source_target_pairs={{0,4},{4,0},{8,12},{12,8},{16,20},{20,16},{24,28},{28,24},{32,36},... | collective-permute-start | bytes 417800 | tf_op jit(solution)/shard_map/ppermute | solution.py:331
  14.0 0.0 collective-permute-start.5
  14.0 2.8 %collective-permute-done.4.far3 = bf16[272,256]{1,0:T(8,128)(2,1)S(1)} collective-permute-done((bf16[272,256]{1,0:T(8,128)(2,1)S(1)}, bf16[272,256]{1,0:T(8,128)(2,1)S(1)}, u32[]{:S(2)}, u32[]{:S(2)}) %collective-permute-start.4) | collective-permute-done | bytes 139296 | tf_op jit(solution)/shard_map/ppermute | solution.py:331
  16.8 0.0 collective-permute-start.8
  16.8 0.0 collective-permute-done.3.far2
  16.8 0.5 collective-permute-start.7
  17.4 0.8 collective-permute-done.2.far1
  18.1 0.0 collective-permute-start.6
  18.1 0.0 collective-permute-done.5.near0
  18.1 0.1 collective-permute-done.8.near3
  18.2 0.2 collective-permute-done.7.near2
  18.4 1.1 collective-permute-done.6.near1
  19.5 0.0 collective-permute-done.1.core
  19.5 5.8 %wave_terms.1 = (bf16[4,256,256]{2,1,0:T(8,128)(2,1)S(1)}, bf16[16,256,256]{2,1,0:T(8,128)(2,1)S(1)}, f32[16,8,256]{2,1,0:T(8,128)S(1)}, f32[2,8,256]{2,1,0:T(8,128)S(1)}, bf16[8,4,256,256]{3,2,1,0:T(8,128)(2,1)S(1)}) custom-call(s32[4,16]{1,0:T(4,128)} %bitcast.11, bf16[4,272,256]{2,1,0:T(8,128)(2,1)S(1)} %get-tuple-element.21.own, ...), custom_call_target="tpu_custom_call" | custom-call | tf_op jit(solution)/shard_map/wave_terms/pallas_call | solution.py:334
  25.2 0.0 copy-start
  25.3 19.6 %all_to_all.20.parts = bf16[32,32,256]{2,1,0:T(8,128)(2,1)S(1)} all-to-all(bf16[32,32,256]{2,1,0:T(8,128)(2,1)S(1)} %bitcast.9), channel_id=1, replica_groups=mesh['op'=32,'blk'=4] {'op'}, dimensions={0} | all-to-all | bytes 1048576 | tf_op jit(solution)/shard_map/all_to_all | solution.py:355
  44.9 0.7 sum_wave.1
  45.6 23.6 %all_to_all.21 = bf16[64,32,256]{2,1,0:T(8,128)(2,1)S(1)} all-to-all(bf16[64,32,256]{2,1,0:T(8,128)(2,1)S(1)} %sum_wave.1), channel_id=1, replica_groups={{0,4,8,12,16,20,24,28,32,36,40,44,48,52,56,60,64,68,72,76,80,84,88,92,9..., dimensions={0} | all-to-all | bytes 2097152 | tf_op jit(solution)/shard_map/all_to_all | solution.py:364
  69.2 0.0 collective-permute-start.9
  69.2 1.3 %decode_half.1 = (f32[2,8,256]{2,1,0:T(8,128)S(1)}, f32[16,256,256]{2,1,0:T(8,128)S(1)}) custom-call(bf16[16,256,256]{2,1,0:T(8,128)(2,1)S(1)} %get-tuple-element.26.wave, f32[2,8,256]{2,1,0:T(8,128)S(1)} %get-tuple-element.28.squares, bf16[2,4,256,256]{3,2,1,0:T(8,128)(2,1)S(1)} %bitcast.6), custom_call_target="tpu_custom_call" | custom-call | flops 16777216 | bytes 4194304 | tf_op jit(solution)/shard_map/decode_half/pallas_call | solution.py:368
  70.5 1.3 %collective-permute-done.9 = bf16[64,32,256]{2,1,0:T(8,128)(2,1)S(1)} collective-permute-done((bf16[64,32,256]{2,1,0:T(8,128)(2,1)S(1)}, bf16[64,32,256]{2,1,0:T(8,128)(2,1)S(1)}, u32[]{:S(2)}, u32[]{:S(2)}) %collective-permute-start.9) | collective-permute-done | bytes 1048608 | tf_op jit(solution)/shard_map/ppermute | solution.py:367
  71.9 0.0 copy-done
  71.9 7.7 %corr_terms.1 = (f32[4,256,256]{2,1,0:T(8,128)}, bf16[4,256,256]{2,1,0:T(8,128)(2,1)S(1)}, bf16[32,4,16,128]{3,2,1,0:T(8,128)(2,1)S(1)}, f32[16,256,256]{2,1,0:T(8,128)S(1)}) custom-call(s32[4,16]{1,0:T(4,128)S(1)} %bitcast.12, bf16[16,256,256]{2,1,0:T(8,128)(2,1)S(1)} %get-tuple-element.26.wave, ...), custom_call_target="tpu_custom_call", output_to_operand_aliasing={{3}: (4, {})} | custom-call | tf_op jit(solution)/shard_map/corr_terms/pallas_call | solution.py:380
  79.6 16.7 %all_to_all.22 = bf16[128,16,128]{2,1,0:T(8,128)(2,1)S(1)} all-to-all(bf16[128,16,128]{2,1,0:T(8,128)(2,1)S(1)} %bitcast.10), channel_id=1, replica_groups=mesh['op'=32,'blk'=4] {'op','blk'}, dimensions={0} | all-to-all | bytes 1048576 | tf_op jit(solution)/shard_map/all_to_all | solution.py:401
  96.4 0.1 sum_corr.1
  96.5 15.3 %all_to_all.23.parts = bf16[32,4,16,128]{3,2,1,0:T(8,128)(2,1)S(1)} all-to-all(bf16[32,4,16,128]{3,2,1,0:T(8,128)(2,1)S(1)} %sum_corr.1), channel_id=1, replica_groups=mesh['op'=32,'blk'=4] {'op'}, dimensions={0} | all-to-all | bytes 1048576 | tf_op jit(solution)/shard_map/all_to_all | solution.py:410
  111.8 1.0 finish.1
Async XLA Ops:
  1.6 9.0 %collective-permute-start = (bf16[272,256]{1,0:T(8,128)(2,1)S(1)}, bf16[272,256]{1,0:T(8,128)(2,1)S(1)}, u32[]{:S(2)}, u32[]{:S(2)}) collective-permute-start(bf16[272,256]{1,0:T(8,128)(2,1)S(1)} %pack_first.1.first), channel_id=1, source_target_pairs={{0,66},{1,67},{2,64},{3,65},{4,70},{5,71},{6,68},{7,69},{8,74},{9,... | collective-permute-start | bytes 417800 | tf_op jit(solution)/shard_map/ppermute | solution.py:315
  10.7 8.8 %collective-permute-start.1 = (bf16[4,272,256]{2,1,0:T(8,128)(2,1)S(1)}, bf16[4,272,256]{2,1,0:T(8,128)(2,1)S(1)}, u32[]{:S(2)}, u32[]{:S(2)}) collective-permute-start(bf16[4,272,256]{2,1,0:T(8,128)(2,1)S(1)} %get-tuple-element.21.own), channel_id=1, source_target_pairs={{0,1},{1,0},{2,3},{3,2},{4,5},{5,4},{6,7},{7,6},{8,9},{9,8},{10,11... | collective-permute-start | bytes 1671176 | tf_op jit(solution)/shard_map/ppermute | solution.py:329
  10.7 6.1 %collective-permute-start.4 = (bf16[272,256]{1,0:T(8,128)(2,1)S(1)}, bf16[272,256]{1,0:T(8,128)(2,1)S(1)}, u32[]{:S(2)}, u32[]{:S(2)}) collective-permute-start(bf16[272,256]{1,0:T(8,128)(2,1)S(1)} %collective-permute-done.far0), channel_id=1, source_target_pairs={{0,64},{4,68},{8,72},{12,76},{16,80},{20,84},{24,88},{28,92},{32,9... | collective-permute-start | bytes 417800 | tf_op jit(solution)/shard_map/ppermute | solution.py:331
  10.8 6.0 %collective-permute-start.3 = (bf16[272,256]{1,0:T(8,128)(2,1)S(1)}, bf16[272,256]{1,0:T(8,128)(2,1)S(1)}, u32[]{:S(2)}, u32[]{:S(2)}) collective-permute-start(bf16[272,256]{1,0:T(8,128)(2,1)S(1)} %collective-permute-done.far0), channel_id=1, source_target_pairs={{0,16},{4,20},{8,24},{12,28},{16,0},{20,4},{24,8},{28,12},{32,48},... | collective-permute-start | bytes 417800 | tf_op jit(solution)/shard_map/ppermute | solution.py:331
  12.5 5.6 %collective-permute-start.2 = (bf16[272,256]{1,0:T(8,128)(2,1)S(1)}, bf16[272,256]{1,0:T(8,128)(2,1)S(1)}, u32[]{:S(2)}, u32[]{:S(2)}) collective-permute-start(bf16[272,256]{1,0:T(8,128)(2,1)S(1)} %collective-permute-done.far0), channel_id=1, source_target_pairs={{0,4},{4,0},{8,12},{12,8},{16,20},{20,16},{24,28},{28,24},{32,36},... | collective-permute-start | bytes 417800 | tf_op jit(solution)/shard_map/ppermute | solution.py:331
  14.0 4.1 %collective-permute-start.5 = (bf16[272,256]{1,0:T(8,128)(2,1)S(1)}, bf16[272,256]{1,0:T(8,128)(2,1)S(1)}, u32[]{:S(2)}, u32[]{:S(2)}) collective-permute-start(bf16[272,256]{1,0:T(8,128)(2,1)S(1)} %collective-permute-done.far0), channel_id=1, source_target_pairs={{0,1},{1,0},{2,3},{3,2},{4,5},{5,4},{6,7},{7,6},{8,9},{9,8},{10,11... | collective-permute-start | bytes 417800 | tf_op jit(solution)/shard_map/ppermute | solution.py:332
  16.8 1.4 %collective-permute-start.8 = (bf16[272,256]{1,0:T(8,128)(2,1)S(1)}, bf16[272,256]{1,0:T(8,128)(2,1)S(1)}, u32[]{:S(2)}, u32[]{:S(2)}) collective-permute-start(bf16[272,256]{1,0:T(8,128)(2,1)S(1)} %collective-permute-done.4.far3), channel_id=1, source_target_pairs={{0,1},{1,0},{2,3},{3,2},{4,5},{5,4},{6,7},{7,6},{8,9},{9,8},{10,11... | collective-permute-start | bytes 417800 | tf_op jit(solution)/shard_map/ppermute | solution.py:332
  16.8 1.6 %collective-permute-start.7 = (bf16[272,256]{1,0:T(8,128)(2,1)S(1)}, bf16[272,256]{1,0:T(8,128)(2,1)S(1)}, u32[]{:S(2)}, u32[]{:S(2)}) collective-permute-start(bf16[272,256]{1,0:T(8,128)(2,1)S(1)} %collective-permute-done.3.far2), channel_id=1, source_target_pairs={{0,1},{1,0},{2,3},{3,2},{4,5},{5,4},{6,7},{7,6},{8,9},{9,8},{10,11... | collective-permute-start | bytes 417800 | tf_op jit(solution)/shard_map/ppermute | solution.py:332
  18.1 1.4 %collective-permute-start.6 = (bf16[272,256]{1,0:T(8,128)(2,1)S(1)}, bf16[272,256]{1,0:T(8,128)(2,1)S(1)}, u32[]{:S(2)}, u32[]{:S(2)}) collective-permute-start(bf16[272,256]{1,0:T(8,128)(2,1)S(1)} %collective-permute-done.2.far1), channel_id=1, source_target_pairs={{0,1},{1,0},{2,3},{3,2},{4,5},{5,4},{6,7},{7,6},{8,9},{9,8},{10,11... | collective-permute-start | bytes 417800 | tf_op jit(solution)/shard_map/ppermute | solution.py:332
  25.2 46.6 %copy-start = (s32[16,4]{0,1:T(4,128)S(1)}, s32[16,4]{0,1:T(4,128)}, u32[]{:S(2)}) copy-start(s32[16,4]{0,1:T(4,128)} %param.9) | copy-start | bytes 772
  69.2 2.7 %collective-permute-start.9 = (bf16[64,32,256]{2,1,0:T(8,128)(2,1)S(1)}, bf16[64,32,256]{2,1,0:T(8,128)(2,1)S(1)}, u32[]{:S(2)}, u32[]{:S(2)}) collective-permute-start(bf16[64,32,256]{2,1,0:T(8,128)(2,1)S(1)} %all_to_all.21), channel_id=1, source_target_pairs={{0,1},{1,0},{2,3},{3,2},{4,5},{5,4},{6,7},{7,6},{8,9},{9,8},{10,11... | collective-permute-start | bytes 3145736 | tf_op jit(solution)/shard_map/ppermute | solution.py:367

commit v8 on v7

--- a/solution.py
+++ b/solution.py
@@ -280,8 +280,11 @@
             rows = pl.ds(i * 16, 16)
             summed = jnp.concatenate([parts[2 * i, b], parts[2 * i + 1, b]], axis=1)
             blocks[b, rows] = summed.astype(F32) + level * corr[b, rows].astype(F32)
-        copies.append(pltpu.make_async_copy(blocks.at[b], out.at[b], sems.at[b]))
-        copies[b].start()
+            if i % 8 == 7:
+                done = pl.ds(i // 8 * 128, 128)
+                place = sems.at[b * 2 + i // 8]
+                copies.append(pltpu.make_async_copy(blocks.at[b, done], out.at[b, done], place))
+                copies[-1].start()
     for copy in copies:
         copy.wait()
 
@@ -413,7 +416,7 @@
         out_shape=shape((4, BD, BD), F32),
         in_specs=[VMEM, VMEM, VMEM],
         out_specs=HBM,
-        scratch_shapes=[pltpu.VMEM((4, BD, BD), F32), pltpu.SemaphoreType.DMA((4,))],
+        scratch_shapes=[pltpu.VMEM((4, BD, BD), F32), pltpu.SemaphoreType.DMA((8,))],
         compiler_params=params(8),
         name="finish",
     )(info, gathered, corr)

time: 113 us -> 113 us (level)
  no operation moved by 1% of the time
where the time goes in v8:
time: 113 us
  blocking collectives  75.3 us (67%)
  Pallas kernels  22.5 us (20%)
  starting transfers between devices  8.04 us (7%)
  waiting for transfers between devices  6.32 us (6%)
    all_to_all x1, blocking collectives, shards(): lax.all_to_all(copies, ALL, 0, 0, tiled=True, axis_index_groups=core_grou...  23.6 us
    all_to_all x1, blocking collectives, shards(): pieces = lax.all_to_all(partial.reshape(32, 32, BD), 'op', 0, 0, tiled=True)  19.6 us
    all_to_all x1, blocking collectives, shards(): lax.all_to_all(partial.reshape(128, 16, 128), ALL, 0, 0, tiled=True)  16.7 us
    all_to_all x1, blocking collectives, shards(): gathered = lax.all_to_all(copies, 'op', 0, 0, tiled=True)  15.3 us
    pallas_call x1, Pallas kernels, shards(): pl.pallas_call(corr_kernel, out_shape=(shape((4, BD, BD), F32), shape((4,...  7.75 us
    pallas_call x1, Pallas kernels, shards(): pl.pallas_call(wave_kernel, out_shape=(shape((4, BD, BD)), shape((16, BD,...  5.75 us
    pallas_call x1, Pallas kernels, shards(): pl.pallas_call(load_kernel, out_shape=(shape((4, ROWS, BD)), pltpu.VMEM(l...  4.8 us
    ppermute x1, starting transfers between devices, shards(): far = [lax.ppermute(first, ALL, cross_pairs())]  4.2 us
  transfers between devices with their start and end apart: 10, of which 6 were waited for; matrix products, arithmetic and copies ran while one was open for 0% of the time, Pallas kernels for 5%

profile of v8, /device:TPU:0, one launch (start us, length us, event | category | flops | bytes accessed | tf_op | source)
XLA Modules:
  0.0 113.0 jit_solution(9438851293345264756)
XLA Ops:
  0.6 1.0 pack_first.1.first
  1.6 4.2 %collective-permute-start = (bf16[272,256]{1,0:T(8,128)(2,1)S(1)}, bf16[272,256]{1,0:T(8,128)(2,1)S(1)}, u32[]{:S(2)}, u32[]{:S(2)}) collective-permute-start(bf16[272,256]{1,0:T(8,128)(2,1)S(1)} %pack_first.1.first), channel_id=1, source_target_pairs={{0,66},{1,67},{2,64},{3,65},{4,70},{5,71},{6,68},{7,69},{8,74},{9,... | collective-permute-start | bytes 417800 | tf_op jit(solution)/shard_map/ppermute | solution.py:318
  5.8 4.8 %load.1 = (bf16[4,272,256]{2,1,0:T(8,128)(2,1)S(1)}, bf16[16,4,256,256]{3,2,1,0:T(8,128)(2,1)S(1)}, bf16[8,4,256,256]{3,2,1,0:T(8,128)(2,1)S(1)}, f32[8,128]{1,0:T(8,128)S(1)}) custom-call(bf16[272,256]{1,0:T(8,128)(2,1)S(1)} %pack_first.1.first, s32[2,4]{1,0:T(2,128)} %dims_in.3, f32[4]{0:T(128)} %energy_in.3, bf16[4,256,256]{2,1,0:T(8,128)(2,1)} %wave_in.3, ...), custom_call_target="tpu_custom_call" | custom-call | tf_op jit(solution)/shard_map/load/pallas_call | solution.py:319
  10.6 0.0 collective-permute-done.far0
  10.7 0.1 collective-permute-start.1
  10.7 0.1 collective-permute-start.4
  10.8 1.7 %collective-permute-start.3 = (bf16[272,256]{1,0:T(8,128)(2,1)S(1)}, bf16[272,256]{1,0:T(8,128)(2,1)S(1)}, u32[]{:S(2)}, u32[]{:S(2)}) collective-permute-start(bf16[272,256]{1,0:T(8,128)(2,1)S(1)} %collective-permute-done.far0), channel_id=1, source_target_pairs={{0,16},{4,20},{8,24},{12,28},{16,0},{20,4},{24,8},{28,12},{32,48},... | collective-permute-start | bytes 417800 | tf_op jit(solution)/shard_map/ppermute | solution.py:334
  12.5 1.5 %collective-permute-start.2 = (bf16[272,256]{1,0:T(8,128)(2,1)S(1)}, bf16[272,256]{1,0:T(8,128)(2,1)S(1)}, u32[]{:S(2)}, u32[]{:S(2)}) collective-permute-start(bf16[272,256]{1,0:T(8,128)(2,1)S(1)} %collective-permute-done.far0), channel_id=1, source_target_pairs={{0,4},{4,0},{8,12},{12,8},{16,20},{20,16},{24,28},{28,24},{32,36},... | collective-permute-start | bytes 417800 | tf_op jit(solution)/shard_map/ppermute | solution.py:334
  14.0 0.0 collective-permute-start.5
  14.0 2.8 %collective-permute-done.4.far3 = bf16[272,256]{1,0:T(8,128)(2,1)S(1)} collective-permute-done((bf16[272,256]{1,0:T(8,128)(2,1)S(1)}, bf16[272,256]{1,0:T(8,128)(2,1)S(1)}, u32[]{:S(2)}, u32[]{:S(2)}) %collective-permute-start.4) | collective-permute-done | bytes 139296 | tf_op jit(solution)/shard_map/ppermute | solution.py:334
  16.8 0.0 collective-permute-start.8
  16.8 0.0 collective-permute-done.3.far2
  16.8 0.5 collective-permute-start.7
  17.4 0.8 collective-permute-done.2.far1
  18.1 0.0 collective-permute-start.6
  18.1 0.0 collective-permute-done.5.near0
  18.1 0.1 collective-permute-done.8.near3
  18.2 0.2 collective-permute-done.7.near2
  18.4 1.1 collective-permute-done.6.near1
  19.5 0.0 collective-permute-done.1.core
  19.5 5.8 %wave_terms.1 = (bf16[4,256,256]{2,1,0:T(8,128)(2,1)S(1)}, bf16[16,256,256]{2,1,0:T(8,128)(2,1)S(1)}, f32[16,8,256]{2,1,0:T(8,128)S(1)}, f32[2,8,256]{2,1,0:T(8,128)S(1)}, bf16[8,4,256,256]{3,2,1,0:T(8,128)(2,1)S(1)}) custom-call(s32[4,16]{1,0:T(4,128)} %bitcast.11, bf16[4,272,256]{2,1,0:T(8,128)(2,1)S(1)} %get-tuple-element.21.own, ...), custom_call_target="tpu_custom_call" | custom-call | tf_op jit(solution)/shard_map/wave_terms/pallas_call | solution.py:337
  25.2 0.0 copy-start
  25.3 19.6 %all_to_all.20.parts = bf16[32,32,256]{2,1,0:T(8,128)(2,1)S(1)} all-to-all(bf16[32,32,256]{2,1,0:T(8,128)(2,1)S(1)} %bitcast.9), channel_id=1, replica_groups=mesh['op'=32,'blk'=4] {'op'}, dimensions={0} | all-to-all | bytes 1048576 | tf_op jit(solution)/shard_map/all_to_all | solution.py:358
  44.9 0.7 sum_wave.1
  45.6 23.6 %all_to_all.21 = bf16[64,32,256]{2,1,0:T(8,128)(2,1)S(1)} all-to-all(bf16[64,32,256]{2,1,0:T(8,128)(2,1)S(1)} %sum_wave.1), channel_id=1, replica_groups={{0,4,8,12,16,20,24,28,32,36,40,44,48,52,56,60,64,68,72,76,80,84,88,92,9..., dimensions={0} | all-to-all | bytes 2097152 | tf_op jit(solution)/shard_map/all_to_all | solution.py:367
  69.2 0.0 collective-permute-start.9
  69.2 1.3 %decode_half.1 = (f32[2,8,256]{2,1,0:T(8,128)S(1)}, f32[16,256,256]{2,1,0:T(8,128)S(1)}) custom-call(bf16[16,256,256]{2,1,0:T(8,128)(2,1)S(1)} %get-tuple-element.26.wave, f32[2,8,256]{2,1,0:T(8,128)S(1)} %get-tuple-element.28.squares, bf16[2,4,256,256]{3,2,1,0:T(8,128)(2,1)S(1)} %bitcast.6), custom_call_target="tpu_custom_call" | custom-call | flops 16777216 | bytes 4194304 | tf_op jit(solution)/shard_map/decode_half/pallas_call | solution.py:371
  70.5 1.3 %collective-permute-done.9 = bf16[64,32,256]{2,1,0:T(8,128)(2,1)S(1)} collective-permute-done((bf16[64,32,256]{2,1,0:T(8,128)(2,1)S(1)}, bf16[64,32,256]{2,1,0:T(8,128)(2,1)S(1)}, u32[]{:S(2)}, u32[]{:S(2)}) %collective-permute-start.9) | collective-permute-done | bytes 1048608 | tf_op jit(solution)/shard_map/ppermute | solution.py:370
  71.9 0.0 copy-done
  71.9 7.7 %corr_terms.1 = (f32[4,256,256]{2,1,0:T(8,128)}, bf16[4,256,256]{2,1,0:T(8,128)(2,1)S(1)}, bf16[32,4,16,128]{3,2,1,0:T(8,128)(2,1)S(1)}, f32[16,256,256]{2,1,0:T(8,128)S(1)}) custom-call(s32[4,16]{1,0:T(4,128)S(1)} %bitcast.12, bf16[16,256,256]{2,1,0:T(8,128)(2,1)S(1)} %get-tuple-element.26.wave, ...), custom_call_target="tpu_custom_call", output_to_operand_aliasing={{3}: (4, {})} | custom-call | tf_op jit(solution)/shard_map/corr_terms/pallas_call | solution.py:383
  79.6 16.7 %all_to_all.22 = bf16[128,16,128]{2,1,0:T(8,128)(2,1)S(1)} all-to-all(bf16[128,16,128]{2,1,0:T(8,128)(2,1)S(1)} %bitcast.10), channel_id=1, replica_groups=mesh['op'=32,'blk'=4] {'op','blk'}, dimensions={0} | all-to-all | bytes 1048576 | tf_op jit(solution)/shard_map/all_to_all | solution.py:404
  96.4 0.1 sum_corr.1
  96.5 15.3 %all_to_all.23.parts = bf16[32,4,16,128]{3,2,1,0:T(8,128)(2,1)S(1)} all-to-all(bf16[32,4,16,128]{3,2,1,0:T(8,128)(2,1)S(1)} %sum_corr.1), channel_id=1, replica_groups=mesh['op'=32,'blk'=4] {'op'}, dimensions={0} | all-to-all | bytes 1048576 | tf_op jit(solution)/shard_map/all_to_all | solution.py:413
  111.8 1.0 finish.1
Async XLA Ops:
  1.6 9.0 %collective-permute-start = (bf16[272,256]{1,0:T(8,128)(2,1)S(1)}, bf16[272,256]{1,0:T(8,128)(2,1)S(1)}, u32[]{:S(2)}, u32[]{:S(2)}) collective-permute-start(bf16[272,256]{1,0:T(8,128)(2,1)S(1)} %pack_first.1.first), channel_id=1, source_target_pairs={{0,66},{1,67},{2,64},{3,65},{4,70},{5,71},{6,68},{7,69},{8,74},{9,... | collective-permute-start | bytes 417800 | tf_op jit(solution)/shard_map/ppermute | solution.py:318
  10.7 8.8 %collective-permute-start.1 = (bf16[4,272,256]{2,1,0:T(8,128)(2,1)S(1)}, bf16[4,272,256]{2,1,0:T(8,128)(2,1)S(1)}, u32[]{:S(2)}, u32[]{:S(2)}) collective-permute-start(bf16[4,272,256]{2,1,0:T(8,128)(2,1)S(1)} %get-tuple-element.21.own), channel_id=1, source_target_pairs={{0,1},{1,0},{2,3},{3,2},{4,5},{5,4},{6,7},{7,6},{8,9},{9,8},{10,11... | collective-permute-start | bytes 1671176 | tf_op jit(solution)/shard_map/ppermute | solution.py:332
  10.7 6.1 %collective-permute-start.4 = (bf16[272,256]{1,0:T(8,128)(2,1)S(1)}, bf16[272,256]{1,0:T(8,128)(2,1)S(1)}, u32[]{:S(2)}, u32[]{:S(2)}) collective-permute-start(bf16[272,256]{1,0:T(8,128)(2,1)S(1)} %collective-permute-done.far0), channel_id=1, source_target_pairs={{0,64},{4,68},{8,72},{12,76},{16,80},{20,84},{24,88},{28,92},{32,9... | collective-permute-start | bytes 417800 | tf_op jit(solution)/shard_map/ppermute | solution.py:334
  10.8 6.0 %collective-permute-start.3 = (bf16[272,256]{1,0:T(8,128)(2,1)S(1)}, bf16[272,256]{1,0:T(8,128)(2,1)S(1)}, u32[]{:S(2)}, u32[]{:S(2)}) collective-permute-start(bf16[272,256]{1,0:T(8,128)(2,1)S(1)} %collective-permute-done.far0), channel_id=1, source_target_pairs={{0,16},{4,20},{8,24},{12,28},{16,0},{20,4},{24,8},{28,12},{32,48},... | collective-permute-start | bytes 417800 | tf_op jit(solution)/shard_map/ppermute | solution.py:334
  12.5 5.6 %collective-permute-start.2 = (bf16[272,256]{1,0:T(8,128)(2,1)S(1)}, bf16[272,256]{1,0:T(8,128)(2,1)S(1)}, u32[]{:S(2)}, u32[]{:S(2)}) collective-permute-start(bf16[272,256]{1,0:T(8,128)(2,1)S(1)} %collective-permute-done.far0), channel_id=1, source_target_pairs={{0,4},{4,0},{8,12},{12,8},{16,20},{20,16},{24,28},{28,24},{32,36},... | collective-permute-start | bytes 417800 | tf_op jit(solution)/shard_map/ppermute | solution.py:334
  14.0 4.1 %collective-permute-start.5 = (bf16[272,256]{1,0:T(8,128)(2,1)S(1)}, bf16[272,256]{1,0:T(8,128)(2,1)S(1)}, u32[]{:S(2)}, u32[]{:S(2)}) collective-permute-start(bf16[272,256]{1,0:T(8,128)(2,1)S(1)} %collective-permute-done.far0), channel_id=1, source_target_pairs={{0,1},{1,0},{2,3},{3,2},{4,5},{5,4},{6,7},{7,6},{8,9},{9,8},{10,11... | collective-permute-start | bytes 417800 | tf_op jit(solution)/shard_map/ppermute | solution.py:335
  16.8 1.4 %collective-permute-start.8 = (bf16[272,256]{1,0:T(8,128)(2,1)S(1)}, bf16[272,256]{1,0:T(8,128)(2,1)S(1)}, u32[]{:S(2)}, u32[]{:S(2)}) collective-permute-start(bf16[272,256]{1,0:T(8,128)(2,1)S(1)} %collective-permute-done.4.far3), channel_id=1, source_target_pairs={{0,1},{1,0},{2,3},{3,2},{4,5},{5,4},{6,7},{7,6},{8,9},{9,8},{10,11... | collective-permute-start | bytes 417800 | tf_op jit(solution)/shard_map/ppermute | solution.py:335
  16.8 1.6 %collective-permute-start.7 = (bf16[272,256]{1,0:T(8,128)(2,1)S(1)}, bf16[272,256]{1,0:T(8,128)(2,1)S(1)}, u32[]{:S(2)}, u32[]{:S(2)}) collective-permute-start(bf16[272,256]{1,0:T(8,128)(2,1)S(1)} %collective-permute-done.3.far2), channel_id=1, source_target_pairs={{0,1},{1,0},{2,3},{3,2},{4,5},{5,4},{6,7},{7,6},{8,9},{9,8},{10,11... | collective-permute-start | bytes 417800 | tf_op jit(solution)/shard_map/ppermute | solution.py:335
  18.1 1.4 %collective-permute-start.6 = (bf16[272,256]{1,0:T(8,128)(2,1)S(1)}, bf16[272,256]{1,0:T(8,128)(2,1)S(1)}, u32[]{:S(2)}, u32[]{:S(2)}) collective-permute-start(bf16[272,256]{1,0:T(8,128)(2,1)S(1)} %collective-permute-done.2.far1), channel_id=1, source_target_pairs={{0,1},{1,0},{2,3},{3,2},{4,5},{5,4},{6,7},{7,6},{8,9},{9,8},{10,11... | collective-permute-start | bytes 417800 | tf_op jit(solution)/shard_map/ppermute | solution.py:335
  25.2 46.6 %copy-start = (s32[16,4]{0,1:T(4,128)S(1)}, s32[16,4]{0,1:T(4,128)}, u32[]{:S(2)}) copy-start(s32[16,4]{0,1:T(4,128)} %param.9) | copy-start | bytes 772
  69.2 2.7 %collective-permute-start.9 = (bf16[64,32,256]{2,1,0:T(8,128)(2,1)S(1)}, bf16[64,32,256]{2,1,0:T(8,128)(2,1)S(1)}, u32[]{:S(2)}, u32[]{:S(2)}) collective-permute-start(bf16[64,32,256]{2,1,0:T(8,128)(2,1)S(1)} %all_to_all.21), channel_id=1, source_target_pairs={{0,1},{1,0},{2,3},{3,2},{4,5},{5,4},{6,7},{7,6},{8,9},{9,8},{10,11... | collective-permute-start | bytes 3145736 | tf_op jit(solution)/shard_map/ppermute | solution.py:370
